TPU v7x, 32 devices: a whole 2x2x4 slice. The times are simulated.
32 devices in a mesh: dp: 8 (over y, x, core), inner: 4 (over z).
Axes of the slice: x: 2, y: 2, z: 4, core: 2. Of those that a mesh axis runs over, the one named last changes fastest.
Arguments:
- queries: bfloat16 [32, 512, 1024], P('dp', 'inner'), may hold values from -6 to 6
- passages: bfloat16 [32, 512, 1024], P('dp', 'inner'), may hold values from -6 to 6
- neg_lists: int32 [32, 8], replicated, may hold values from 0 to 31, as said below
Outputs:
- mean_loss: float32 [], replicated
- query_grad: bfloat16 [32, 512, 1024], P('dp', 'inner')
- passage_grad: bfloat16 [32, 512, 1024], P('dp', 'inner')
Inputs may be any that keep to these rules, and one draw needn't show every extreme that they name: `neg_lists`: each row lists 8 different passage blocks, none from the row's own group (blocks with the same id // 4). The blocks that the rows of one group list include at least one and at most 2 blocks of every other group; in every draw some group lists exactly 2 blocks of every other group.
All inputs are finite; a program needn't handle non-finite values.
Results may differ from a plain program's by a relative error of at most 0.009.
Values may be sent and summed in bfloat16 or wider, within the bound.
No kernel may reach another device: no remote copies, remote signals or barrier semaphores. Data moves between devices by JAX's collectives and lax.ppermute only.
A program may use at most 128 MiB of HBM per device.

v0:
```python
import math

import jax
import jax.numpy as jnp
from jax import lax
from jax.sharding import PartitionSpec as P

CAP = 2


NEG_FILL = -1e30


def slot_tables(neg_lists, groups, per_group, slot_depth):
    block_count = neg_lists.shape[0]
    block_ids = jnp.arange(block_count, dtype=jnp.int32)
    named = jnp.any(neg_lists[:, :, None] == block_ids[None, None, :], axis=1)
    present = jnp.any(named.reshape(groups, per_group, block_count), axis=1)
    present = present.reshape(groups, groups, per_group).astype(jnp.int32)
    slot_ranks = jnp.cumsum(present, axis=2) - 1
    slot_ids = jnp.arange(slot_depth, dtype=jnp.int32)
    hits = (present[..., None] == 1) & (slot_ranks[..., None] == slot_ids[None, None, None, :])
    local_ids = jnp.arange(per_group, dtype=jnp.int32)
    slot_block = jnp.sum(jnp.where(hits, local_ids[None, None, :, None], 0), axis=2)
    slot_live = jnp.any(hits, axis=2)
    return (slot_ranks, slot_block, slot_live)


def body(queries, passages, neg_lists):
    per_group, slice_rows, embed_width = queries.shape
    pick_count = neg_lists.shape[1]
    groups = lax.axis_size("dp")
    inner_count = lax.axis_size("inner")
    full_rows = slice_rows * inner_count
    cand_rows = (pick_count + 1) * slice_rows
    slot_count = groups * CAP
    score_scale = 1.0 / math.sqrt(embed_width)
    my_group = lax.axis_index("dp")
    inner_pos = lax.axis_index("inner")
    slot_ranks, slot_block, slot_live = slot_tables(neg_lists, groups, per_group, CAP)
    listed = lax.dynamic_slice_in_dim(neg_lists, my_group * per_group, per_group, 0)
    owner_group = listed // per_group
    owner_local = listed % per_group
    my_ranks = lax.dynamic_index_in_dim(slot_ranks, my_group, 0, keepdims=False)
    slot_of = owner_group * CAP + my_ranks[owner_group, owner_local]
    sends_for = lax.dynamic_index_in_dim(slot_block, my_group, 1, keepdims=False)
    live_for = lax.dynamic_index_in_dim(slot_live, my_group, 1, keepdims=False)
    block_ids = jnp.arange(per_group, dtype=jnp.int32)
    outgoing = passages[sends_for]
    arrived = lax.all_to_all(outgoing, "dp", split_axis=0, concat_axis=0, tiled=True)
    negatives = arrived.reshape(slot_count, slice_rows, embed_width)[slot_of]
    whole_queries = lax.all_gather(queries, "inner", axis=1, tiled=True)

    def candidates(block_index):
        own_rows = lax.dynamic_index_in_dim(passages, block_index, 0, keepdims=True)
        other_rows = lax.dynamic_index_in_dim(negatives, block_index, 0, keepdims=False)
        return jnp.concatenate([own_rows, other_rows], axis=0).reshape(cand_rows, embed_width)

    def scores(block_index, query_block):
        return (
            jnp.einsum(
                "cd,rd->cr",
                candidates(block_index),
                query_block,
                preferred_element_type=jnp.float32,
            )
            * score_scale
        )

    def forward(inputs):
        block_index, query_block = inputs
        logits = scores(block_index, query_block)
        row_peak = jnp.max(logits, axis=0)
        row_mass = jnp.sum(jnp.exp(logits - row_peak[None, :]), axis=0)
        col_peak = jnp.max(logits, axis=1)
        col_mass = jnp.sum(jnp.exp(logits - col_peak[:, None]), axis=1)
        return (row_peak, row_mass, col_peak, col_mass)

    row_peak, row_mass, col_peak, col_mass = lax.map(forward, (block_ids, whole_queries))
    peak_all = lax.pmax(row_peak, "inner")
    mass_all = lax.psum(row_mass * jnp.exp(row_peak - peak_all), "inner")
    query_lse = peak_all + jnp.log(mass_all)
    own_peak = col_peak[:, :slice_rows]
    own_mass = col_mass[:, :slice_rows]
    far_peak = col_peak[:, slice_rows:].reshape(per_group * pick_count, slice_rows)
    far_mass = col_mass[:, slice_rows:].reshape(per_group * pick_count, slice_rows)
    flat_slots = slot_of.reshape(-1)
    onehot = flat_slots[:, None] == jnp.arange(slot_count, dtype=jnp.int32)[None, :]
    slot_peak = jnp.max(jnp.where(onehot[:, :, None], far_peak[:, None, :], NEG_FILL), axis=0)
    rescaled = far_mass * jnp.exp(far_peak - slot_peak[flat_slots])
    slot_mass = jnp.dot(onehot.astype(jnp.float32).T, rescaled, precision=lax.Precision.HIGHEST)
    got_peak, got_mass = (
        lax.all_to_all(
            slot_peak.reshape(groups, CAP, slice_rows),
            "dp",
            split_axis=0,
            concat_axis=0,
            tiled=True,
        ),
        lax.all_to_all(
            slot_mass.reshape(groups, CAP, slice_rows),
            "dp",
            split_axis=0,
            concat_axis=0,
            tiled=True,
        ),
    )
    belongs = (sends_for[:, :, None] == block_ids[None, None, :]) & live_for[:, :, None]
    belongs = belongs.reshape(slot_count, per_group)
    got_peak = got_peak.reshape(slot_count, slice_rows)
    got_mass = got_mass.reshape(slot_count, slice_rows)
    spread_peak = jnp.where(belongs[:, :, None], got_peak[:, None, :], NEG_FILL)
    pass_peak = jnp.maximum(own_peak, jnp.max(spread_peak, axis=0))
    spread_mass = jnp.where(
        belongs[:, :, None],
        got_mass[:, None, :] * jnp.exp(spread_peak - pass_peak[None, :, :]),
        0.0,
    )
    pass_mass = own_mass * jnp.exp(own_peak - pass_peak) + jnp.sum(spread_mass, axis=0)
    passage_lse = pass_peak + jnp.log(pass_mass)
    own_scores = (
        jnp.einsum("lrd,lrd->lr", queries, passages, preferred_element_type=jnp.float32)
        * score_scale
    )
    my_query_lse = lax.dynamic_slice_in_dim(query_lse, inner_pos * slice_rows, slice_rows, 1)
    local_loss = jnp.sum(my_query_lse - own_scores) + jnp.sum(passage_lse - own_scores)
    mean_loss = lax.psum(local_loss, ("dp", "inner")) / (2.0 * groups * per_group * full_rows)
    lse_out = passage_lse[sends_for]
    lse_back = lax.all_to_all(lse_out, "dp", split_axis=0, concat_axis=0, tiled=True).reshape(
        slot_count, slice_rows
    )
    cand_lse = jnp.concatenate([passage_lse[:, None, :], lse_back[slot_of]], axis=1).reshape(
        per_group, cand_rows
    )
    cand_pos = jnp.arange(cand_rows, dtype=jnp.int32)
    row_pos = jnp.arange(full_rows, dtype=jnp.int32)
    target = (
        (cand_pos[:, None] < slice_rows)
        & (row_pos[None, :] == inner_pos * slice_rows + cand_pos[:, None])
    ).astype(jnp.float32)

    def backward(block_index, carry):
        weights, slot_grad, own_grad = carry
        query_block = lax.dynamic_index_in_dim(whole_queries, block_index, 0, keepdims=False)
        logits = scores(block_index, query_block)
        row_lse = lax.dynamic_index_in_dim(query_lse, block_index, 0, keepdims=False)
        col_lse = lax.dynamic_index_in_dim(cand_lse, block_index, 0, keepdims=False)
        probs = (
            0.5 * jnp.exp(logits - row_lse[None, :])
            + 0.5 * jnp.exp(logits - col_lse[:, None])
            - target
        )
        rounded = probs.astype(jnp.bfloat16)
        passage_part = jnp.einsum(
            "cr,rd->cd", rounded, query_block, preferred_element_type=jnp.float32
        )
        own_grad = lax.dynamic_update_index_in_dim(
            own_grad, passage_part[:slice_rows], block_index, 0
        )
        slot_targets = lax.dynamic_index_in_dim(slot_of, block_index, 0, keepdims=False)
        slot_grad = slot_grad.at[slot_targets].add(
            passage_part[slice_rows:].reshape(pick_count, slice_rows, embed_width)
        )
        weights = lax.dynamic_update_index_in_dim(weights, rounded, block_index, 0)
        return (weights, slot_grad, own_grad)

    start_carry = (
        jnp.zeros((per_group, cand_rows, full_rows), jnp.bfloat16),
        jnp.zeros((slot_count, slice_rows, embed_width), jnp.float32),
        jnp.zeros((per_group, slice_rows, embed_width), jnp.float32),
    )
    weights, slot_grad, own_grad = lax.fori_loop(0, per_group, backward, start_carry)

    def one_block(inputs):
        block_index, block_weights = inputs
        return jnp.einsum(
            "cr,cd->rd", block_weights, candidates(block_index), preferred_element_type=jnp.float32
        )

    query_sum = lax.psum_scatter(
        jnp.swapaxes(lax.map(one_block, (block_ids, weights)), 0, 1).astype(jnp.bfloat16),
        "inner",
        scatter_dimension=0,
        tiled=True,
    ).astype(jnp.float32)
    query_grad = jnp.swapaxes(query_sum, 0, 1).astype(jnp.bfloat16)
    returned = lax.all_to_all(
        slot_grad.astype(jnp.bfloat16).reshape(groups, CAP, slice_rows, embed_width),
        "dp",
        split_axis=0,
        concat_axis=0,
        tiled=True,
    )
    passage_sum = jnp.einsum(
        "eg,ecd->gcd",
        belongs.astype(jnp.bfloat16),
        returned.reshape(slot_count, slice_rows, embed_width),
        preferred_element_type=jnp.float32,
    )
    passage_grad = (passage_sum + own_grad).astype(jnp.bfloat16)
    return (mean_loss, query_grad, passage_grad)


def solution(mesh):
    in_specs = (P("dp", "inner", None), P("dp", "inner", None), P())
    out_specs = (P(), P("dp", "inner", None), P("dp", "inner", None))
    return jax.shard_map(body, mesh=mesh, in_specs=in_specs, out_specs=out_specs, check_vma=False)
```

profile of v0, /device:TPU:0, one launch (start us, length us, event | category | flops | bytes accessed | tf_op | source)
XLA Modules:
  0.0 457.8 jit_solution(15847594601991787747)
XLA Ops:
  12.3 5.2 %all-to-all-start = ((bf16[8,2,128,1024]{3,2,1,0:T(8,128)(2,1)}), bf16[8,2,128,1024]{3,2,1,0:T(8,128)(2,1)}, u32[]{:S(2)}, u32[]{:S(2)}) async-start(bf16[8,2,128,1024]{3,2,1,0:T(8,128)(2,1)} %bitcast.149), calls=%async_computation | async-start | bytes 8388608 | tf_op jit(solution)/shard_map/all_to_all | solution.py:50
  20.7 46.1 %all-to-all-done = bf16[8,2,128,1024]{3,2,1,0:T(8,128)(2,1)} async-done(((bf16[8,2,128,1024]{3,2,1,0:T(8,128)(2,1)}), bf16[8,2,128,1024]{3,2,1,0:T(8,128)(2,1)}, u32[]{:S(2)}, u32[]{:S(2)}) %all-to-all-start) | async-done | bytes 4194336 | tf_op jit(solution)/shard_map/all_to_all | solution.py:50
  66.7 7.3 %gather_fusion.2 = bf16[32,128,1024]{2,1,0:T(8,128)(2,1)} fusion(bf16[16,128,1024]{2,1,0:T(8,128)(2,1)} %bitcast.14, s32[1024]{0:T(1024)S(1)} %pad_clamp_fusion.1), kind=kCustom, calls=%fused_computation.2 | custom fusion | bytes 16777344 | tf_op jit(solution)/shard_map/gather | solution.py:51
  74.0 19.1 %all-gather.2.cloned.1.call-done = bf16[4,512,1024]{2,1,0:T(8,128)(2,1)} async-done(((bf16[4,128,1024]{2,1,0:T(8,128)(2,1)}), bf16[4,512,1024]{2,1,0:T(8,128)(2,1)}) %all-gather.2.cloned.1.call-update) | async-done | bytes 4194320 | tf_op jit(solution)/shard_map/all_gather | solution.py:52
  93.2 34.6 %while.44 = (s32[]{:T(128)}, f32[4,512]{1,0:T(4,128)S(1)}, f32[4,512]{1,0:T(4,128)S(1)}, f32[4,1152]{1,0:T(4,128)S(1)}, f32[4,1152]{1,0:T(4,128)S(1)}, /*index=5...) while((s32[]{:T(128)}, f32[4,512]{1,0:T(4,128)S(1)}, ...), condition=%wide.region_9.10_spmd, body=%wide.region_4.9_spmd.sunk | while | flops 1213264640 | bytes 17629372 | solution.py:79
  129.9 3.6 all-to-all-start.1
  133.5 9.3 %pmax.7 = f32[4,512]{1,0:T(4,128)S(1)} all-reduce(f32[4,512]{1,0:T(4,128)S(1)} %get-tuple-element.271), channel_id=1, replica_groups=mesh['dp'=8,'inner'=4] {'inner'}, use_global_device_ids=true, to_apply=%region_10.11 | all-reduce | flops 2048 | bytes 16384 | tf_op jit(solution)/shard_map/pmax | solution.py:80
  142.8 9.7 %psum.14 = f32[4,512]{1,0:T(4,128)S(1)} all-reduce(f32[4,512]{1,0:T(4,128)S(1)} %exponential_multiply_fusion.1), channel_id=1, replica_groups=mesh['dp'=8,'inner'=4] {'inner'}, use_global_device_ids=true, to_apply=%region_11.12 | all-reduce | flops 2048 | bytes 16384 | tf_op jit(solution)/shard_map/psum | solution.py:81
  153.4 4.2 all-to-all-start.2
  157.7 4.6 %all-to-all-done.2 = f32[8,2,128]{2,1,0:T(2,128)S(1)} async-done(((f32[8,2,128]{2,1,0:T(2,128)}), f32[8,2,128]{2,1,0:T(2,128)S(1)}, u32[]{:S(2)}, u32[]{:S(2)}) %all-to-all-start.2) | async-done | bytes 8224 | tf_op jit(solution)/shard_map/all_to_all | solution.py:100
  167.8 4.4 all-to-all-done.3
  172.7 4.3 broadcast_in_dim.168
  177.0 136.4 %while.46 = (s32[]{:T(128)}, bf16[4,1152,512]{2,1,0:T(8,128)(2,1)}, f32[16,128,1024]{2,1,0:T(8,128)}, f32[4,128,1024]{2,0,1:T(4,128)}, bf16[4,128,1024]{2,1,0:T(...) while((s32[]{:T(128)}, bf16[4,1152,512]{2,1,0:T(8,128)(2,1)}, ...), condition=%wide.region_21.22_spmd.clone, body=%wide.region_19.21_spmd.clone.sunk | while | flops 2424045568 | bytes 81955128 | solution.py:172
  189.5 9.4 %scatter_fusion = f32[16,128,1024]{2,1,0:T(8,128)} fusion(f32[16,128,1024]{2,1,0:T(8,128)} %get-tuple-element.623, s32[8]{0:T(128)S(1)} %fusion.73, f32[8,128,1024]{2,1,0:T(8,128)} %bitcast.143), kind=kCustom, calls=%fused_computation.6.clone.clone.1 | custom fusion | flops 1048576 | bytes 12582944 | tf_op jit(solution)/shard_map/while/body/eval_jaxpr/scatter-add | solution.py:161
  200.6 10.5 %dynamic_update_slice.51 = f32[4,128,1024]{2,0,1:T(4,128)} dynamic-update-slice(f32[4,128,1024]{2,0,1:T(4,128)} %get-tuple-element.624, f32[1,128,1024]{2,0,1:T(1,128)S(1)} %copy.95, s32[]{:T(128)} %get-tuple-element.621, s32[]{:T(128)} %constant.187.clone.1..sunk.2, s32[]{:T(128)} %constant.187.clone.1..sunk.2) | dynamic-update-slice | bytes 1048580 | tf_op jit(solution)/shard_map/while/body/eval_jaxpr/jit(dynamic_update_index_in_dim)/dynamic_update_slice | solution.py:157
  215.1 3.6 bitcast_dynamic-update-slice_fusion.5
  223.7 9.4 %scatter_fusion = f32[16,128,1024]{2,1,0:T(8,128)} fusion(f32[16,128,1024]{2,1,0:T(8,128)} %get-tuple-element.623, s32[8]{0:T(128)S(1)} %fusion.73, f32[8,128,1024]{2,1,0:T(8,128)} %bitcast.143), kind=kCustom, calls=%fused_computation.6.clone.clone.1 | custom fusion | flops 1048576 | bytes 12582944 | tf_op jit(solution)/shard_map/while/body/eval_jaxpr/scatter-add | solution.py:161
  234.6 10.5 %dynamic_update_slice.51 = f32[4,128,1024]{2,0,1:T(4,128)} dynamic-update-slice(f32[4,128,1024]{2,0,1:T(4,128)} %get-tuple-element.624, f32[1,128,1024]{2,0,1:T(1,128)S(1)} %copy.95, s32[]{:T(128)} %get-tuple-element.621, s32[]{:T(128)} %constant.187.clone.1..sunk.2, s32[]{:T(128)} %constant.187.clone.1..sunk.2) | dynamic-update-slice | bytes 1048580 | tf_op jit(solution)/shard_map/while/body/eval_jaxpr/jit(dynamic_update_index_in_dim)/dynamic_update_slice | solution.py:157
  257.7 9.5 %scatter_fusion = f32[16,128,1024]{2,1,0:T(8,128)} fusion(f32[16,128,1024]{2,1,0:T(8,128)} %get-tuple-element.623, s32[8]{0:T(128)S(1)} %fusion.73, f32[8,128,1024]{2,1,0:T(8,128)} %bitcast.143), kind=kCustom, calls=%fused_computation.6.clone.clone.1 | custom fusion | flops 1048576 | bytes 12582944 | tf_op jit(solution)/shard_map/while/body/eval_jaxpr/scatter-add | solution.py:161
  268.8 10.5 %dynamic_update_slice.51 = f32[4,128,1024]{2,0,1:T(4,128)} dynamic-update-slice(f32[4,128,1024]{2,0,1:T(4,128)} %get-tuple-element.624, f32[1,128,1024]{2,0,1:T(1,128)S(1)} %copy.95, s32[]{:T(128)} %get-tuple-element.621, s32[]{:T(128)} %constant.187.clone.1..sunk.2, s32[]{:T(128)} %constant.187.clone.1..sunk.2) | dynamic-update-slice | bytes 1048580 | tf_op jit(solution)/shard_map/while/body/eval_jaxpr/jit(dynamic_update_index_in_dim)/dynamic_update_slice | solution.py:157
  291.9 9.4 %scatter_fusion = f32[16,128,1024]{2,1,0:T(8,128)} fusion(f32[16,128,1024]{2,1,0:T(8,128)} %get-tuple-element.623, s32[8]{0:T(128)S(1)} %fusion.73, f32[8,128,1024]{2,1,0:T(8,128)} %bitcast.143), kind=kCustom, calls=%fused_computation.6.clone.clone.1 | custom fusion | flops 1048576 | bytes 12582944 | tf_op jit(solution)/shard_map/while/body/eval_jaxpr/scatter-add | solution.py:161
  302.9 10.5 %dynamic_update_slice.51 = f32[4,128,1024]{2,0,1:T(4,128)} dynamic-update-slice(f32[4,128,1024]{2,0,1:T(4,128)} %get-tuple-element.624, f32[1,128,1024]{2,0,1:T(1,128)S(1)} %copy.95, s32[]{:T(128)} %get-tuple-element.621, s32[]{:T(128)} %constant.187.clone.1..sunk.2, s32[]{:T(128)} %constant.187.clone.1..sunk.2) | dynamic-update-slice | bytes 1048580 | tf_op jit(solution)/shard_map/while/body/eval_jaxpr/jit(dynamic_update_index_in_dim)/dynamic_update_slice | solution.py:157
  313.4 33.5 %while.45 = (s32[]{:T(128)}, bf16[4,512,1024]{2,1,0:T(8,128)(2,1)}, bf16[4,1152,512]{2,1,0:T(8,128)(2,1)}, s32[4]{0:T(128)S(1)}, bf16[4,128,1024]{2,1,0:T(8,128)...) while((s32[]{:T(128)}, bf16[4,512,1024]{2,1,0:T(8,128)(2,1)}, ...), condition=%wide.region_23.24_spmd, body=%wide.region_22.23_spmd.sunk | while | flops 1209139200 | bytes 15074451 | solution.py:181
  318.0 3.8 bitcast_dynamic-update-slice_fusion.4
  326.4 3.8 bitcast_dynamic-update-slice_fusion.4
  334.7 3.8 bitcast_dynamic-update-slice_fusion.4
  343.1 3.8 bitcast_dynamic-update-slice_fusion.4
  347.0 4.6 %convert_element_type.45 = bf16[16,128,1024]{2,1,0:T(8,128)(2,1)S(1)} convert(f32[16,128,1024]{2,1,0:T(8,128)} %get-tuple-element.277) | non-fusion elementwise | flops 2097152 | bytes 12582912 | tf_op jit(solution)/shard_map/convert_element_type | solution.py:188
  351.6 6.3 %copy.71 = bf16[8,2,128,1024]{3,1,2,0:T(2,128)(2,1)} copy(bf16[8,2,128,1024]{3,2,1,0:T(8,128)(2,1)S(1)} %bitcast.148) | data formatting | bytes 8388608 | tf_op jit(solution)/shard_map/reshape | solution.py:188
  357.9 4.7 %all-to-all-start.4 = ((bf16[8,2,128,1024]{3,1,2,0:T(2,128)(2,1)}), bf16[8,2,128,1024]{3,1,2,0:T(2,128)(2,1)}, u32[]{:S(2)}, u32[]{:S(2)}) async-start(bf16[8,2,128,1024]{3,1,2,0:T(2,128)(2,1)} %copy.71), calls=%async_computation.5 | async-start | bytes 8388608 | tf_op jit(solution)/shard_map/all_to_all | solution.py:187
  363.9 79.1 %psum.15 = f32[]{:T(128)} all-reduce(f32[]{:T(128)S(6)} %add.194), channel_id=1, replica_groups=mesh['dp'=8,'inner'=4] {'dp','inner'}, use_global_device_ids=true, to_apply=%region_18.19 | all-reduce | flops 1 | bytes 8 | tf_op jit(solution)/shard_map/psum | solution.py:127
  443.6 5.0 %fusion.21 = bf16[4,128,1024]{2,0,1:T(4,128)(2,1)S(1)} fusion(f32[4,128,1024]{2,0,1:T(4,128)S(1)} %copy-done.4, bf16[8,2,128,1024]{3,1,2,0:T(2,128)(2,1)} %all-to-all-done.4, s32[8,2]{0,1:T(2,128)S(1)} %copy-done.6, pred[8,2]{0,1:T(4,128)(4,1)S(1)} %copy-done.7), kind=kOutput, calls=%fused_computation.51 | convolution fusion | flops 17825920 | bytes 7340112 | tf_op jit(solution)/shard_map/eg,ecd->gcd/dot_general | solution.py:194
  (214 shorter events, 108.2 us)
Async XLA Ops:
  7.2 2.4 copy-start.1
  7.2 86.0 %all-gather.2.cloned.1.call-start = ((), (), s32[]{:S(2)}) async-start(), calls=%async_computation.6 | async-start | bytes 5242880 | tf_op jit(solution)/shard_map/all_gather | solution.py:52
  9.4 2.9 copy-start.5
  12.3 54.4 %all-to-all-start = ((bf16[8,2,128,1024]{3,2,1,0:T(8,128)(2,1)}), bf16[8,2,128,1024]{3,2,1,0:T(8,128)(2,1)}, u32[]{:S(2)}, u32[]{:S(2)}) async-start(bf16[8,2,128,1024]{3,2,1,0:T(8,128)(2,1)} %bitcast.149), calls=%async_computation | async-start | bytes 8388608 | tf_op jit(solution)/shard_map/all_to_all | solution.py:50
  17.5 2.7 copy-start.3
  129.9 23.5 %all-to-all-start.1 = ((f32[8,2,128]{2,1,0:T(2,128)}), f32[8,2,128]{2,1,0:T(2,128)S(1)}, u32[]{:S(2)}, u32[]{:S(2)}) async-start(f32[8,2,128]{2,1,0:T(2,128)} %bitcast.17), calls=%async_computation.1 | async-start | bytes 16384 | tf_op jit(solution)/shard_map/all_to_all | solution.py:93
  153.4 8.9 %all-to-all-start.2 = ((f32[8,2,128]{2,1,0:T(2,128)}), f32[8,2,128]{2,1,0:T(2,128)S(1)}, u32[]{:S(2)}, u32[]{:S(2)}) async-start(f32[8,2,128]{2,1,0:T(2,128)} %copy.69), calls=%async_computation.2 | async-start | bytes 16384 | tf_op jit(solution)/shard_map/all_to_all | solution.py:100
  164.2 8.0 %all-to-all-start.3 = ((f32[8,2,128]{2,1,0:T(2,128)}), f32[8,2,128]{2,1,0:T(2,128)S(1)}, u32[]{:S(2)}, u32[]{:S(2)}) async-start(f32[8,2,128]{2,1,0:T(2,128)} %bitcast.23), calls=%async_computation.3 | async-start | bytes 16384 | tf_op jit(solution)/shard_map/all_to_all | solution.py:129
  167.5 282.4 %reduce-scatter.2.cloned.1.call-start = ((), (), s32[]{:S(2)}) async-start(), calls=%async_computation.7 | async-start | bytes 5242880 | tf_op jit(solution)/shard_map/reduce_scatter | solution.py:180
  178.8 2.2 copy-start.2
  185.9 3.6 copy-start
  212.9 2.2 copy-start.2
  220.1 3.6 copy-start
  247.0 2.2 copy-start.2
  254.1 3.6 copy-start
  281.1 2.2 copy-start.2
  288.3 3.6 copy-start
  357.9 85.7 %copy-start.4 = (f32[4,128,1024]{2,0,1:T(4,128)S(1)}, f32[4,128,1024]{2,0,1:T(4,128)}, u32[]{:S(2)}) copy-start(f32[4,128,1024]{2,0,1:T(4,128)} %get-tuple-element.278) | copy-start | bytes 6291460
  357.9 85.7 %copy-start.6 = (s32[8,2]{0,1:T(2,128)S(1)}, s32[8,2]{0,1:T(2,128)}, u32[]{:S(2)}) copy-start(s32[8,2]{0,1:T(2,128)} %copy-done.5) | copy-start | bytes 196
  357.9 85.7 %copy-start.7 = (pred[8,2]{0,1:T(4,128)(4,1)S(1)}, pred[8,2]{0,1:T(4,128)(4,1)}, u32[]{:S(2)}) copy-start(pred[8,2]{0,1:T(4,128)(4,1)} %get-tuple-element.382) | copy-start | bytes 52
  357.9 85.7 %all-to-all-start.4 = ((bf16[8,2,128,1024]{3,1,2,0:T(2,128)(2,1)}), bf16[8,2,128,1024]{3,1,2,0:T(2,128)(2,1)}, u32[]{:S(2)}, u32[]{:S(2)}) async-start(bf16[8,2,128,1024]{3,1,2,0:T(2,128)(2,1)} %copy.71), calls=%async_computation.5 | async-start | bytes 8388608 | tf_op jit(solution)/shard_map/all_to_all | solution.py:187
Sparse Core Ops, SparseCore 0:
  9.6 83.5 all-gather.1
  347.1 73.4 reduce-scatter.1
where the time goes:
time: 461 us; the launch traced here: 458 us
  local copies, waits for them, and re-layouts  127 us (28%)
  blocking collectives  98.1 us (21%)
  waiting for transfers between devices  74.9 us (16%)
  other arithmetic  51.3 us (11%)
  matrix products  51.2 us (11%)
  starting transfers between devices  21.3 us (5%)
  between operations  17.5 us (4%)
  loops' own time  16.2 us (4%)
    psum x1, blocking collectives, body(): lax.psum(local_loss, ('dp', 'inner'))  79.1 us
    all_to_all x1, waiting for transfers between devices, body(): lax.all_to_all(outgoing, 'dp', split_axis=0, concat_axis=0, tiled=True)  46.1 us
    dynamic_update_slice x8, local copies, waits for them, and re-layouts, backward(): lax.dynamic_update_index_in_dim(own_grad, passage_part[:slice_rows], bloc...  44.3 us
    scatter-add x4, other arithmetic, backward(): slot_grad.at[slot_targets]  37.6 us
    dot_general x8, matrix products, scores(): jnp.einsum('cd,rd->cr', candidates(block_index), query_block, preferred_e...  25.1 us
    squeeze x12, local copies, waits for them, and re-layouts, candidates(): lax.dynamic_index_in_dim(negatives, block_index, 0, keepdims=False)  21.2 us
    all_gather x1, waiting for transfers between devices, body(): whole_queries = lax.all_gather(queries, 'inner', axis=1, tiled=True)  19.1 us
    dot_general x4, matrix products, one_block(): jnp.einsum('cr,cd->rd', block_weights, candidates(block_index), preferred...  15.3 us
  transfers between devices with their start and end apart: 7, of which 4 were waited for; matrix products, arithmetic and copies ran while one was open for 7% of the time, Pallas kernels for 0%

commit v1 on v0

v1 whole, which is shorter than its diff:
```python
import functools
import math

import jax
import jax.numpy as jnp
from jax import lax
from jax.experimental import pallas as pl
from jax.experimental.pallas import tpu as pltpu
from jax.sharding import PartitionSpec as P

CAP = 2
NEG_FILL = -1e30
LOG2E = math.log2(math.e)
LN2 = math.log(2.0)
ANY = pl.BlockSpec(memory_space=pl.ANY)
SMEM = pl.BlockSpec(memory_space=pltpu.SMEM)
VMEM = pl.BlockSpec(memory_space=pltpu.VMEM)
VMEM_LIMIT = 48 * 1024 * 1024


def slot_tables(neg_lists, groups, per_group, slot_depth):
    block_count = neg_lists.shape[0]
    block_ids = jnp.arange(block_count, dtype=jnp.int32)
    named = jnp.any(neg_lists[:, :, None] == block_ids[None, None, :], axis=1)
    present = jnp.any(named.reshape(groups, per_group, block_count), axis=1)
    present = present.reshape(groups, groups, per_group).astype(jnp.int32)
    slot_ranks = jnp.cumsum(present, axis=2) - 1
    slot_ids = jnp.arange(slot_depth, dtype=jnp.int32)
    hits = (present[..., None] == 1) & (slot_ranks[..., None] == slot_ids[None, None, None, :])
    local_ids = jnp.arange(per_group, dtype=jnp.int32)
    slot_block = jnp.sum(jnp.where(hits, local_ids[None, None, :, None], 0), axis=2)
    slot_live = jnp.any(hits, axis=2)
    return (slot_ranks, slot_block, slot_live)


def join_log2(a, b):
    return jnp.maximum(a, b) + jnp.log2(1.0 + jnp.exp2(-jnp.abs(a - b)))


def row_tile(rows):
    return math.gcd(rows, 256)


class Fetch:
    def __init__(self, first, inner, picks, pos_ref, slot_ref, own_q, from_left, from_right, own_p, far_p,
                 cands, whole_q, sems):
        self.first, self.inner, self.picks = first, inner, picks
        self.pos_ref, self.slot_ref = pos_ref, slot_ref
        self.own_q, self.from_left, self.from_right = own_q, from_left, from_right
        self.own_p, self.far_p = own_p, far_p
        self.cands, self.whole_q, self.sems = cands, whole_q, sems
        self.rows = own_q.shape[1]

    def cand_copy(self, b, buf, k):
        block = self.first + b
        if k == 0:
            src = self.own_p.at[block]
        else:
            src = self.far_p.at[self.slot_ref[block * self.picks + k - 1]]
        dst = self.cands.at[buf, pl.ds(k * self.rows, self.rows)]
        return pltpu.make_async_copy(src, dst, self.sems.at[buf, k])

    def query_copy(self, src, buf, pos, k):
        dst = self.whole_q.at[buf, pl.ds(pl.multiple_of(pos * self.rows, self.rows), self.rows)]
        return pltpu.make_async_copy(src, dst, self.sems.at[buf, self.picks + 1 + k])

    def start_q(self, b, buf):
        pos = self.pos_ref[0]
        self.query_copy(self.own_q.at[self.first + b], buf, pos, 0).start()
        for k in range(1, self.inner):
            @pl.when(pos >= k)
            def _():
                self.query_copy(self.from_left[k - 1].at[b], buf, pos - k, k).start()

            @pl.when(pos < k)
            def _():
                self.query_copy(
                    self.from_right[self.inner - k - 1].at[b], buf, pos - k + self.inner, k
                ).start()

    def start(self, b, buf):
        self.start_q(b, buf)
        for k in range(self.picks + 1):
            self.cand_copy(b, buf, k).start()

    def wait_q(self, b, buf):
        for k in range(self.inner):
            self.query_copy(self.own_q.at[self.first + b], buf, k, k).wait()

    def wait(self, b, buf):
        self.wait_q(b, buf)
        for k in range(self.picks + 1):
            self.cand_copy(b, buf, 0 if k == 0 else k).wait()


def dot_t(a, b):
    return lax.dot_general(a, b, (((1,), (1,)), ((), ())), preferred_element_type=jnp.float32)


def forward_kernel(first, count, inner, picks, scale, *refs):
    pos_ref, slot_ref, id_ref, own_q = refs[:4]
    from_left = refs[4:3 + inner]
    from_right = refs[3 + inner:2 + 2 * inner]
    own_p, far_p, col_in, row_out, col_out, cands, whole_q, sems = refs[2 + 2 * inner:]
    rows = own_q.shape[1]
    full = rows * inner
    tile = row_tile(full)
    fetch = Fetch(first, inner, picks, pos_ref, slot_ref, own_q, from_left, from_right, own_p, far_p,
                  cands, whole_q, sems)
    fetch.start(0, 0)
    col_out[...] = col_in[...]
    for b in range(count):
        buf = b % 2
        if b + 1 < count:
            fetch.start(b + 1, 1 - buf)
        fetch.wait(b, buf)
        block_col = None
        for t in range(full // tile):
            logits = dot_t(whole_q[buf, t * tile:(t + 1) * tile, :], cands[buf]) * scale
            peak = jnp.max(logits, axis=1, keepdims=True)
            mass = jnp.sum(jnp.exp2(logits - peak), axis=1, keepdims=True)
            row_lse = jnp.broadcast_to(peak + jnp.log2(mass), (tile, 128))
            row_out[b:b + 1, t * tile:(t + 1) * tile] = row_lse.T[0:1, :]
            col_peak = jnp.max(logits, axis=0, keepdims=True)
            col_mass = jnp.sum(jnp.exp2(logits - col_peak), axis=0, keepdims=True)
            col_lse = col_peak + jnp.log2(col_mass)
            block_col = col_lse if block_col is None else join_log2(block_col, col_lse)
        for k in range(picks + 1):
            row = pl.ds(id_ref[(first + b) * (picks + 1) + k], 1)
            col_out[row, :] = join_log2(col_out[row, :], block_col[:, k * rows:(k + 1) * rows])


def query_kernel(first, count, inner, picks, scale, *refs):
    pos_ref, slot_ref, id_ref, own_q = refs[:4]
    from_left = refs[4:3 + inner]
    from_right = refs[3 + inner:2 + 2 * inner]
    own_p, far_p, row_lse, col_lse, dq_out, w_out, cands, whole_q, sems = refs[2 + 2 * inner:]
    rows = own_q.shape[1]
    full = rows * inner
    tile = row_tile(full)
    fetch = Fetch(first, inner, picks, pos_ref, slot_ref, own_q, from_left, from_right, own_p, far_p,
                  cands, whole_q, sems)
    fetch.start(0, 0)
    pos = pos_ref[0]
    for b in range(count):
        buf = b % 2
        if b + 1 < count:
            fetch.start(b + 1, 1 - buf)
        col = jnp.concatenate(
            [
                col_lse[pl.ds(id_ref[(first + b) * (picks + 1) + k], 1), :]
                for k in range(picks + 1)
            ],
            axis=1,
        ) + 1.0
        row = jnp.broadcast_to(row_lse[first + b:first + b + 1, :] + 1.0, (128, full)).T
        fetch.wait(b, buf)
        for t in range(full // tile):
            part = slice(t * tile, (t + 1) * tile)
            logits = dot_t(whole_q[buf, part, :], cands[buf]) * scale
            probs = jnp.exp2(logits - row[part, 0:1]) + jnp.exp2(logits - col)
            r_id = lax.broadcasted_iota(jnp.int32, (tile, rows), 0) + t * tile - pos * rows
            c_id = lax.broadcasted_iota(jnp.int32, (tile, rows), 1)
            target = jnp.where(r_id == c_id, 1.0, 0.0)
            w_out[b, part, 0:rows] = (probs[:, 0:rows] - target).astype(jnp.bfloat16)
            w_out[b, part, rows:] = probs[:, rows:].astype(jnp.bfloat16)
            grad = jnp.dot(w_out[b, part, :], cands[buf], preferred_element_type=jnp.float32)
            dq_out[b, part, :] = grad.astype(jnp.bfloat16)


def passage_kernel(chunk, chunks, inner, picks, *refs):
    pos_ref, slot_ref, own_q = refs[:3]
    place = 3
    lefts, rights = [], []
    for _ in range(chunks):
        lefts.append(refs[place:place + inner - 1])
        rights.append(refs[place + inner - 1:place + 2 * inner - 2])
        place += 2 * inner - 2
    w_refs = refs[place:place + chunks]
    own_out, far_out, far_acc, w_buf, whole_q, sems = refs[place + chunks:]
    rows = own_q.shape[1]
    total = chunk * chunks

    def fetcher(b):
        c = b // chunk
        return Fetch(c * chunk, inner, picks, pos_ref, slot_ref, own_q, lefts[c], rights[c], None, None,
                     None, whole_q, sems), b % chunk

    def w_copy(b, buf):
        return pltpu.make_async_copy(w_refs[b // chunk].at[b % chunk], w_buf.at[buf], sems.at[buf, 0])

    def start(b):
        f, local = fetcher(b)
        f.start_q(local, b % 2)
        w_copy(b, b % 2).start()

    start(0)
    far_acc[...] = jnp.zeros_like(far_acc)
    for b in range(total):
        buf = b % 2
        if b + 1 < total:
            start(b + 1)
        f, local = fetcher(b)
        f.wait_q(local, buf)
        w_copy(b, buf).wait()
        for k in range(picks + 1):
            part = lax.dot_general(
                w_buf[buf, :, k * rows:(k + 1) * rows], whole_q[buf],
                (((0,), (0,)), ((), ())), preferred_element_type=jnp.float32,
            )
            if k == 0:
                own_out[b] = part
            else:
                slot = slot_ref[b * picks + k - 1]
                far_acc[slot] = far_acc[slot] + part
    far_out[...] = far_acc[...].astype(jnp.bfloat16)


def finish_kernel(slots, dest_ref, own_ref, far_ref, out_ref, acc):
    acc[0:own_ref.shape[0]] = own_ref[...]
    for e in range(slots):
        dest = dest_ref[e]
        acc[dest] = acc[dest] + far_ref[e].astype(jnp.float32)
    out_ref[...] = acc[0:own_ref.shape[0]].astype(jnp.bfloat16)


def butterfly(value, axis, size, join):
    step = 1
    while step < size:
        other = lax.ppermute(value, axis, [(i, i ^ step) for i in range(size)])
        value = join(value, other)
        step *= 2
    return value


def body(queries, passages, neg_lists):
    per_group, rows, width = queries.shape
    picks = neg_lists.shape[1]
    blocks = neg_lists.shape[0]
    groups = lax.axis_size("dp")
    inner = lax.axis_size("inner")
    full = rows * inner
    cand_rows = (picks + 1) * rows
    slot_count = groups * CAP
    scale = 1.0 / math.sqrt(width)
    my_group = lax.axis_index("dp")
    pos = lax.axis_index("inner")
    chunks = 2
    chunk = per_group // chunks

    slot_ranks, slot_block, slot_live = slot_tables(neg_lists, groups, per_group, CAP)
    listed = lax.dynamic_slice_in_dim(neg_lists, my_group * per_group, per_group, 0)
    my_ranks = lax.dynamic_index_in_dim(slot_ranks, my_group, 0, keepdims=False)
    slot_of = (listed // per_group) * CAP + my_ranks[listed // per_group, listed % per_group]
    slot_flat = slot_of.reshape(-1)
    own_ids = my_group * per_group + jnp.arange(per_group, dtype=jnp.int32)
    id_flat = jnp.concatenate([own_ids[:, None], listed], axis=1).reshape(-1)
    pos_arr = pos.reshape(1)
    sends_for = lax.dynamic_index_in_dim(slot_block, my_group, 1, keepdims=False)
    live_for = lax.dynamic_index_in_dim(slot_live, my_group, 1, keepdims=False)

    lefts = [[] for _ in range(chunks)]
    rights = [[] for _ in range(chunks)]
    moving_r = [queries[c * chunk:(c + 1) * chunk] for c in range(chunks)]
    moving_l = list(moving_r)
    for s in range(1, inner):
        for c in range(chunks):
            moving_r[c] = lax.ppermute(moving_r[c], "inner", [(i, i + 1) for i in range(s - 1, inner - 1)])
            moving_l[c] = lax.ppermute(moving_l[c], "inner", [(i, i - 1) for i in range(inner - s, 0, -1)])
            lefts[c].append(moving_r[c])
            rights[c].append(moving_l[c])

    outgoing = passages[sends_for]
    arrived = lax.all_to_all(outgoing, "dp", split_axis=0, concat_axis=0, tiled=True)
    arrived = arrived.reshape(slot_count, rows, width)

    fetch_scratch = [
        pltpu.VMEM((2, cand_rows, width), jnp.bfloat16),
        pltpu.VMEM((2, full, width), jnp.bfloat16),
        pltpu.SemaphoreType.DMA((2, picks + 1 + inner)),
    ]
    params = pltpu.CompilerParams(vmem_limit_bytes=VMEM_LIMIT)
    tile_flops = 2 * full * cand_rows * width

    col = jnp.full((blocks, rows), NEG_FILL, jnp.float32)
    row_parts = []
    for c in range(chunks):
        row_part, col = pl.pallas_call(
            functools.partial(forward_kernel, c * chunk, chunk, inner, picks, scale * LOG2E),
            out_shape=(
                jax.ShapeDtypeStruct((chunk, full), jnp.float32),
                jax.ShapeDtypeStruct((blocks, rows), jnp.float32),
            ),
            in_specs=[SMEM] * 3 + [ANY] * (2 * inner + 1) + [VMEM],
            out_specs=(VMEM, VMEM),
            scratch_shapes=fetch_scratch,
            compiler_params=params,
            cost_estimate=pl.CostEstimate(
                flops=chunk * tile_flops, bytes_accessed=chunk * (full + cand_rows) * width * 2, transcendentals=0
            ),
            name=f"forward_{c}",
        )(pos_arr, slot_flat, id_flat, queries, *lefts[c], *rights[c], passages, arrived, col)
        row_parts.append(row_part)
    row = jnp.concatenate(row_parts, axis=0)
    col_lse = butterfly(col, "dp", groups, join_log2)
    row_lse = butterfly(row, "inner", inner, join_log2)

    dq, weights = [], []
    for c in range(chunks):
        grad, weight = pl.pallas_call(
            functools.partial(query_kernel, c * chunk, chunk, inner, picks, scale * LOG2E),
            out_shape=(
                jax.ShapeDtypeStruct((chunk, full, width), jnp.bfloat16),
                jax.ShapeDtypeStruct((chunk, full, cand_rows), jnp.bfloat16),
            ),
            in_specs=[SMEM] * 3 + [ANY] * (2 * inner + 1) + [VMEM, VMEM],
            out_specs=(VMEM, VMEM),
            scratch_shapes=fetch_scratch,
            compiler_params=params,
            cost_estimate=pl.CostEstimate(
                flops=2 * chunk * tile_flops, bytes_accessed=chunk * (full + cand_rows) * width * 4, transcendentals=0
            ),
            name=f"query_{c}",
        )(pos_arr, slot_flat, id_flat, queries, *lefts[c], *rights[c], passages, arrived, row_lse, col_lse)
        dq.append(grad)
        weights.append(weight)

    rings = []
    for c in range(chunks):
        rings += [*lefts[c], *rights[c]]
    own_grad, far_grad = pl.pallas_call(
        functools.partial(passage_kernel, chunk, chunks, inner, picks),
        out_shape=(
            jax.ShapeDtypeStruct((per_group, rows, width), jnp.float32),
            jax.ShapeDtypeStruct((slot_count, rows, width), jnp.bfloat16),
        ),
        in_specs=[SMEM] * 2 + [ANY] * (1 + chunks * (2 * inner - 1)),
        out_specs=(VMEM, VMEM),
        scratch_shapes=[
            pltpu.VMEM((slot_count, rows, width), jnp.float32),
            pltpu.VMEM((2, full, cand_rows), jnp.bfloat16),
            pltpu.VMEM((2, full, width), jnp.bfloat16),
            pltpu.SemaphoreType.DMA((2, picks + 1 + inner)),
        ],
        compiler_params=params,
        cost_estimate=pl.CostEstimate(
            flops=per_group * tile_flops, bytes_accessed=per_group * (full + cand_rows) * width * 4, transcendentals=0
        ),
        name="passage",
    )(pos_arr, slot_flat, queries, *rings, *weights)

    f32 = jnp.float32
    query_parts = []
    for c in range(chunks):
        parts = dq[c].reshape(chunk, inner, rows, width)

        def part_of(target):
            target = jnp.clip(target, 0, inner - 1)
            return lax.dynamic_index_in_dim(parts, target, 1, keepdims=False).astype(f32)

        going_r = going_l = None
        for s in range(1, inner):
            out_r = part_of(inner - s + pos)
            out_l = part_of(pos + s - inner)
            if going_r is not None:
                out_r = out_r + going_r
                out_l = out_l + going_l
            going_r = lax.ppermute(out_r.astype(jnp.bfloat16), "inner", [(i, i + 1) for i in range(s)])
            going_l = lax.ppermute(
                out_l.astype(jnp.bfloat16), "inner", [(i, i - 1) for i in range(inner - 1, inner - 1 - s, -1)]
            )
        query_parts.append((part_of(pos) + going_r + going_l).astype(jnp.bfloat16))
    query_grad = jnp.concatenate(query_parts, axis=0)

    returned = lax.all_to_all(
        far_grad.reshape(groups, CAP, rows, width), "dp", split_axis=0, concat_axis=0, tiled=True
    ).reshape(slot_count, rows, width)
    dest = jnp.where(live_for, sends_for, per_group).reshape(-1)
    passage_grad = pl.pallas_call(
        functools.partial(finish_kernel, slot_count),
        out_shape=jax.ShapeDtypeStruct((per_group, rows, width), jnp.bfloat16),
        in_specs=[SMEM, VMEM, VMEM],
        out_specs=VMEM,
        scratch_shapes=[pltpu.VMEM((per_group + 1, rows, width), f32)],
        compiler_params=params,
        name="finish",
    )(dest, own_grad, returned)

    own_scores = jnp.einsum("lrd,lrd->lr", queries, passages, preferred_element_type=f32) * scale
    my_row = lax.dynamic_slice_in_dim(row_lse, pos * rows, rows, 1) * LN2
    my_col = lax.dynamic_slice_in_dim(col_lse, my_group * per_group, per_group, 0) * LN2
    loss = jnp.sum(my_row - own_scores) + jnp.sum(my_col - own_scores)
    loss = butterfly(loss.reshape(1, 1), "dp", groups, jnp.add)
    loss = butterfly(loss, "inner", inner, jnp.add)
    mean_loss = loss[0, 0] / (2.0 * groups * per_group * full)
    return (mean_loss, query_grad, passage_grad)


def solution(mesh):
    in_specs = (P("dp", "inner", None), P("dp", "inner", None), P())
    out_specs = (P(), P("dp", "inner", None), P("dp", "inner", None))
    return jax.shard_map(body, mesh=mesh, in_specs=in_specs, out_specs=out_specs, check_vma=False)
```

time: 461 us -> 236 us (0.51)
  local copies, waits for them, and re-layouts: 127 us -> 10.3 us
  blocking collectives: 98.1 us -> 0 us
  starting transfers between devices: 21.3 us -> 89.7 us
  matrix products: 51.2 us -> 0 us
  Pallas kernels: 0 us -> 49.2 us
  other arithmetic: 51.3 us -> 17.2 us
  loops' own time: 16.2 us -> 0 us
  waiting for transfers between devices: 74.9 us -> 61.9 us
  between operations: 17.5 us -> 6.62 us
    psum x2 -> x0, blocking collectives: 88.8 us -> none  [the longest x1 79.1 us: body(): lax.psum(local_loss, ('dp', 'inner'))]
    ppermute x0 -> x34, starting transfers between devices: none -> 79.9 us  [the longest x6 30.1 us: body(): lax.ppermute(out_r.astype(jnp.bfloat16), 'inner', [(i, i + 1) for i in ra...]
    ppermute x0 -> x34, waiting for transfers between devices: none -> 61.9 us  [the longest x6 35.6 us: body(): lax.ppermute(moving_l[c], 'inner', [(i, i - 1) for i in range(inner - s,...]
    dot_general x18 -> x0, matrix products: 51.2 us -> none  [the longest x8 25.1 us: scores(): jnp.einsum('cd,rd->cr', candidates(block_index), query_block, preferred_e...]
    pallas_call x0 -> x6, Pallas kernels: none -> 49.2 us  [the longest x2 20.6 us: body(): pl.pallas_call(functools.partial(query_kernel, c * chunk, chunk, inner, p...]
    all_to_all x1, waiting for transfers between devices: 46.1 us -> 0.01 us  [body(): lax.all_to_all(outgoing, 'dp', split_axis=0, concat_axis=0, tiled=True)]
    dynamic_update_slice x24 -> x0, local copies, waits for them, and re-layouts: 45.3 us -> none  [the longest x8 44.3 us: backward(): lax.dynamic_update_index_in_dim(own_grad, passage_part[:slice_rows], bloc...]
    scatter-add x4 -> x0, other arithmetic: 37.6 us -> none  [backward(): slot_grad.at[slot_targets]]
  transfers between devices with their start and end apart: 7 -> 36, of which waited for: 4 -> 22; matrix products, arithmetic and copies ran while one was open for 7% -> 9% of each run, Pallas kernels for 0% -> 3%
where the time goes in v1:
time: 236 us; the launch traced here: 235 us
  starting transfers between devices  89.7 us (38%)
  waiting for transfers between devices  61.9 us (26%)
  Pallas kernels  49.2 us (21%)
  other arithmetic  17.2 us (7%)
  local copies, waits for them, and re-layouts  10.3 us (4%)
  between operations  6.62 us (3%)
    ppermute x6, waiting for transfers between devices, body(): lax.ppermute(moving_l[c], 'inner', [(i, i - 1) for i in range(inner - s,...  35.6 us
    ppermute x6, starting transfers between devices, body(): lax.ppermute(out_r.astype(jnp.bfloat16), 'inner', [(i, i + 1) for i in ra...  30.1 us
    pallas_call x2, Pallas kernels, body(): pl.pallas_call(functools.partial(query_kernel, c * chunk, chunk, inner, p...  20.6 us
    ppermute x10, starting transfers between devices, butterfly(): other = lax.ppermute(value, axis, [(i, i ^ step) for i in range(size)])  17.9 us
    ppermute x6, starting transfers between devices, body(): lax.ppermute(moving_r[c], 'inner', [(i, i + 1) for i in range(s - 1, inne...  15.7 us
    pallas_call x2, Pallas kernels, body(): pl.pallas_call(functools.partial(forward_kernel, c * chunk, chunk, inner,...  13.9 us
    convert_element_type x4, other arithmetic, body(): out_r.astype(jnp.bfloat16)  11 us
    pallas_call x1, Pallas kernels, body(): pl.pallas_call(functools.partial(passage_kernel, chunk, chunks, inner, pi...  10.5 us
  transfers between devices with their start and end apart: 36, of which 22 were waited for; matrix products, arithmetic and copies ran while one was open for 9% of the time, Pallas kernels for 3%

profile of v1, /device:TPU:0, one launch (start us, length us, event | category | flops | bytes accessed | tf_op | source)
XLA Modules:
  0.0 234.9 jit_solution(7983558937525347404)
XLA Ops:
  2.3 4.1 %gather_fusion.1 = bf16[16,128,1024]{2,1,0:T(8,128)(2,1)} fusion(bf16[4,128,1024]{2,1,0:T(8,128)(2,1)} %refs_10_.7, s32[1024]{0:T(1024)S(1)} %pad_clamp_fusion), kind=kCustom, calls=%fused_computation.1 | custom fusion | bytes 8388672 | tf_op jit(solution)/shard_map/gather | solution.py:273
  6.4 5.3 %all-to-all-start = ((bf16[8,2,128,1024]{3,2,1,0:T(8,128)(2,1)}), bf16[8,2,128,1024]{3,2,1,0:T(8,128)(2,1)}, u32[]{:S(2)}, u32[]{:S(2)}) async-start(bf16[8,2,128,1024]{3,2,1,0:T(8,128)(2,1)} %bitcast.77), calls=%async_computation | async-start | bytes 8388608 | tf_op jit(solution)/shard_map/all_to_all | solution.py:274
  11.8 4.5 %collective-permute-start = (bf16[2,128,1024]{2,1,0:T(8,128)(2,1)S(1)}, bf16[2,128,1024]{2,1,0:T(8,128)(2,1)S(1)}, u32[]{:S(2)}, u32[]{:S(2)}) collective-permute-start(bf16[2,128,1024]{2,1,0:T(8,128)(2,1)S(1)} %get-tuple-element.39), channel_id=1, source_target_pairs={{0,1},{1,2},{2,3},{4,5},{5,6},{6,7},{8,9},{9,10},{10,11},{12,13},{... | collective-permute-start | bytes 1572872 | tf_op jit(solution)/shard_map/ppermute | solution.py:268
  17.6 5.3 %collective-permute-start.6 = (bf16[2,128,1024]{2,1,0:T(8,128)(2,1)S(1)}, bf16[2,128,1024]{2,1,0:T(8,128)(2,1)}, u32[]{:S(2)}, u32[]{:S(2)}) collective-permute-start(bf16[2,128,1024]{2,1,0:T(8,128)(2,1)S(1)} %get-tuple-element.40), channel_id=1, source_target_pairs={{0,1},{1,2},{2,3},{4,5},{5,6},{6,7},{8,9},{9,10},{10,11},{12,13},{... | collective-permute-start | bytes 1572872 | tf_op jit(solution)/shard_map/ppermute | solution.py:268
  24.2 4.3 %collective-permute-done.refs_4_.refs_3_ = bf16[2,128,1024]{2,1,0:T(8,128)(2,1)S(1)} collective-permute-done((bf16[2,128,1024]{2,1,0:T(8,128)(2,1)S(1)}, bf16[2,128,1024]{2,1,0:T(8,128)(2,1)S(1)}, u32[]{:S(2)}, u32[]{:S(2)}) %collective-permute-start) | collective-permute-done | bytes 524320 | tf_op jit(solution)/shard_map/ppermute | solution.py:268
  29.9 3.0 %collective-permute-done.3.refs_7_.refs_6_ = bf16[2,128,1024]{2,1,0:T(8,128)(2,1)S(1)} collective-permute-done((bf16[2,128,1024]{2,1,0:T(8,128)(2,1)S(1)}, bf16[2,128,1024]{2,1,0:T(8,128)(2,1)S(1)}, u32[]{:S(2)}, u32[]{:S(2)}) %collective-permute-start.3) | collective-permute-done | bytes 524320 | tf_op jit(solution)/shard_map/ppermute | solution.py:269
  34.3 4.9 %collective-permute-done.6.refs_4_.refs_9_ = bf16[2,128,1024]{2,1,0:T(8,128)(2,1)} collective-permute-done((bf16[2,128,1024]{2,1,0:T(8,128)(2,1)S(1)}, bf16[2,128,1024]{2,1,0:T(8,128)(2,1)}, u32[]{:S(2)}, u32[]{:S(2)}) %collective-permute-start.6) | collective-permute-done | bytes 524320 | tf_op jit(solution)/shard_map/ppermute | solution.py:268
  40.6 3.7 %collective-permute-done.9.refs_7_.refs_12_ = bf16[2,128,1024]{2,1,0:T(8,128)(2,1)} collective-permute-done((bf16[2,128,1024]{2,1,0:T(8,128)(2,1)S(1)}, bf16[2,128,1024]{2,1,0:T(8,128)(2,1)}, u32[]{:S(2)}, u32[]{:S(2)}) %collective-permute-start.9) | collective-permute-done | bytes 524320 | tf_op jit(solution)/shard_map/ppermute | solution.py:269
  47.3 8.3 %collective-permute-done.4.refs_8_.refs_7_ = bf16[2,128,1024]{2,1,0:T(8,128)(2,1)} collective-permute-done((bf16[2,128,1024]{2,1,0:T(8,128)(2,1)S(1)}, bf16[2,128,1024]{2,1,0:T(8,128)(2,1)}, u32[]{:S(2)}, u32[]{:S(2)}) %collective-permute-start.4) | collective-permute-done | bytes 524320 | tf_op jit(solution)/shard_map/ppermute | solution.py:269
  59.2 7.5 %collective-permute-done.10.refs_8_.refs_13_ = bf16[2,128,1024]{2,1,0:T(8,128)(2,1)} collective-permute-done((bf16[2,128,1024]{2,1,0:T(8,128)(2,1)}, bf16[2,128,1024]{2,1,0:T(8,128)(2,1)}, u32[]{:S(2)}, u32[]{:S(2)}) %collective-permute-start.10) | collective-permute-done | bytes 524320 | tf_op jit(solution)/shard_map/ppermute | solution.py:269
  68.3 9.7 %collective-permute-done.5.refs_9_.refs_8_ = bf16[2,128,1024]{2,1,0:T(8,128)(2,1)} collective-permute-done((bf16[2,128,1024]{2,1,0:T(8,128)(2,1)}, bf16[2,128,1024]{2,1,0:T(8,128)(2,1)}, u32[]{:S(2)}, u32[]{:S(2)}) %collective-permute-start.5) | collective-permute-done | bytes 524320 | tf_op jit(solution)/shard_map/ppermute | solution.py:269
  78.0 6.9 %forward_0.1 = (f32[2,512]{1,0:T(2,128)S(1)}, f32[32,128]{1,0:T(8,128)S(1)}) custom-call(s32[1]{0:T(128)} %bitcast.refs_0_, s32[32]{0:T(128)S(1)} %reshape.114.refs_1_, s32[36]{0:T(128)S(1)} %reshape.115.refs_2_, bf16[4,128,1024]{2,1,0:T(8,128)(2,1)S(1)} %copy-done.1, bf16[2,128,1024]{2,1,0:T(8,128)(2,1)S(1)} %collective-permute-done.refs_4_.refs_3_, ...), custom_call_target="tpu_custom_call" | custom-call | flops 2415919104 | bytes 6815744 | tf_op jit(solution)/shard_map/forward_0/pallas_call | solution.py:288
  85.0 3.4 %collective-permute-done.11.refs_9_.refs_14_ = bf16[2,128,1024]{2,1,0:T(8,128)(2,1)} collective-permute-done((bf16[2,128,1024]{2,1,0:T(8,128)(2,1)}, bf16[2,128,1024]{2,1,0:T(8,128)(2,1)}, u32[]{:S(2)}, u32[]{:S(2)}) %collective-permute-start.11) | collective-permute-done | bytes 524320 | tf_op jit(solution)/shard_map/ppermute | solution.py:269
  88.4 7.0 %forward_1.1 = (f32[2,512]{1,0:T(2,128)S(1)}, f32[32,128]{1,0:T(8,128)S(1)}) custom-call(s32[1]{0:T(128)} %bitcast.refs_0_, s32[32]{0:T(128)S(1)} %reshape.114.refs_1_, s32[36]{0:T(128)S(1)} %reshape.115.refs_2_, bf16[4,128,1024]{2,1,0:T(8,128)(2,1)S(1)} %copy-done.1, bf16[2,128,1024]{2,1,0:T(8,128)(2,1)} %collective-permute-done.6.refs_4_.refs_9_, ...), custom_call_target="tpu_custom_call" | custom-call | flops 2415919104 | bytes 6815744 | tf_op jit(solution)/shard_map/forward_1/pallas_call | solution.py:288
  104.3 10.3 %query_1.1 = (bf16[2,512,1024]{2,1,0:T(8,128)(2,1)}, bf16[2,512,1152]{2,1,0:T(8,128)(2,1)}) custom-call(s32[1]{0:T(128)} %bitcast.refs_0_, s32[32]{0:T(128)S(1)} %reshape.114.refs_1_, s32[36]{0:T(128)S(1)} %reshape.115.refs_2_, bf16[4,128,1024]{2,1,0:T(8,128)(2,1)S(1)} %copy-done.1, bf16[2,128,1024]{2,1,0:T(8,128)(2,1)} %collective-permute-done.6.refs_4_.refs_9_, ...), custom_call_target="tpu_custom_call" | custom-call | flops 4831838208 | bytes 13631488 | tf_op jit(solution)/shard_map/query_1/pallas_call | solution.py:310
  114.6 10.3 %query_0.1 = (bf16[2,512,1024]{2,1,0:T(8,128)(2,1)}, bf16[2,512,1152]{2,1,0:T(8,128)(2,1)}) custom-call(s32[1]{0:T(128)} %bitcast.refs_0_, s32[32]{0:T(128)S(1)} %reshape.114.refs_1_, s32[36]{0:T(128)S(1)} %reshape.115.refs_2_, bf16[4,128,1024]{2,1,0:T(8,128)(2,1)S(1)} %copy-done.1, bf16[2,128,1024]{2,1,0:T(8,128)(2,1)S(1)} %collective-permute-done.refs_4_.refs_3_, ...), custom_call_target="tpu_custom_call" | custom-call | flops 4831838208 | bytes 13631488 | tf_op jit(solution)/shard_map/query_0/pallas_call | solution.py:310
  124.9 10.5 %passage.1 = (f32[4,128,1024]{2,1,0:T(8,128)}, bf16[16,128,1024]{2,1,0:T(8,128)(2,1)}) custom-call(s32[1]{0:T(128)} %bitcast.refs_0_, s32[32]{0:T(128)S(1)} %reshape.114.refs_1_, bf16[4,128,1024]{2,1,0:T(8,128)(2,1)} %refs_2_.1, bf16[2,128,1024]{2,1,0:T(8,128)(2,1)S(1)} %collective-permute-done.refs_4_.refs_3_, ...), custom_call_target="tpu_custom_call" | custom-call | flops 4831838208 | bytes 27262976 | tf_op jit(solution)/shard_map/passage/pallas_call | solution.py:331
  135.4 4.6 %all-to-all-start.1 = ((bf16[8,2,128,1024]{3,2,1,0:T(8,128)(2,1)}), bf16[8,2,128,1024]{3,2,1,0:T(8,128)(2,1)}, u32[]{:S(2)}, u32[]{:S(2)}) async-start(bf16[8,2,128,1024]{3,2,1,0:T(8,128)(2,1)} %bitcast.86), calls=%async_computation.1 | async-start | bytes 8388608 | tf_op jit(solution)/shard_map/all_to_all | solution.py:375
  142.4 3.7 %collective-permute-start.28 = (bf16[2,128,1024]{2,1,0:T(8,128)(2,1)}, bf16[2,128,1024]{2,1,0:T(8,128)(2,1)}, u32[]{:S(2)}, u32[]{:S(2)}) collective-permute-start(bf16[2,128,1024]{2,1,0:T(8,128)(2,1)} %get-tuple-element.37), channel_id=1, source_target_pairs={{0,1},{4,5},{8,9},{12,13},{16,17},{20,21},{24,25},{28,29}} | collective-permute-start | bytes 1572872 | tf_op jit(solution)/shard_map/ppermute | solution.py:368
  152.1 5.7 %collective-permute-done.28 = bf16[2,128,1024]{2,1,0:T(8,128)(2,1)} collective-permute-done((bf16[2,128,1024]{2,1,0:T(8,128)(2,1)}, bf16[2,128,1024]{2,1,0:T(8,128)(2,1)}, u32[]{:S(2)}, u32[]{:S(2)}) %collective-permute-start.28) | collective-permute-done | bytes 524320 | tf_op jit(solution)/shard_map/ppermute | solution.py:368
  157.7 2.9 %fusion.3 = (bf16[2,128,1024]{2,1,0:T(8,128)(2,1)}, bf16[2,128,1024]{2,1,0:T(8,128)(2,1)}) fusion(bf16[2,128,1024]{2,1,0:T(8,128)(2,1)} %collective-permute-done.28, bf16[2,4,128,1024]{3,2,1,0:T(8,128)(2,1)} %bitcast.83, s32[]{:T(128)S(6)} %min.31, bf16[2,128,1024]{2,1,0:T(8,128)(2,1)} %collective-permute-done.31, s32[]{:T(128)S(6)} %min.34), kind=kLoop, calls=%fused_computation.10 | loop fusion | flops 2097152 | bytes 3145736 | tf_op jit(solution)/shard_map/convert_element_type | solution.py:368
  160.6 5.3 %collective-permute-start.29 = (bf16[2,128,1024]{2,1,0:T(8,128)(2,1)}, bf16[2,128,1024]{2,1,0:T(8,128)(2,1)}, u32[]{:S(2)}, u32[]{:S(2)}) collective-permute-start(bf16[2,128,1024]{2,1,0:T(8,128)(2,1)} %get-tuple-element.35), channel_id=1, source_target_pairs={{0,1},{1,2},{4,5},{5,6},{8,9},{9,10},{12,13},{13,14},{16,17},{17,1... | collective-permute-start | bytes 1572872 | tf_op jit(solution)/shard_map/ppermute | solution.py:368
  171.6 5.2 %collective-permute-start.23 = (bf16[2,128,1024]{2,1,0:T(8,128)(2,1)}, bf16[2,128,1024]{2,1,0:T(8,128)(2,1)}, u32[]{:S(2)}, u32[]{:S(2)}) collective-permute-start(bf16[2,128,1024]{2,1,0:T(8,128)(2,1)} %get-tuple-element.29), channel_id=1, source_target_pairs={{0,1},{1,2},{4,5},{5,6},{8,9},{9,10},{12,13},{13,14},{16,17},{17,1... | collective-permute-start | bytes 1572872 | tf_op jit(solution)/shard_map/ppermute | solution.py:368
  180.2 2.9 %fusion.4 = (bf16[2,128,1024]{2,1,0:T(8,128)(2,1)}, bf16[2,128,1024]{2,1,0:T(8,128)(2,1)}) fusion(bf16[2,128,1024]{2,1,0:T(8,128)(2,1)} %collective-permute-done.29, bf16[2,4,128,1024]{3,2,1,0:T(8,128)(2,1)} %bitcast.84, s32[]{:T(128)S(6)} %min.30, bf16[2,128,1024]{2,1,0:T(8,128)(2,1)} %collective-permute-done.32, s32[]{:T(128)S(6)} %min.33), kind=kLoop, calls=%fused_computation.12 | loop fusion | flops 2097152 | bytes 3145736 | tf_op jit(solution)/shard_map/convert_element_type | solution.py:368
  184.5 6.0 %collective-permute-start.30 = (bf16[2,128,1024]{2,1,0:T(8,128)(2,1)}, bf16[2,128,1024]{2,1,0:T(8,128)(2,1)}, u32[]{:S(2)}, u32[]{:S(2)}) collective-permute-start(bf16[2,128,1024]{2,1,0:T(8,128)(2,1)} %get-tuple-element.33), channel_id=1, source_target_pairs={{0,1},{1,2},{2,3},{4,5},{5,6},{6,7},{8,9},{9,10},{10,11},{12,13},{... | collective-permute-start | bytes 1572872 | tf_op jit(solution)/shard_map/ppermute | solution.py:368
  191.5 2.6 %fusion.10 = (bf16[2,128,1024]{2,1,0:T(8,128)(2,1)}, bf16[2,128,1024]{2,1,0:T(8,128)(2,1)}) fusion(bf16[2,128,1024]{2,1,0:T(8,128)(2,1)} %collective-permute-done.23, bf16[2,4,128,1024]{3,2,1,0:T(8,128)(2,1)S(1)} %bitcast.81, s32[]{:T(128)S(6)} %min.30, bf16[2,128,1024]{2,1,0:T(8,128)(2,1)} %collective-permute-done.26, s32[]{:T(128)S(6)} %min.33), kind=kLoop, calls=%fused_computation.23 | loop fusion | flops 2097152 | bytes 3145736 | tf_op jit(solution)/shard_map/convert_element_type | solution.py:368
  195.3 7.8 %collective-permute-start.24 = (bf16[2,128,1024]{2,1,0:T(8,128)(2,1)}, bf16[2,128,1024]{2,1,0:T(8,128)(2,1)}, u32[]{:S(2)}, u32[]{:S(2)}) collective-permute-start(bf16[2,128,1024]{2,1,0:T(8,128)(2,1)} %get-tuple-element.27), channel_id=1, source_target_pairs={{0,1},{1,2},{2,3},{4,5},{5,6},{6,7},{8,9},{9,10},{10,11},{12,13},{... | collective-permute-start | bytes 1572872 | tf_op jit(solution)/shard_map/ppermute | solution.py:368
  207.3 3.3 %collective-permute-start.18 = (f32[1,1]{1,0:T(1,128)}, f32[1,1]{1,0:T(1,128)}, u32[]{:S(2)}, u32[]{:S(2)}) collective-permute-start(f32[1,1]{1,0:T(1,128)} %add.211), channel_id=1, source_target_pairs={{0,8},{4,12},{8,0},{12,4},{16,24},{20,28},{24,16},{28,20},{1,9},{5... | collective-permute-start | bytes 20 | tf_op jit(solution)/shard_map/ppermute | solution.py:230
  211.5 3.3 %collective-permute-start.19 = (f32[1,1]{1,0:T(1,128)}, f32[1,1]{1,0:T(1,128)}, u32[]{:S(2)}, u32[]{:S(2)}) collective-permute-start(f32[1,1]{1,0:T(1,128)} %add.212), channel_id=1, source_target_pairs={{0,16},{4,20},{8,24},{12,28},{16,0},{20,4},{24,8},{28,12},{1,17},{... | collective-permute-start | bytes 20 | tf_op jit(solution)/shard_map/ppermute | solution.py:230
  215.7 2.8 %collective-permute-start.20 = (f32[1,1]{1,0:T(1,128)}, f32[1,1]{1,0:T(1,128)}, u32[]{:S(2)}, u32[]{:S(2)}) collective-permute-start(f32[1,1]{1,0:T(1,128)} %add.213), channel_id=1, source_target_pairs={{0,1},{1,0},{2,3},{3,2},{4,5},{5,4},{6,7},{7,6},{8,9},{9,8},{10,11... | collective-permute-start | bytes 20 | tf_op jit(solution)/shard_map/ppermute | solution.py:230
  219.9 4.0 %collective-permute-start.21 = (f32[1,1]{1,0:T(1,128)}, f32[1,1]{1,0:T(1,128)}, u32[]{:S(2)}, u32[]{:S(2)}) collective-permute-start(f32[1,1]{1,0:T(1,128)} %add.214), channel_id=1, source_target_pairs={{0,2},{1,3},{2,0},{3,1},{4,6},{5,7},{6,4},{7,5},{8,10},{9,11},{10,... | collective-permute-start | bytes 20 | tf_op jit(solution)/shard_map/ppermute | solution.py:230
  229.6 4.2 %finish.1 = bf16[4,128,1024]{2,1,0:T(8,128)(2,1)} custom-call(s32[16]{0:T(128)S(1)} %select_n.81.dest_ref, f32[4,128,1024]{2,1,0:T(8,128)S(1)} %copy-done.3, bf16[16,128,1024]{2,1,0:T(8,128)(2,1)} %bitcast.25.far_ref), custom_call_target="tpu_custom_call" | custom-call | tf_op jit(solution)/shard_map/finish/pallas_call | solution.py:379
  (106 shorter events, 55.1 us)
Async XLA Ops:
  6.4 71.6 %all-to-all-start = ((bf16[8,2,128,1024]{3,2,1,0:T(8,128)(2,1)}), bf16[8,2,128,1024]{3,2,1,0:T(8,128)(2,1)}, u32[]{:S(2)}, u32[]{:S(2)}) async-start(bf16[8,2,128,1024]{3,2,1,0:T(8,128)(2,1)} %bitcast.77), calls=%async_computation | async-start | bytes 8388608 | tf_op jit(solution)/shard_map/all_to_all | solution.py:274
  11.8 16.7 %collective-permute-start = (bf16[2,128,1024]{2,1,0:T(8,128)(2,1)S(1)}, bf16[2,128,1024]{2,1,0:T(8,128)(2,1)S(1)}, u32[]{:S(2)}, u32[]{:S(2)}) collective-permute-start(bf16[2,128,1024]{2,1,0:T(8,128)(2,1)S(1)} %get-tuple-element.39), channel_id=1, source_target_pairs={{0,1},{1,2},{2,3},{4,5},{5,6},{6,7},{8,9},{9,10},{10,11},{12,13},{... | collective-permute-start | bytes 1572872 | tf_op jit(solution)/shard_map/ppermute | solution.py:268
  16.3 16.7 %collective-permute-start.3 = (bf16[2,128,1024]{2,1,0:T(8,128)(2,1)S(1)}, bf16[2,128,1024]{2,1,0:T(8,128)(2,1)S(1)}, u32[]{:S(2)}, u32[]{:S(2)}) collective-permute-start(bf16[2,128,1024]{2,1,0:T(8,128)(2,1)S(1)} %get-tuple-element.39), channel_id=1, source_target_pairs={{3,2},{2,1},{1,0},{7,6},{6,5},{5,4},{11,10},{10,9},{9,8},{15,14},{... | collective-permute-start | bytes 1572872 | tf_op jit(solution)/shard_map/ppermute | solution.py:269
  17.6 21.6 %collective-permute-start.6 = (bf16[2,128,1024]{2,1,0:T(8,128)(2,1)S(1)}, bf16[2,128,1024]{2,1,0:T(8,128)(2,1)}, u32[]{:S(2)}, u32[]{:S(2)}) collective-permute-start(bf16[2,128,1024]{2,1,0:T(8,128)(2,1)S(1)} %get-tuple-element.40), channel_id=1, source_target_pairs={{0,1},{1,2},{2,3},{4,5},{5,6},{6,7},{8,9},{9,10},{10,11},{12,13},{... | collective-permute-start | bytes 1572872 | tf_op jit(solution)/shard_map/ppermute | solution.py:268
  22.9 21.4 %collective-permute-start.9 = (bf16[2,128,1024]{2,1,0:T(8,128)(2,1)S(1)}, bf16[2,128,1024]{2,1,0:T(8,128)(2,1)}, u32[]{:S(2)}, u32[]{:S(2)}) collective-permute-start(bf16[2,128,1024]{2,1,0:T(8,128)(2,1)S(1)} %get-tuple-element.40), channel_id=1, source_target_pairs={{3,2},{2,1},{1,0},{7,6},{6,5},{5,4},{11,10},{10,9},{9,8},{15,14},{... | collective-permute-start | bytes 1572872 | tf_op jit(solution)/shard_map/ppermute | solution.py:269
  28.5 17.3 %collective-permute-start.1 = (bf16[2,128,1024]{2,1,0:T(8,128)(2,1)S(1)}, bf16[2,128,1024]{2,1,0:T(8,128)(2,1)}, u32[]{:S(2)}, u32[]{:S(2)}) collective-permute-start(bf16[2,128,1024]{2,1,0:T(8,128)(2,1)S(1)} %collective-permute-done.refs_4_.refs_3_), channel_id=1, source_target_pairs={{1,2},{2,3},{5,6},{6,7},{9,10},{10,11},{13,14},{14,15},{17,18},{18... | collective-permute-start | bytes 1572872 | tf_op jit(solution)/shard_map/ppermute | solution.py:268
  33.0 22.6 %collective-permute-start.4 = (bf16[2,128,1024]{2,1,0:T(8,128)(2,1)S(1)}, bf16[2,128,1024]{2,1,0:T(8,128)(2,1)}, u32[]{:S(2)}, u32[]{:S(2)}) collective-permute-start(bf16[2,128,1024]{2,1,0:T(8,128)(2,1)S(1)} %collective-permute-done.3.refs_7_.refs_6_), channel_id=1, source_target_pairs={{2,1},{1,0},{6,5},{5,4},{10,9},{9,8},{14,13},{13,12},{18,17},{17,1... | collective-permute-start | bytes 1572872 | tf_op jit(solution)/shard_map/ppermute | solution.py:269
  39.2 18.6 %collective-permute-start.7 = (bf16[2,128,1024]{2,1,0:T(8,128)(2,1)}, bf16[2,128,1024]{2,1,0:T(8,128)(2,1)}, u32[]{:S(2)}, u32[]{:S(2)}) collective-permute-start(bf16[2,128,1024]{2,1,0:T(8,128)(2,1)} %collective-permute-done.6.refs_4_.refs_9_), channel_id=1, source_target_pairs={{1,2},{2,3},{5,6},{6,7},{9,10},{10,11},{13,14},{14,15},{17,18},{18... | collective-permute-start | bytes 1572872 | tf_op jit(solution)/shard_map/ppermute | solution.py:268
  44.3 22.5 %collective-permute-start.10 = (bf16[2,128,1024]{2,1,0:T(8,128)(2,1)}, bf16[2,128,1024]{2,1,0:T(8,128)(2,1)}, u32[]{:S(2)}, u32[]{:S(2)}) collective-permute-start(bf16[2,128,1024]{2,1,0:T(8,128)(2,1)} %collective-permute-done.9.refs_7_.refs_12_), channel_id=1, source_target_pairs={{2,1},{1,0},{6,5},{5,4},{10,9},{9,8},{14,13},{13,12},{18,17},{17,1... | collective-permute-start | bytes 1572872 | tf_op jit(solution)/shard_map/ppermute | solution.py:269
  45.8 22.6 %collective-permute-start.2 = (bf16[2,128,1024]{2,1,0:T(8,128)(2,1)}, bf16[2,128,1024]{2,1,0:T(8,128)(2,1)}, u32[]{:S(2)}, u32[]{:S(2)}) collective-permute-start(bf16[2,128,1024]{2,1,0:T(8,128)(2,1)} %collective-permute-done.1.refs_5_.refs_4_), channel_id=1, source_target_pairs={{2,3},{6,7},{10,11},{14,15},{18,19},{22,23},{26,27},{30,31}} | collective-permute-start | bytes 1572872 | tf_op jit(solution)/shard_map/ppermute | solution.py:268
  55.5 22.5 %collective-permute-start.5 = (bf16[2,128,1024]{2,1,0:T(8,128)(2,1)}, bf16[2,128,1024]{2,1,0:T(8,128)(2,1)}, u32[]{:S(2)}, u32[]{:S(2)}) collective-permute-start(bf16[2,128,1024]{2,1,0:T(8,128)(2,1)} %collective-permute-done.4.refs_8_.refs_7_), channel_id=1, source_target_pairs={{1,0},{5,4},{9,8},{13,12},{17,16},{21,20},{25,24},{29,28}} | collective-permute-start | bytes 1572872 | tf_op jit(solution)/shard_map/ppermute | solution.py:269
  57.8 27.2 %collective-permute-start.8 = (bf16[2,128,1024]{2,1,0:T(8,128)(2,1)}, bf16[2,128,1024]{2,1,0:T(8,128)(2,1)}, u32[]{:S(2)}, u32[]{:S(2)}) collective-permute-start(bf16[2,128,1024]{2,1,0:T(8,128)(2,1)} %collective-permute-done.7.refs_5_.refs_10_), channel_id=1, source_target_pairs={{2,3},{6,7},{10,11},{14,15},{18,19},{22,23},{26,27},{30,31}} | collective-permute-start | bytes 1572872 | tf_op jit(solution)/shard_map/ppermute | solution.py:268
  66.8 21.6 %collective-permute-start.11 = (bf16[2,128,1024]{2,1,0:T(8,128)(2,1)}, bf16[2,128,1024]{2,1,0:T(8,128)(2,1)}, u32[]{:S(2)}, u32[]{:S(2)}) collective-permute-start(bf16[2,128,1024]{2,1,0:T(8,128)(2,1)} %collective-permute-done.10.refs_8_.refs_13_), channel_id=1, source_target_pairs={{1,0},{5,4},{9,8},{13,12},{17,16},{21,20},{25,24},{29,28}} | collective-permute-start | bytes 1572872 | tf_op jit(solution)/shard_map/ppermute | solution.py:269
  95.5 3.7 %collective-permute-start.12 = (f32[4,512]{1,0:T(4,128)S(1)}, f32[4,512]{1,0:T(4,128)S(1)}, u32[]{:S(2)}, u32[]{:S(2)}) collective-permute-start(f32[4,512]{1,0:T(4,128)S(1)} %pad_maximum_fusion.1), channel_id=1, source_target_pairs={{0,1},{1,0},{2,3},{3,2},{4,5},{5,4},{6,7},{7,6},{8,9},{9,8},{10,11... | collective-permute-start | bytes 24584 | tf_op jit(solution)/shard_map/ppermute | solution.py:230
  96.6 3.8 %collective-permute-start.15 = (f32[32,128]{1,0:T(8,128)S(1)}, f32[32,128]{1,0:T(8,128)S(1)}, u32[]{:S(2)}, u32[]{:S(2)}) collective-permute-start(f32[32,128]{1,0:T(8,128)S(1)} %multiply_add_fusion.2), channel_id=1, source_target_pairs={{0,8},{4,12},{8,0},{12,4},{16,24},{20,28},{24,16},{28,20},{1,9},{5... | collective-permute-start | bytes 49160 | tf_op jit(solution)/shard_map/ppermute | solution.py:230
  99.2 4.6 %collective-permute-start.13 = (f32[4,512]{1,0:T(4,128)S(1)}, f32[4,512]{1,0:T(4,128)S(1)}, u32[]{:S(2)}, u32[]{:S(2)}) collective-permute-start(f32[4,512]{1,0:T(4,128)S(1)} %multiply_add_fusion.4), channel_id=1, source_target_pairs={{0,2},{1,3},{2,0},{3,1},{4,6},{5,7},{6,4},{7,5},{8,10},{9,11},{10,... | collective-permute-start | bytes 24584 | tf_op jit(solution)/shard_map/ppermute | solution.py:230
  100.5 3.8 %collective-permute-start.16 = (f32[32,128]{1,0:T(8,128)S(1)}, f32[32,128]{1,0:T(8,128)S(1)}, u32[]{:S(2)}, u32[]{:S(2)}) collective-permute-start(f32[32,128]{1,0:T(8,128)S(1)} %multiply_add_fusion.1), channel_id=1, source_target_pairs={{0,16},{4,20},{8,24},{12,28},{16,0},{20,4},{24,8},{28,12},{1,17},{... | collective-permute-start | bytes 49160 | tf_op jit(solution)/shard_map/ppermute | solution.py:230
  135.4 94.2 %all-to-all-start.1 = ((bf16[8,2,128,1024]{3,2,1,0:T(8,128)(2,1)}), bf16[8,2,128,1024]{3,2,1,0:T(8,128)(2,1)}, u32[]{:S(2)}, u32[]{:S(2)}) async-start(bf16[8,2,128,1024]{3,2,1,0:T(8,128)(2,1)} %bitcast.86), calls=%async_computation.1 | async-start | bytes 8388608 | tf_op jit(solution)/shard_map/all_to_all | solution.py:375
  142.4 15.3 %collective-permute-start.28 = (bf16[2,128,1024]{2,1,0:T(8,128)(2,1)}, bf16[2,128,1024]{2,1,0:T(8,128)(2,1)}, u32[]{:S(2)}, u32[]{:S(2)}) collective-permute-start(bf16[2,128,1024]{2,1,0:T(8,128)(2,1)} %get-tuple-element.37), channel_id=1, source_target_pairs={{0,1},{4,5},{8,9},{12,13},{16,17},{20,21},{24,25},{28,29}} | collective-permute-start | bytes 1572872 | tf_op jit(solution)/shard_map/ppermute | solution.py:368
  146.1 11.7 %collective-permute-start.31 = (bf16[2,128,1024]{2,1,0:T(8,128)(2,1)}, bf16[2,128,1024]{2,1,0:T(8,128)(2,1)}, u32[]{:S(2)}, u32[]{:S(2)}) collective-permute-start(bf16[2,128,1024]{2,1,0:T(8,128)(2,1)} %get-tuple-element.38), channel_id=1, source_target_pairs={{3,2},{7,6},{11,10},{15,14},{19,18},{23,22},{27,26},{31,30}} | collective-permute-start | bytes 1572872 | tf_op jit(solution)/shard_map/ppermute | solution.py:369
  148.6 20.4 %collective-permute-start.22 = (bf16[2,128,1024]{2,1,0:T(8,128)(2,1)}, bf16[2,128,1024]{2,1,0:T(8,128)(2,1)}, u32[]{:S(2)}, u32[]{:S(2)}) collective-permute-start(bf16[2,128,1024]{2,1,0:T(8,128)(2,1)} %get-tuple-element.31), channel_id=1, source_target_pairs={{0,1},{4,5},{8,9},{12,13},{16,17},{20,21},{24,25},{28,29}} | collective-permute-start | bytes 1572872 | tf_op jit(solution)/shard_map/ppermute | solution.py:368
  150.6 18.3 %collective-permute-start.25 = (bf16[2,128,1024]{2,1,0:T(8,128)(2,1)}, bf16[2,128,1024]{2,1,0:T(8,128)(2,1)}, u32[]{:S(2)}, u32[]{:S(2)}) collective-permute-start(bf16[2,128,1024]{2,1,0:T(8,128)(2,1)} %get-tuple-element.32), channel_id=1, source_target_pairs={{3,2},{7,6},{11,10},{15,14},{19,18},{23,22},{27,26},{31,30}} | collective-permute-start | bytes 1572872 | tf_op jit(solution)/shard_map/ppermute | solution.py:369
  160.6 19.6 %collective-permute-start.29 = (bf16[2,128,1024]{2,1,0:T(8,128)(2,1)}, bf16[2,128,1024]{2,1,0:T(8,128)(2,1)}, u32[]{:S(2)}, u32[]{:S(2)}) collective-permute-start(bf16[2,128,1024]{2,1,0:T(8,128)(2,1)} %get-tuple-element.35), channel_id=1, source_target_pairs={{0,1},{1,2},{4,5},{5,6},{8,9},{9,10},{12,13},{13,14},{16,17},{17,1... | collective-permute-start | bytes 1572872 | tf_op jit(solution)/shard_map/ppermute | solution.py:368
  165.9 14.3 %collective-permute-start.32 = (bf16[2,128,1024]{2,1,0:T(8,128)(2,1)}, bf16[2,128,1024]{2,1,0:T(8,128)(2,1)}, u32[]{:S(2)}, u32[]{:S(2)}) collective-permute-start(bf16[2,128,1024]{2,1,0:T(8,128)(2,1)} %get-tuple-element.36), channel_id=1, source_target_pairs={{3,2},{2,1},{7,6},{6,5},{11,10},{10,9},{15,14},{14,13},{19,18},{18... | collective-permute-start | bytes 1572872 | tf_op jit(solution)/shard_map/ppermute | solution.py:369
  171.6 19.9 %collective-permute-start.23 = (bf16[2,128,1024]{2,1,0:T(8,128)(2,1)}, bf16[2,128,1024]{2,1,0:T(8,128)(2,1)}, u32[]{:S(2)}, u32[]{:S(2)}) collective-permute-start(bf16[2,128,1024]{2,1,0:T(8,128)(2,1)} %get-tuple-element.29), channel_id=1, source_target_pairs={{0,1},{1,2},{4,5},{5,6},{8,9},{9,10},{12,13},{13,14},{16,17},{17,1... | collective-permute-start | bytes 1572872 | tf_op jit(solution)/shard_map/ppermute | solution.py:368
  176.8 14.7 %collective-permute-start.26 = (bf16[2,128,1024]{2,1,0:T(8,128)(2,1)}, bf16[2,128,1024]{2,1,0:T(8,128)(2,1)}, u32[]{:S(2)}, u32[]{:S(2)}) collective-permute-start(bf16[2,128,1024]{2,1,0:T(8,128)(2,1)} %get-tuple-element.30), channel_id=1, source_target_pairs={{3,2},{2,1},{7,6},{6,5},{11,10},{10,9},{15,14},{14,13},{19,18},{18... | collective-permute-start | bytes 1572872 | tf_op jit(solution)/shard_map/ppermute | solution.py:369
  183.1 41.9 %collective-permute-start.33 = (bf16[2,128,1024]{2,1,0:T(8,128)(2,1)}, bf16[2,128,1024]{2,1,0:T(8,128)(2,1)}, u32[]{:S(2)}, u32[]{:S(2)}) collective-permute-start(bf16[2,128,1024]{2,1,0:T(8,128)(2,1)} %get-tuple-element.34), channel_id=1, source_target_pairs={{3,2},{2,1},{1,0},{7,6},{6,5},{5,4},{11,10},{10,9},{9,8},{15,14},{... | collective-permute-start | bytes 1572872 | tf_op jit(solution)/shard_map/ppermute | solution.py:369
  184.5 40.5 %collective-permute-start.30 = (bf16[2,128,1024]{2,1,0:T(8,128)(2,1)}, bf16[2,128,1024]{2,1,0:T(8,128)(2,1)}, u32[]{:S(2)}, u32[]{:S(2)}) collective-permute-start(bf16[2,128,1024]{2,1,0:T(8,128)(2,1)} %get-tuple-element.33), channel_id=1, source_target_pairs={{0,1},{1,2},{2,3},{4,5},{5,6},{6,7},{8,9},{9,10},{10,11},{12,13},{... | collective-permute-start | bytes 1572872 | tf_op jit(solution)/shard_map/ppermute | solution.py:368
  194.1 32.6 %collective-permute-start.27 = (bf16[2,128,1024]{2,1,0:T(8,128)(2,1)}, bf16[2,128,1024]{2,1,0:T(8,128)(2,1)}, u32[]{:S(2)}, u32[]{:S(2)}) collective-permute-start(bf16[2,128,1024]{2,1,0:T(8,128)(2,1)} %get-tuple-element.28), channel_id=1, source_target_pairs={{3,2},{2,1},{1,0},{7,6},{6,5},{5,4},{11,10},{10,9},{9,8},{15,14},{... | collective-permute-start | bytes 1572872 | tf_op jit(solution)/shard_map/ppermute | solution.py:369
  195.3 31.4 %collective-permute-start.24 = (bf16[2,128,1024]{2,1,0:T(8,128)(2,1)}, bf16[2,128,1024]{2,1,0:T(8,128)(2,1)}, u32[]{:S(2)}, u32[]{:S(2)}) collective-permute-start(bf16[2,128,1024]{2,1,0:T(8,128)(2,1)} %get-tuple-element.27), channel_id=1, source_target_pairs={{0,1},{1,2},{2,3},{4,5},{5,6},{6,7},{8,9},{9,10},{10,11},{12,13},{... | collective-permute-start | bytes 1572872 | tf_op jit(solution)/shard_map/ppermute | solution.py:368
  207.3 3.6 %collective-permute-start.18 = (f32[1,1]{1,0:T(1,128)}, f32[1,1]{1,0:T(1,128)}, u32[]{:S(2)}, u32[]{:S(2)}) collective-permute-start(f32[1,1]{1,0:T(1,128)} %add.211), channel_id=1, source_target_pairs={{0,8},{4,12},{8,0},{12,4},{16,24},{20,28},{24,16},{28,20},{1,9},{5... | collective-permute-start | bytes 20 | tf_op jit(solution)/shard_map/ppermute | solution.py:230
  219.9 4.5 %collective-permute-start.21 = (f32[1,1]{1,0:T(1,128)}, f32[1,1]{1,0:T(1,128)}, u32[]{:S(2)}, u32[]{:S(2)}) collective-permute-start(f32[1,1]{1,0:T(1,128)} %add.214), channel_id=1, source_target_pairs={{0,2},{1,3},{2,0},{3,1},{4,6},{5,7},{6,4},{7,5},{8,10},{9,11},{10,... | collective-permute-start | bytes 20 | tf_op jit(solution)/shard_map/ppermute | solution.py:230
  (9 other events, 111.6 us)

commit v2 on v1

v2 whole, which is shorter than its diff:
```python
import functools
import math

import jax
import jax.numpy as jnp
from jax import lax
from jax.experimental import pallas as pl
from jax.experimental.pallas import tpu as pltpu
from jax.sharding import PartitionSpec as P

CAP = 2
NEG_FILL = -1e30
LOG2E = math.log2(math.e)
LN2 = math.log(2.0)
ANY = pl.BlockSpec(memory_space=pl.ANY)
SMEM = pl.BlockSpec(memory_space=pltpu.SMEM)
VMEM = pl.BlockSpec(memory_space=pltpu.VMEM)
EXTRA = 16
GROUPED = 3
VMEM_LIMIT = 56 * 1024 * 1024


def slot_tables(neg_lists, groups, per_group, slot_depth):
    block_count = neg_lists.shape[0]
    block_ids = jnp.arange(block_count, dtype=jnp.int32)
    named = jnp.any(neg_lists[:, :, None] == block_ids[None, None, :], axis=1)
    present = jnp.any(named.reshape(groups, per_group, block_count), axis=1)
    present = present.reshape(groups, groups, per_group).astype(jnp.int32)
    slot_ranks = jnp.cumsum(present, axis=2) - 1
    slot_ids = jnp.arange(slot_depth, dtype=jnp.int32)
    hits = (present[..., None] == 1) & (slot_ranks[..., None] == slot_ids[None, None, None, :])
    local_ids = jnp.arange(per_group, dtype=jnp.int32)
    slot_block = jnp.sum(jnp.where(hits, local_ids[None, None, :, None], 0), axis=2)
    slot_live = jnp.any(hits, axis=2)
    return (slot_ranks, slot_block, slot_live)


def join_log2(a, b):
    return jnp.maximum(a, b) + jnp.log2(1.0 + jnp.exp2(-jnp.abs(a - b)))


def row_tile(rows):
    return math.gcd(rows, 256)


def dot_t(a, b):
    return lax.dot_general(a, b, (((1,), (1,)), ((), ())), preferred_element_type=jnp.float32)


def dot_n(a, b):
    return lax.dot_general(a, b, (((0,), (0,)), ((), ())), preferred_element_type=jnp.float32)


def cand_copy(own_p, far_p, slot_ref, picks, block, k, dst, sem):
    rows = own_p.shape[1]
    src = own_p.at[block] if k == 0 else far_p.at[slot_ref[block * picks + k - 1]]
    return pltpu.make_async_copy(src, dst.at[pl.ds(k * rows, rows)], sem)


def query_copies(block, chunk, pos, own_q, from_left, from_right, dst, sems, arrive):
    first, inner = chunk[0], len(from_left) + 1
    rows = own_q.shape[1]

    def piece(src, at, k):
        return pltpu.make_async_copy(src, dst.at[pl.ds(pl.multiple_of(at * rows, rows), rows)], sems.at[k])

    if arrive:
        for k in range(inner):
            piece(own_q.at[block], k, k).wait()
        return
    piece(own_q.at[block], pos, 0).start()
    for k in range(1, inner):
        @pl.when(pos >= k)
        def _():
            piece(from_left[k - 1].at[block - first], pos - k, k).start()

        @pl.when(pos < k)
        def _():
            piece(from_right[inner - k - 1].at[block - first], pos - k + inner, k).start()


def forward_kernel(chunk, inner, picks, scale, *refs):
    pos_ref, slot_ref, id_ref, own_q = refs[:4]
    from_left = refs[4:3 + inner]
    from_right = refs[3 + inner:2 + 2 * inner]
    own_p, far_p, col_in, row_out, col_out, l_out, cands, whole_q, l_buf, sems, q_sems, l_sems = refs[2 + 2 * inner:]
    rows = own_q.shape[1]
    full = rows * inner
    tile = row_tile(full)
    pos = pos_ref[0]
    first, count = chunk

    def cand_copies(b):
        return [
            cand_copy(own_p, far_p, slot_ref, picks, first + b, k, cands.at[b % 2], sems.at[b % 2, k])
            for k in range(picks + 1)
        ]

    def queries(b, arrive):
        query_copies(first + b, chunk, pos, own_q, from_left, from_right, whole_q.at[b % 2], q_sems.at[b % 2], arrive)

    def start(b):
        queries(b, False)
        for copy in cand_copies(b):
            copy.start()

    def keep(b, t):
        part = pl.ds(t * tile, tile)
        return pltpu.make_async_copy(l_buf.at[b, part], l_out.at[b, part], l_sems.at[b, t])

    start(0)
    col_out[...] = col_in[...]
    for b in range(count):
        buf = b % 2
        if b + 1 < count:
            start(b + 1)
        queries(b, True)
        for copy in cand_copies(b):
            copy.wait()
        block_col = None
        for t in range(full // tile):
            logits = dot_t(whole_q[buf, t * tile:(t + 1) * tile, :], cands[buf]) * scale
            l_buf[b, t * tile:(t + 1) * tile] = logits
            keep(b, t).start()
            peak = jnp.max(logits, axis=1, keepdims=True)
            mass = jnp.sum(jnp.exp2(logits - peak), axis=1, keepdims=True)
            row_lse = jnp.broadcast_to(peak + jnp.log2(mass), (tile, 128))
            row_out[b:b + 1, t * tile:(t + 1) * tile] = row_lse.T[0:1, :]
            col_peak = jnp.max(logits, axis=0, keepdims=True)
            col_mass = jnp.sum(jnp.exp2(logits - col_peak), axis=0, keepdims=True)
            col_lse = col_peak + jnp.log2(col_mass)
            block_col = col_lse if block_col is None else join_log2(block_col, col_lse)
        for k in range(picks + 1):
            row = pl.ds(id_ref[(first + b) * (picks + 1) + k], 1)
            col_out[row, :] = join_log2(col_out[row, :], block_col[:, k * rows:(k + 1) * rows])
    for b in range(count):
        for t in range(full // tile):
            keep(b, t).wait()


def scatter_plan(inner):
    if inner == 4:
        return [
            (((0, 1), (3, 2)), {0: 2, 3: 1}, None, False, ()),
            (((2, 0), (1, 3)), {2: 0, 1: 3}, None, True, ()),
            (((2, 1), (1, 2)), {2: 1, 1: 2}, 0, True, ()),
            (((3, 0), (0, 3)), {3: 0, 0: 3}, None, True, (0, 1)),
            (((1, 0), (2, 3)), {1: 0, 2: 3}, None, True, (0, 1)),
            (((0, 1), (3, 2)), {0: 1, 3: 2}, None, True, (0, 1)),
        ]
    plan, place = [], {}
    for m in range(inner - 1):
        for t in range(inner - 1 - m):
            place[(t, m)] = len(plan)
            pairs = ((t, t + 1), (inner - 1 - t, inner - 2 - t))
            sends = {t: inner - 1 - m, inner - 1 - t: m}
            plan.append((pairs, sends, place.get((t - 1, m)), m == inner - 2 - t, ()))
    return plan


def slice_for(pos, sends):
    at = 0
    for device, target in sends.items():
        at = jnp.where(pos == device, target, at)
    return at


def in_pieces(value, width, lane):
    high = value.astype(jnp.bfloat16).astype(jnp.float32)
    mid = (value - high).astype(jnp.bfloat16).astype(jnp.float32)
    low = value - high - mid
    at = lax.broadcasted_iota(jnp.int32, (EXTRA, width), 1) - lane
    pieces = jnp.where(at == 0, high, jnp.where(at == 1, mid, jnp.where(at == 2, low, 0.0)))
    return pieces.astype(jnp.bfloat16)


def query_kernel(plan, chunks, blocks, inner, picks, *refs):
    pos_ref, slot_ref, id_ref, own_p, far_p, row_lse, col_lse = refs[:7]
    l_refs = refs[7:7 + len(chunks)]
    refs = refs[7 + len(chunks):]
    outs = refs[:len(plan) + 1]
    w_out, cands, l_buf, w_buf, dq_buf, piece_buf, sems, l_sems, dq_sems, w_sems = refs[len(plan) + 1:]
    per_group, rows, width = own_p.shape
    full = rows * inner
    tile = row_tile(full)
    pos = pos_ref[0]
    home = {at + n: (c, n) for c, (at, size) in enumerate(chunks) for n in range(size)}

    def incoming(b):
        c, n = home[b]
        return [pltpu.make_async_copy(l_refs[c].at[n], l_buf.at[b % 2], l_sems.at[b % 2])] + [
            cand_copy(own_p, far_p, slot_ref, picks, b, k, cands.at[b % 2], sems.at[b % 2, k])
            for k in range(picks + 1)
        ]

    def w_copy(b, t):
        part = pl.ds(t * tile, tile)
        return pltpu.make_async_copy(w_buf.at[b, part], w_out.at[b, part], w_sems.at[b, t])

    def outgoing(b, act):
        for n, out in enumerate(outs):
            sends = plan[n][1] if n < len(plan) else {d: d for d in range(inner)}

            @pl.when(functools.reduce(jnp.logical_or, [pos == d for d in sends]))
            def _():
                if b < per_group:
                    at = pl.multiple_of(slice_for(pos, sends) * rows, rows)
                    src, dst = dq_buf.at[b, pl.ds(at, rows)], out.at[pl.ds(b * rows, rows)]
                else:
                    src, dst = piece_buf, out.at[pl.ds(per_group * rows, EXTRA)]
                copy = pltpu.make_async_copy(src, dst, dq_sems.at[b, n])
                copy.wait() if act == "wait" else copy.start()

    for copy in incoming(0):
        copy.start()
    loss_cols = jnp.sum(col_lse[0:blocks, :]) * LN2 - 2.0 * jnp.sum(col_lse[blocks:blocks + 1, 0:1])
    piece_buf[...] = in_pieces(loss_cols, width, 3 * pos)
    outgoing(per_group, "start")
    for b in range(per_group):
        buf = b % 2
        if b + 1 < per_group:
            for copy in incoming(b + 1):
                copy.start()
        col = jnp.concatenate(
            [col_lse[pl.ds(id_ref[b * (picks + 1) + k], 1), :] for k in range(picks + 1)], axis=1
        ) + 1.0
        row = jnp.broadcast_to(row_lse[b:b + 1, :] + 1.0, (128, full)).T
        for copy in incoming(b):
            copy.wait()
        for t in range(full // tile):
            part = slice(t * tile, (t + 1) * tile)
            logits = l_buf[buf, part, :]
            probs = jnp.exp2(logits - row[part, 0:1]) + jnp.exp2(logits - col)
            r_id = lax.broadcasted_iota(jnp.int32, (tile, rows), 0) + t * tile - pos * rows
            c_id = lax.broadcasted_iota(jnp.int32, (tile, rows), 1)
            target = jnp.where(r_id == c_id, 1.0, 0.0)
            w_buf[b, part, 0:rows] = (probs[:, 0:rows] - target).astype(jnp.bfloat16)
            w_buf[b, part, rows:] = probs[:, rows:].astype(jnp.bfloat16)
            w_copy(b, t).start()
            grad = jnp.dot(w_buf[b, part, :], cands[buf], preferred_element_type=jnp.float32)
            dq_buf[b, part] = grad.astype(jnp.bfloat16)
        outgoing(b, "start")
    for b in range(per_group + 1):
        outgoing(b, "wait")
    for b in range(per_group):
        for t in range(full // tile):
            w_copy(b, t).wait()


def passage_kernel(chunks, inner, picks, *refs):
    pos_ref, slot_ref, own_q = refs[:3]
    place = 3
    rings = []
    for _ in chunks:
        rings.append((refs[place:place + inner - 1], refs[place + inner - 1:place + 2 * inner - 2]))
        place += 2 * inner - 2
    w_in, row_lse, own_out, far_out, whole_q, w_buf, own_acc, far_acc, far_buf, q_sems, w_sems, far_sems = refs[place:]
    per_group, rows, width = own_q.shape
    groups, packed = far_buf.shape[:2]
    depth = packed // rows
    pos = pos_ref[0]
    home = {at + n: c for c, (at, size) in enumerate(chunks) for n in range(size)}

    def queries(b, arrive):
        c = home[b]
        query_copies(b, chunks[c], pos, own_q, *rings[c], whole_q.at[b % 2], q_sems.at[b % 2], arrive)

    def w_copy(b):
        return pltpu.make_async_copy(w_in.at[b], w_buf.at[b % 2], w_sems.at[b % 2])

    def own_copy(b):
        return pltpu.make_async_copy(own_acc.at[b], own_out.at[b], far_sems.at[groups + b])

    queries(0, False)
    w_copy(0).start()
    far_acc[...] = jnp.zeros_like(far_acc)
    for b in range(per_group):
        buf = b % 2
        if b + 1 < per_group:
            queries(b + 1, False)
            w_copy(b + 1).start()
        queries(b, True)
        w_copy(b).wait()
        step = math.gcd(picks + 1, GROUPED)
        for k in range(0, picks + 1, step):
            parts = dot_n(w_buf[buf, :, k * rows:(k + step) * rows], whole_q[buf])
            for j in range(step):
                part = parts[j * rows:(j + 1) * rows]
                if k + j == 0:
                    own_acc[b] = part
                    own_copy(b).start()
                else:
                    slot = slot_ref[b * picks + k + j - 1]
                    far_acc[slot] = far_acc[slot] + part
    row_pieces = in_pieces(jnp.sum(row_lse[0:per_group, :]) * LN2, width, 0)
    for g in range(groups):
        for c in range(depth):
            far_buf[g, c * rows:(c + 1) * rows] = far_acc[g * depth + c].astype(jnp.bfloat16)
        far_buf[g, depth * rows:] = row_pieces
        pltpu.make_async_copy(far_buf.at[g], far_out.at[g], far_sems.at[g]).start()
    for g in range(groups):
        pltpu.make_async_copy(far_buf.at[g], far_out.at[g], far_sems.at[g]).wait()
    for b in range(per_group):
        own_copy(b).wait()


def finish_kernel(depth, dest_ref, own_ref, far_ref, out_ref, loss_ref, acc, got, sems):
    groups = far_ref.shape[0]
    per_group, rows, _ = out_ref.shape

    def copy(g):
        return pltpu.make_async_copy(far_ref.at[g], got.at[g], sems.at[g])

    own = pltpu.make_async_copy(own_ref, acc.at[pl.ds(0, per_group)], sems.at[groups])
    own.start()
    for g in range(groups):
        copy(g).start()
    own.wait()
    pieces = None
    for g in range(groups):
        copy(g).wait()
        for c in range(depth):
            dest = dest_ref[g * depth + c]
            acc[dest] = acc[dest] + got[g, c * rows:(c + 1) * rows].astype(jnp.float32)
        row = got[g, depth * rows:, 0:128].astype(jnp.float32)
        pieces = row if pieces is None else pieces + row
    loss_ref[...] = jnp.sum(pieces[0:8], axis=1, keepdims=True) + jnp.zeros((8, 128), jnp.float32)
    out_ref[...] = acc[0:per_group].astype(jnp.bfloat16)


def after(value, *events):
    return lax.optimization_barrier((value, *events))[0]


def doublings(size):
    return [1 << n for n in range(size.bit_length() - 1)]


def butterfly(value, axis, size, join):
    for step in doublings(size):
        other = lax.ppermute(value, axis, [(i, i ^ step) for i in range(size)])
        value = join(value, other)
    return value


def body(queries, passages, neg_lists):
    per_group, rows, width = queries.shape
    picks = neg_lists.shape[1]
    blocks = neg_lists.shape[0]
    groups = lax.axis_size("dp")
    inner = lax.axis_size("inner")
    full = rows * inner
    cand_rows = (picks + 1) * rows
    slot_count = groups * CAP
    scale = 1.0 / math.sqrt(width)
    my_group = lax.axis_index("dp")
    pos = lax.axis_index("inner")
    f32, bf16 = jnp.float32, jnp.bfloat16
    params = pltpu.CompilerParams(vmem_limit_bytes=VMEM_LIMIT)
    block_flops = 2 * full * cand_rows * width
    block_bytes = 2 * (full + cand_rows) * width

    def cost(blocks, products):
        return pl.CostEstimate(
            flops=blocks * products * block_flops, bytes_accessed=blocks * products * block_bytes, transcendentals=0
        )

    half = per_group // 2
    chunks = [(0, half), (half, per_group - half)]
    lefts = [[] for _ in chunks]
    rights = [[] for _ in chunks]
    moving = [[queries[at:at + size]] * 2 for at, size in chunks]
    for s in range(1, inner):
        for c in range(len(chunks)):
            moving[c] = [
                lax.ppermute(moving[c][0], "inner", [(i, i + 1) for i in range(s - 1, inner - 1)]),
                lax.ppermute(moving[c][1], "inner", [(i, i - 1) for i in range(inner - s, 0, -1)]),
            ]
            lefts[c].append(moving[c][0])
            rights[c].append(moving[c][1])

    slot_ranks, slot_block, slot_live = slot_tables(neg_lists, groups, per_group, CAP)
    listed = lax.dynamic_slice_in_dim(neg_lists, my_group * per_group, per_group, 0)
    my_ranks = lax.dynamic_index_in_dim(slot_ranks, my_group, 0, keepdims=False)
    slot_of = (listed // per_group) * CAP + my_ranks[listed // per_group, listed % per_group]
    slot_flat = slot_of.reshape(-1)
    own_ids = my_group * per_group + jnp.arange(per_group, dtype=jnp.int32)
    id_flat = jnp.concatenate([own_ids[:, None], listed], axis=1).reshape(-1)
    pos_arr = pos.reshape(1)
    sends_for = lax.dynamic_index_in_dim(slot_block, my_group, 1, keepdims=False)
    live_for = lax.dynamic_index_in_dim(slot_live, my_group, 1, keepdims=False)
    outgoing = passages[sends_for]
    arrived = lax.all_to_all(outgoing, "dp", split_axis=0, concat_axis=0, tiled=True)
    arrived = arrived.reshape(slot_count, rows, width)

    fetch_scratch = [
        pltpu.VMEM((2, cand_rows, width), bf16),
        pltpu.VMEM((2, full, width), bf16),
    ]
    fetch_sems = [pltpu.SemaphoreType.DMA((2, picks + 1)), pltpu.SemaphoreType.DMA((2, inner))]
    own_sum = jnp.sum(queries.astype(f32) * passages.astype(f32)) * scale
    col = jnp.concatenate([jnp.full((blocks, rows), NEG_FILL, f32), jnp.broadcast_to(own_sum, (8, rows))])
    row_parts, logits = [], []
    tiles = full // row_tile(full)
    for c, chunk in enumerate(chunks):
        row_part, col, logit = pl.pallas_call(
            functools.partial(forward_kernel, chunk, inner, picks, scale * LOG2E),
            out_shape=(
                jax.ShapeDtypeStruct((chunk[1], full), f32),
                jax.ShapeDtypeStruct(col.shape, f32),
                jax.ShapeDtypeStruct((chunk[1], full, cand_rows), f32),
            ),
            in_specs=[SMEM] * 3 + [ANY] * (2 * inner + 1) + [VMEM],
            out_specs=(VMEM, VMEM, ANY),
            scratch_shapes=fetch_scratch + [pltpu.VMEM((chunk[1], full, cand_rows), f32)] + fetch_sems + [
                pltpu.SemaphoreType.DMA((chunk[1], tiles))
            ],
            compiler_params=params,
            cost_estimate=cost(chunk[1], 1),
            name=f"forward_{c}",
        )(pos_arr, slot_flat, id_flat, queries, *lefts[c], *rights[c], passages, arrived, col)
        row_parts.append(row_part)
        logits.append(logit)
    row = jnp.concatenate(row_parts, axis=0)
    is_lse = jnp.arange(blocks + 8)[:, None] < blocks
    col_lse = butterfly(col, "dp", groups, lambda a, b: jnp.where(is_lse, join_log2(a, b), a + b))
    row_lse = butterfly(row, "inner", inner, join_log2)

    packed = CAP * rows + EXTRA
    flat = per_group * rows + EXTRA
    plan = scatter_plan(inner)
    *parts, weights = pl.pallas_call(
        functools.partial(query_kernel, plan, chunks, blocks, inner, picks),
        out_shape=(jax.ShapeDtypeStruct((flat, width), bf16),) * (len(plan) + 1)
        + (jax.ShapeDtypeStruct((per_group, full, cand_rows), bf16),),
        in_specs=[SMEM] * 3 + [ANY] * 2 + [VMEM] * 2 + [ANY] * len(chunks),
        out_specs=(ANY,) * (len(plan) + 2),
        scratch_shapes=[
            pltpu.VMEM((2, cand_rows, width), bf16),
            pltpu.VMEM((2, full, cand_rows), f32),
            pltpu.VMEM((per_group, full, cand_rows), bf16),
            pltpu.VMEM((per_group, full, width), bf16),
            pltpu.VMEM((EXTRA, width), bf16),
            pltpu.SemaphoreType.DMA((2, picks + 1)),
            pltpu.SemaphoreType.DMA((2,)),
            pltpu.SemaphoreType.DMA((per_group + 1, len(plan) + 1)),
            pltpu.SemaphoreType.DMA((per_group, tiles)),
        ],
        compiler_params=params,
        cost_estimate=cost(per_group, 1),
        name="query",
    )(pos_arr, slot_flat, id_flat, passages, arrived, row_lse, col_lse, *logits)

    rings = []
    for c in range(len(chunks)):
        rings += [*lefts[c], *rights[c]]
    own_grad, far_grad = pl.pallas_call(
        functools.partial(passage_kernel, chunks, inner, picks),
        out_shape=(
            jax.ShapeDtypeStruct((per_group, rows, width), f32),
            jax.ShapeDtypeStruct((groups, packed, width), bf16),
        ),
        in_specs=[SMEM] * 2 + [ANY] * (2 + len(rings)) + [VMEM],
        out_specs=(ANY, ANY),
        scratch_shapes=[
            pltpu.VMEM((2, full, width), bf16),
            pltpu.VMEM((2, full, cand_rows), bf16),
            pltpu.VMEM((per_group, rows, width), f32),
            pltpu.VMEM((slot_count, rows, width), f32),
            pltpu.VMEM((groups, packed, width), bf16),
            pltpu.SemaphoreType.DMA((2, inner)),
            pltpu.SemaphoreType.DMA((2,)),
            pltpu.SemaphoreType.DMA((groups + per_group,)),
        ],
        compiler_params=params,
        cost_estimate=cost(per_group, 1),
        name="passage",
    )(pos_arr, slot_flat, queries, *rings, weights, row_lse)

    sums = []
    query_sum = parts[-1].astype(f32)
    for n, (pairs, sends, adds, final, gates) in enumerate(plan):
        out = parts[n]
        if adds is not None:
            out = (out.astype(f32) + sums[adds]).astype(bf16)
        if gates:
            out = after(out, *[sums[g] for g in gates])
        sums.append(lax.ppermute(out, "inner", pairs))
        if final:
            query_sum = query_sum + sums[-1]
    loss_cols = jnp.sum(query_sum[per_group * rows, :3 * inner])
    query_grad = query_sum[:per_group * rows].astype(bf16).reshape(per_group, rows, width)

    far_grad = after(far_grad, *sums[:2])
    returned = lax.all_to_all(far_grad, "dp", split_axis=0, concat_axis=0, tiled=True)
    dest = jnp.where(live_for, sends_for, per_group).reshape(-1)
    passage_grad, total = pl.pallas_call(
        functools.partial(finish_kernel, CAP),
        out_shape=(
            jax.ShapeDtypeStruct((per_group, rows, width), bf16),
            jax.ShapeDtypeStruct((8, 128), f32),
        ),
        in_specs=[SMEM, ANY, ANY],
        out_specs=(VMEM, VMEM),
        scratch_shapes=[
            pltpu.VMEM((per_group + 1, rows, width), f32),
            pltpu.VMEM((groups, packed, width), bf16),
            pltpu.SemaphoreType.DMA((groups + 1,)),
        ],
        compiler_params=params,
        name="finish",
    )(dest, own_grad, returned)
    mean_loss = (total[0, 0] + loss_cols) / (2.0 * groups * per_group * full)
    return (mean_loss, query_grad, passage_grad)


def solution(mesh):
    in_specs = (P("dp", "inner", None), P("dp", "inner", None), P())
    out_specs = (P(), P("dp", "inner", None), P("dp", "inner", None))
    return jax.shard_map(body, mesh=mesh, in_specs=in_specs, out_specs=out_specs, check_vma=False)
```

time: 236 us -> 230 us (0.975)
  waiting for transfers between devices: 61.9 us -> 92.6 us
  starting transfers between devices: 89.7 us -> 59.8 us
  other arithmetic: 17.2 us -> 12 us
  between operations: 6.62 us -> 4.01 us
    ppermute x24 -> x18, waiting for transfers between devices: 54.7 us -> 89.8 us  [the longest x6 54.7 us: body(): sums.append(lax.ppermute(out, 'inner', pairs))]
    ppermute x24 -> x18, starting transfers between devices: 61.9 us -> 41.2 us  [the longest x6 17.3 us: body(): sums.append(lax.ppermute(out, 'inner', pairs))]
    convert_element_type x6 -> x1, other arithmetic: 14.4 us -> 2.72 us  [body(): out = (out.astype(f32) + sums[adds]).astype(bf16)]
    ppermute x10 -> x5, starting transfers between devices: 17.9 us -> 8.58 us  [butterfly(): other = lax.ppermute(value, axis, [(i, i ^ step) for i in range(size)])]
    ppermute x10 -> x5, waiting for transfers between devices: 7.13 us -> 2.81 us  [butterfly(): other = lax.ppermute(value, axis, [(i, i ^ step) for i in range(size)])]
    squeeze x2 -> x0, local copies, waits for them, and re-layouts: 3.44 us -> none  [part_of(): lax.dynamic_index_in_dim(parts, target, 1, keepdims=False).astype(f32)]
    add x0 -> x1, other arithmetic: none -> 3.31 us  [body(): query_sum = query_sum + sums[-1]]
    slice x1 -> x3, local copies, waits for them, and re-layouts: 0.07 us -> 3.22 us  [the longest x1 1.19 us: body(): mean_loss = (total[0, 0] + loss_cols) / (2.0 * groups * per_group * full)]
  transfers between devices with their start and end apart: 36 -> 25, of which waited for: 22 -> 14; matrix products, arithmetic and copies ran while one was open for 9% -> 7% of each run, Pallas kernels for 3% -> 9%
where the time goes in v2:
time: 230 us; the launch traced here: 229 us
  waiting for transfers between devices  92.6 us (40%)
  starting transfers between devices  59.8 us (26%)
  Pallas kernels  48.4 us (21%)
  local copies, waits for them, and re-layouts  12.2 us (5%)
  other arithmetic  12 us (5%)
  between operations  4.01 us (2%)
    ppermute x6, waiting for transfers between devices, body(): sums.append(lax.ppermute(out, 'inner', pairs))  54.7 us
    ppermute x6, waiting for transfers between devices, body(): lax.ppermute(moving[c][1], 'inner', [(i, i - 1) for i in range(inner - s,...  34.9 us
    pallas_call x2, Pallas kernels, body(): pl.pallas_call(functools.partial(forward_kernel, chunk, inner, picks, sca...  17.5 us
    ppermute x6, starting transfers between devices, body(): sums.append(lax.ppermute(out, 'inner', pairs))  17.3 us
    ppermute x6, starting transfers between devices, body(): lax.ppermute(moving[c][0], 'inner', [(i, i + 1) for i in range(s - 1, inn...  16.2 us
    pallas_call x1, Pallas kernels, body(): pl.pallas_call(functools.partial(query_kernel, plan, chunks, blocks, inne...  15.1 us
    pallas_call x1, Pallas kernels, body(): pl.pallas_call(functools.partial(passage_kernel, chunks, inner, picks), o...  11 us
    ppermute x5, starting transfers between devices, butterfly(): other = lax.ppermute(value, axis, [(i, i ^ step) for i in range(size)])  8.58 us
  transfers between devices with their start and end apart: 25, of which 14 were waited for; matrix products, arithmetic and copies ran while one was open for 7% of the time, Pallas kernels for 9%

profile of v2, /device:TPU:0, one launch (start us, length us, event | category | flops | bytes accessed | tf_op | source)
XLA Modules:
  0.0 229.0 jit_solution(3720472450130038871)
XLA Ops:
  2.3 4.0 %gather_fusion.1 = bf16[16,128,1024]{2,1,0:T(8,128)(2,1)} fusion(bf16[4,128,1024]{2,1,0:T(8,128)(2,1)} %refs_3_.5, s32[1024]{0:T(1024)S(1)} %pad_clamp_fusion), kind=kCustom, calls=%fused_computation.1 | custom fusion | bytes 8388672 | tf_op jit(solution)/shard_map/gather | solution.py:392
  6.3 5.3 %all-to-all-start = ((bf16[8,2,128,1024]{3,2,1,0:T(8,128)(2,1)}), bf16[8,2,128,1024]{3,2,1,0:T(8,128)(2,1)}, u32[]{:S(2)}, u32[]{:S(2)}) async-start(bf16[8,2,128,1024]{3,2,1,0:T(8,128)(2,1)} %bitcast.15), calls=%async_computation | async-start | bytes 8388608 | tf_op jit(solution)/shard_map/all_to_all | solution.py:393
  13.8 5.0 %collective-permute-start = (bf16[2,128,1024]{2,1,0:T(8,128)(2,1)S(1)}, bf16[2,128,1024]{2,1,0:T(8,128)(2,1)S(1)}, u32[]{:S(2)}, u32[]{:S(2)}) collective-permute-start(bf16[2,128,1024]{2,1,0:T(8,128)(2,1)S(1)} %get-tuple-element.50), channel_id=1, source_target_pairs={{0,1},{1,2},{2,3},{4,5},{5,6},{6,7},{8,9},{9,10},{10,11},{12,13},{... | collective-permute-start | bytes 1572872 | tf_op jit(solution)/shard_map/ppermute | solution.py:376
  20.1 5.4 %collective-permute-start.6 = (bf16[2,128,1024]{2,1,0:T(8,128)(2,1)}, bf16[2,128,1024]{2,1,0:T(8,128)(2,1)}, u32[]{:S(2)}, u32[]{:S(2)}) collective-permute-start(bf16[2,128,1024]{2,1,0:T(8,128)(2,1)} %get-tuple-element.49), channel_id=1, source_target_pairs={{0,1},{1,2},{2,3},{4,5},{5,6},{6,7},{8,9},{9,10},{10,11},{12,13},{... | collective-permute-start | bytes 1572872 | tf_op jit(solution)/shard_map/ppermute | solution.py:376
  25.5 4.1 %collective-permute-done.3.refs_7_.refs_6_ = bf16[2,128,1024]{2,1,0:T(8,128)(2,1)S(1)} collective-permute-done((bf16[2,128,1024]{2,1,0:T(8,128)(2,1)S(1)}, bf16[2,128,1024]{2,1,0:T(8,128)(2,1)S(1)}, u32[]{:S(2)}, u32[]{:S(2)}) %collective-permute-start.3) | collective-permute-done | bytes 524320 | tf_op jit(solution)/shard_map/ppermute | solution.py:377
  31.1 1.5 collective-permute-start.1
  32.6 8.4 %collective-permute-done.9.refs_7_.refs_12_ = bf16[2,128,1024]{2,1,0:T(8,128)(2,1)} collective-permute-done((bf16[2,128,1024]{2,1,0:T(8,128)(2,1)}, bf16[2,128,1024]{2,1,0:T(8,128)(2,1)}, u32[]{:S(2)}, u32[]{:S(2)}) %collective-permute-start.9) | collective-permute-done | bytes 524320 | tf_op jit(solution)/shard_map/ppermute | solution.py:377
  42.3 1.4 collective-permute-start.7
  45.5 6.7 %collective-permute-done.4.refs_8_.refs_7_ = bf16[2,128,1024]{2,1,0:T(8,128)(2,1)} collective-permute-done((bf16[2,128,1024]{2,1,0:T(8,128)(2,1)S(1)}, bf16[2,128,1024]{2,1,0:T(8,128)(2,1)}, u32[]{:S(2)}, u32[]{:S(2)}) %collective-permute-start.4) | collective-permute-done | bytes 524320 | tf_op jit(solution)/shard_map/ppermute | solution.py:377
  53.5 1.5 collective-permute-start.2
  55.6 7.8 %collective-permute-done.10.refs_8_.refs_13_ = bf16[2,128,1024]{2,1,0:T(8,128)(2,1)} collective-permute-done((bf16[2,128,1024]{2,1,0:T(8,128)(2,1)}, bf16[2,128,1024]{2,1,0:T(8,128)(2,1)}, u32[]{:S(2)}, u32[]{:S(2)}) %collective-permute-start.10) | collective-permute-done | bytes 524320 | tf_op jit(solution)/shard_map/ppermute | solution.py:377
  64.7 1.5 collective-permute-start.8
  68.1 6.5 %collective-permute-done.5.refs_9_.refs_8_ = bf16[2,128,1024]{2,1,0:T(8,128)(2,1)} collective-permute-done((bf16[2,128,1024]{2,1,0:T(8,128)(2,1)}, bf16[2,128,1024]{2,1,0:T(8,128)(2,1)}, u32[]{:S(2)}, u32[]{:S(2)}) %collective-permute-start.5) | collective-permute-done | bytes 524320 | tf_op jit(solution)/shard_map/ppermute | solution.py:377
  75.4 8.9 %forward_0.1 = (f32[2,512]{1,0:T(2,128)}, f32[40,128]{1,0:T(8,128)}, f32[2,512,1152]{2,1,0:T(8,128)}) custom-call(s32[1]{0:T(128)} %bitcast.2.refs_0_, s32[32]{0:T(128)} %reshape.85.refs_1_, s32[36]{0:T(128)} %reshape.86.refs_2_, bf16[4,128,1024]{2,1,0:T(8,128)(2,1)} %refs_2_.1, bf16[2,128,1024]{2,1,0:T(8,128)(2,1)} %copy-done.6, ...), custom_call_target="tpu_custom_call" | custom-call | flops 2415919104 | bytes 6815744 | tf_op jit(solution)/shard_map/forward_0/pallas_call | solution.py:406
  85.6 8.7 %forward_1.1 = (f32[2,512]{1,0:T(2,128)}, f32[40,128]{1,0:T(8,128)}, f32[2,512,1152]{2,1,0:T(8,128)}) custom-call(s32[1]{0:T(128)} %bitcast.2.refs_0_, s32[32]{0:T(128)} %reshape.85.refs_1_, s32[36]{0:T(128)} %reshape.86.refs_2_, bf16[4,128,1024]{2,1,0:T(8,128)(2,1)} %refs_2_.1, bf16[2,128,1024]{2,1,0:T(8,128)(2,1)} %collective-permute-done.6.refs_4_.refs_9_, ...), custom_call_target="tpu_custom_call" | custom-call | flops 2415919104 | bytes 6815744 | tf_op jit(solution)/shard_map/forward_1/pallas_call | solution.py:406
  96.6 1.7 collective-permute-start.15
  99.4 5.3 %collective-permute-start.13 = (f32[4,512]{1,0:T(4,128)S(1)}, f32[4,512]{1,0:T(4,128)S(1)}, u32[]{:S(2)}, u32[]{:S(2)}) collective-permute-start(f32[4,512]{1,0:T(4,128)S(1)} %multiply_add_fusion.1), channel_id=1, source_target_pairs={{0,2},{1,3},{2,0},{3,1},{4,6},{5,7},{6,4},{7,5},{8,10},{9,11},{10,... | collective-permute-start | bytes 24584 | tf_op jit(solution)/shard_map/ppermute | solution.py:341
  104.8 1.5 collective-permute-start.16
  107.0 1.6 collective-permute-done.16
  109.3 15.1 %query.1 = (bf16[528,1024]{1,0:T(8,128)(2,1)}, bf16[528,1024]{1,0:T(8,128)(2,1)}, bf16[528,1024]{1,0:T(8,128)(2,1)}, bf16[528,1024]{1,0:T(8,128)(2,1)}, bf16[528...) custom-call(s32[1]{0:T(128)} %bitcast.2.refs_0_, ...), custom_call_target="tpu_custom_call" | custom-call | flops 4831838208 | bytes 13631488 | tf_op jit(solution)/shard_map/query/pallas_call | solution.py:432
  124.4 3.1 %collective-permute-start.17 = (bf16[528,1024]{1,0:T(8,128)(2,1)}, bf16[528,1024]{1,0:T(8,128)(2,1)S(1)}, u32[]{:S(2)}, u32[]{:S(2)}) collective-permute-start(bf16[528,1024]{1,0:T(8,128)(2,1)} %get-tuple-element.34), channel_id=1, source_target_pairs={{0,1},{3,2},{4,5},{7,6},{8,9},{11,10},{12,13},{15,14},{16,17},{19,... | collective-permute-start | bytes 3244040 | tf_op jit(solution)/shard_map/ppermute | solution.py:488
  128.8 11.0 %passage.1 = (f32[4,128,1024]{2,1,0:T(8,128)}, bf16[8,272,1024]{2,1,0:T(8,128)(2,1)}) custom-call(s32[1]{0:T(128)} %bitcast.2.refs_0_, s32[32]{0:T(128)} %reshape.85.refs_1_, bf16[4,128,1024]{2,1,0:T(8,128)(2,1)} %refs_2_.1, bf16[2,128,1024]{2,1,0:T(8,128)(2,1)} %copy-done.6, bf16[2,128,1024]{2,1,0:T(8,128)(2,1)} %collective-permute-done.1.refs_5_.refs_4_, ...), custom_call_target="tpu_custom_call" | custom-call | flops 4831838208 | bytes 13631488 | tf_op jit(solution)/shard_map/passage/pallas_call | solution.py:457
  139.7 9.3 %collective-permute-done.17 = bf16[528,1024]{1,0:T(8,128)(2,1)S(1)} collective-permute-done((bf16[528,1024]{1,0:T(8,128)(2,1)}, bf16[528,1024]{1,0:T(8,128)(2,1)S(1)}, u32[]{:S(2)}, u32[]{:S(2)}) %collective-permute-start.17) | collective-permute-done | bytes 1081376 | tf_op jit(solution)/shard_map/ppermute | solution.py:488
  149.0 5.0 %collective-permute-done.18 = bf16[528,1024]{1,0:T(8,128)(2,1)S(1)} collective-permute-done((bf16[528,1024]{1,0:T(8,128)(2,1)}, bf16[528,1024]{1,0:T(8,128)(2,1)S(1)}, u32[]{:S(2)}, u32[]{:S(2)}) %collective-permute-start.18) | collective-permute-done | bytes 1081376 | tf_op jit(solution)/shard_map/ppermute | solution.py:488
  154.0 4.7 %all-to-all-start.1 = ((bf16[8,272,1024]{2,1,0:T(8,128)(2,1)}), bf16[8,272,1024]{2,1,0:T(8,128)(2,1)}, u32[]{:S(2)}, u32[]{:S(2)}) async-start(bf16[8,272,1024]{2,1,0:T(8,128)(2,1)} %get-tuple-element.36), calls=%async_computation.1 | async-start | bytes 8912896 | tf_op jit(solution)/shard_map/all_to_all | solution.py:495
  158.7 2.7 %add_convert_fusion = bf16[528,1024]{1,0:T(8,128)(2,1)} fusion(bf16[528,1024]{1,0:T(8,128)(2,1)} %copy-done.4, bf16[528,1024]{1,0:T(8,128)(2,1)S(1)} %copy-done.3), kind=kLoop, calls=%fused_computation.3 | loop fusion | flops 2162688 | bytes 3244032 | tf_op jit(solution)/shard_map/convert_element_type | solution.py:485
  162.2 4.3 %collective-permute-start.20 = (bf16[528,1024]{1,0:T(8,128)(2,1)}, bf16[528,1024]{1,0:T(8,128)(2,1)}, u32[]{:S(2)}, u32[]{:S(2)}) collective-permute-start(bf16[528,1024]{1,0:T(8,128)(2,1)} %get-tuple-element.41), channel_id=1, source_target_pairs={{3,0},{0,3},{7,4},{4,7},{11,8},{8,11},{15,12},{12,15},{19,16},{16,... | collective-permute-start | bytes 3244040 | tf_op jit(solution)/shard_map/ppermute | solution.py:488
  167.8 6.6 %collective-permute-start.22 = (bf16[528,1024]{1,0:T(8,128)(2,1)}, bf16[528,1024]{1,0:T(8,128)(2,1)}, u32[]{:S(2)}, u32[]{:S(2)}) collective-permute-start(bf16[528,1024]{1,0:T(8,128)(2,1)} %get-tuple-element.45), channel_id=1, source_target_pairs={{0,1},{3,2},{4,5},{7,6},{8,9},{11,10},{12,13},{15,14},{16,17},{19,... | collective-permute-start | bytes 3244040 | tf_op jit(solution)/shard_map/ppermute | solution.py:488
  175.1 17.9 %collective-permute-done.20 = bf16[528,1024]{1,0:T(8,128)(2,1)} collective-permute-done((bf16[528,1024]{1,0:T(8,128)(2,1)}, bf16[528,1024]{1,0:T(8,128)(2,1)}, u32[]{:S(2)}, u32[]{:S(2)}) %collective-permute-start.20) | collective-permute-done | bytes 1081376 | tf_op jit(solution)/shard_map/ppermute | solution.py:488
  193.0 22.6 %collective-permute-done.21 = bf16[528,1024]{1,0:T(8,128)(2,1)} collective-permute-done((bf16[528,1024]{1,0:T(8,128)(2,1)}, bf16[528,1024]{1,0:T(8,128)(2,1)}, u32[]{:S(2)}, u32[]{:S(2)}) %collective-permute-start.21) | collective-permute-done | bytes 1081376 | tf_op jit(solution)/shard_map/ppermute | solution.py:488
  215.6 3.3 %convert_add_fusion = f32[528,1024]{1,0:T(8,128)S(1)} fusion(bf16[528,1024]{1,0:T(8,128)(2,1)} %collective-permute-done.22, bf16[528,1024]{1,0:T(8,128)(2,1)} %collective-permute-done.21, bf16[528,1024]{1,0:T(8,128)(2,1)} %collective-permute-done.20, bf16[528,1024]{1,0:T(8,128)(2,1)S(1)} %collective-permute-done.19, ...), kind=kLoop, calls=%fused_computation.2 | loop fusion | flops 5947392 | bytes 8650752 | tf_op jit(solution)/shard_map/add | solution.py:490
  220.6 4.8 %finish.1 = (bf16[4,128,1024]{2,1,0:T(8,128)(2,1)}, f32[8,128]{1,0:T(8,128)}) custom-call(s32[16]{0:T(128)} %select_n.65.dest_ref, f32[4,128,1024]{2,1,0:T(8,128)} %get-tuple-element.32.own_ref, bf16[8,272,1024]{2,1,0:T(8,128)(2,1)} %all-to-all-done.1.far_ref), custom_call_target="tpu_custom_call" | custom-call | tf_op jit(solution)/shard_map/finish/pallas_call | solution.py:497
  (87 shorter events, 28.0 us)
Async XLA Ops:
  6.3 5.3 %copy-start.1 = (bf16[4,128,1024]{2,1,0:T(8,128)(2,1)S(1)}, bf16[4,128,1024]{2,1,0:T(8,128)(2,1)}, u32[]{:S(2)}) copy-start(bf16[4,128,1024]{2,1,0:T(8,128)(2,1)} %refs_2_.1) | copy-start | bytes 3145732
  6.3 68.4 %all-to-all-start = ((bf16[8,2,128,1024]{3,2,1,0:T(8,128)(2,1)}), bf16[8,2,128,1024]{3,2,1,0:T(8,128)(2,1)}, u32[]{:S(2)}, u32[]{:S(2)}) async-start(bf16[8,2,128,1024]{3,2,1,0:T(8,128)(2,1)} %bitcast.15), calls=%async_computation | async-start | bytes 8388608 | tf_op jit(solution)/shard_map/all_to_all | solution.py:393
  11.6 54.6 %copy-start = (bf16[4,128,1024]{2,1,0:T(8,128)(2,1)S(1)}, bf16[4,128,1024]{2,1,0:T(8,128)(2,1)}, u32[]{:S(2)}) copy-start(bf16[4,128,1024]{2,1,0:T(8,128)(2,1)} %refs_3_.5) | copy-start | bytes 3145732
  12.5 17.1 %collective-permute-start.3 = (bf16[2,128,1024]{2,1,0:T(8,128)(2,1)S(1)}, bf16[2,128,1024]{2,1,0:T(8,128)(2,1)S(1)}, u32[]{:S(2)}, u32[]{:S(2)}) collective-permute-start(bf16[2,128,1024]{2,1,0:T(8,128)(2,1)S(1)} %get-tuple-element.50), channel_id=1, source_target_pairs={{3,2},{2,1},{1,0},{7,6},{6,5},{5,4},{11,10},{10,9},{9,8},{15,14},{... | collective-permute-start | bytes 1572872 | tf_op jit(solution)/shard_map/ppermute | solution.py:377
  13.8 17.2 %collective-permute-start = (bf16[2,128,1024]{2,1,0:T(8,128)(2,1)S(1)}, bf16[2,128,1024]{2,1,0:T(8,128)(2,1)S(1)}, u32[]{:S(2)}, u32[]{:S(2)}) collective-permute-start(bf16[2,128,1024]{2,1,0:T(8,128)(2,1)S(1)} %get-tuple-element.50), channel_id=1, source_target_pairs={{0,1},{1,2},{2,3},{4,5},{5,6},{6,7},{8,9},{9,10},{10,11},{12,13},{... | collective-permute-start | bytes 1572872 | tf_op jit(solution)/shard_map/ppermute | solution.py:376
  18.8 22.1 %collective-permute-start.9 = (bf16[2,128,1024]{2,1,0:T(8,128)(2,1)}, bf16[2,128,1024]{2,1,0:T(8,128)(2,1)}, u32[]{:S(2)}, u32[]{:S(2)}) collective-permute-start(bf16[2,128,1024]{2,1,0:T(8,128)(2,1)} %get-tuple-element.49), channel_id=1, source_target_pairs={{3,2},{2,1},{1,0},{7,6},{6,5},{5,4},{11,10},{10,9},{9,8},{15,14},{... | collective-permute-start | bytes 1572872 | tf_op jit(solution)/shard_map/ppermute | solution.py:377
  20.1 22.1 %collective-permute-start.6 = (bf16[2,128,1024]{2,1,0:T(8,128)(2,1)}, bf16[2,128,1024]{2,1,0:T(8,128)(2,1)}, u32[]{:S(2)}, u32[]{:S(2)}) collective-permute-start(bf16[2,128,1024]{2,1,0:T(8,128)(2,1)} %get-tuple-element.49), channel_id=1, source_target_pairs={{0,1},{1,2},{2,3},{4,5},{5,6},{6,7},{8,9},{9,10},{10,11},{12,13},{... | collective-permute-start | bytes 1572872 | tf_op jit(solution)/shard_map/ppermute | solution.py:376
  29.6 37.8 %copy-start.5 = (bf16[2,128,1024]{2,1,0:T(8,128)(2,1)}, bf16[2,128,1024]{2,1,0:T(8,128)(2,1)S(1)}, u32[]{:S(2)}) copy-start(bf16[2,128,1024]{2,1,0:T(8,128)(2,1)S(1)} %collective-permute-done.3.refs_7_.refs_6_) | copy-start | bytes 1572868
  29.6 22.6 %collective-permute-start.4 = (bf16[2,128,1024]{2,1,0:T(8,128)(2,1)S(1)}, bf16[2,128,1024]{2,1,0:T(8,128)(2,1)}, u32[]{:S(2)}, u32[]{:S(2)}) collective-permute-start(bf16[2,128,1024]{2,1,0:T(8,128)(2,1)S(1)} %collective-permute-done.3.refs_7_.refs_6_), channel_id=1, source_target_pairs={{2,1},{1,0},{6,5},{5,4},{10,9},{9,8},{14,13},{13,12},{18,17},{17,1... | collective-permute-start | bytes 1572872 | tf_op jit(solution)/shard_map/ppermute | solution.py:377
  31.1 36.4 %copy-start.6 = (bf16[2,128,1024]{2,1,0:T(8,128)(2,1)}, bf16[2,128,1024]{2,1,0:T(8,128)(2,1)S(1)}, u32[]{:S(2)}) copy-start(bf16[2,128,1024]{2,1,0:T(8,128)(2,1)S(1)} %collective-permute-done.refs_4_.refs_3_) | copy-start | bytes 1572868
  31.1 22.4 %collective-permute-start.1 = (bf16[2,128,1024]{2,1,0:T(8,128)(2,1)S(1)}, bf16[2,128,1024]{2,1,0:T(8,128)(2,1)}, u32[]{:S(2)}, u32[]{:S(2)}) collective-permute-start(bf16[2,128,1024]{2,1,0:T(8,128)(2,1)S(1)} %collective-permute-done.refs_4_.refs_3_), channel_id=1, source_target_pairs={{1,2},{2,3},{5,6},{6,7},{9,10},{10,11},{13,14},{14,15},{17,18},{18... | collective-permute-start | bytes 1572872 | tf_op jit(solution)/shard_map/ppermute | solution.py:376
  41.0 22.5 %collective-permute-start.10 = (bf16[2,128,1024]{2,1,0:T(8,128)(2,1)}, bf16[2,128,1024]{2,1,0:T(8,128)(2,1)}, u32[]{:S(2)}, u32[]{:S(2)}) collective-permute-start(bf16[2,128,1024]{2,1,0:T(8,128)(2,1)} %collective-permute-done.9.refs_7_.refs_12_), channel_id=1, source_target_pairs={{2,1},{1,0},{6,5},{5,4},{10,9},{9,8},{14,13},{13,12},{18,17},{17,1... | collective-permute-start | bytes 1572872 | tf_op jit(solution)/shard_map/ppermute | solution.py:377
  42.3 22.5 %collective-permute-start.7 = (bf16[2,128,1024]{2,1,0:T(8,128)(2,1)}, bf16[2,128,1024]{2,1,0:T(8,128)(2,1)}, u32[]{:S(2)}, u32[]{:S(2)}) collective-permute-start(bf16[2,128,1024]{2,1,0:T(8,128)(2,1)} %collective-permute-done.6.refs_4_.refs_9_), channel_id=1, source_target_pairs={{1,2},{2,3},{5,6},{6,7},{9,10},{10,11},{13,14},{14,15},{17,18},{18... | collective-permute-start | bytes 1572872 | tf_op jit(solution)/shard_map/ppermute | solution.py:376
  52.2 22.5 %collective-permute-start.5 = (bf16[2,128,1024]{2,1,0:T(8,128)(2,1)}, bf16[2,128,1024]{2,1,0:T(8,128)(2,1)}, u32[]{:S(2)}, u32[]{:S(2)}) collective-permute-start(bf16[2,128,1024]{2,1,0:T(8,128)(2,1)} %collective-permute-done.4.refs_8_.refs_7_), channel_id=1, source_target_pairs={{1,0},{5,4},{9,8},{13,12},{17,16},{21,20},{25,24},{29,28}} | collective-permute-start | bytes 1572872 | tf_op jit(solution)/shard_map/ppermute | solution.py:377
  53.5 21.2 %collective-permute-start.2 = (bf16[2,128,1024]{2,1,0:T(8,128)(2,1)}, bf16[2,128,1024]{2,1,0:T(8,128)(2,1)}, u32[]{:S(2)}, u32[]{:S(2)}) collective-permute-start(bf16[2,128,1024]{2,1,0:T(8,128)(2,1)} %collective-permute-done.1.refs_5_.refs_4_), channel_id=1, source_target_pairs={{2,3},{6,7},{10,11},{14,15},{18,19},{22,23},{26,27},{30,31}} | collective-permute-start | bytes 1572872 | tf_op jit(solution)/shard_map/ppermute | solution.py:376
  63.4 22.1 %collective-permute-start.11 = (bf16[2,128,1024]{2,1,0:T(8,128)(2,1)}, bf16[2,128,1024]{2,1,0:T(8,128)(2,1)}, u32[]{:S(2)}, u32[]{:S(2)}) collective-permute-start(bf16[2,128,1024]{2,1,0:T(8,128)(2,1)} %collective-permute-done.10.refs_8_.refs_13_), channel_id=1, source_target_pairs={{1,0},{5,4},{9,8},{13,12},{17,16},{21,20},{25,24},{29,28}} | collective-permute-start | bytes 1572872 | tf_op jit(solution)/shard_map/ppermute | solution.py:377
  64.7 20.8 %collective-permute-start.8 = (bf16[2,128,1024]{2,1,0:T(8,128)(2,1)}, bf16[2,128,1024]{2,1,0:T(8,128)(2,1)}, u32[]{:S(2)}, u32[]{:S(2)}) collective-permute-start(bf16[2,128,1024]{2,1,0:T(8,128)(2,1)} %collective-permute-done.7.refs_5_.refs_10_), channel_id=1, source_target_pairs={{2,3},{6,7},{10,11},{14,15},{18,19},{22,23},{26,27},{30,31}} | collective-permute-start | bytes 1572872 | tf_op jit(solution)/shard_map/ppermute | solution.py:376
  85.6 8.8 %copy-start.7 = (f32[2,512]{1,0:T(2,128)S(1)}, f32[2,512]{1,0:T(2,128)}, u32[]{:S(2)}) copy-start(f32[2,512]{1,0:T(2,128)} %get-tuple-element.25) | copy-start | bytes 12292
  94.3 1.5 collective-permute-start.14
  95.1 3.7 %collective-permute-start.12 = (f32[4,512]{1,0:T(4,128)S(1)}, f32[4,512]{1,0:T(4,128)S(1)}, u32[]{:S(2)}, u32[]{:S(2)}) collective-permute-start(f32[4,512]{1,0:T(4,128)S(1)} %pad_maximum_fusion), channel_id=1, source_target_pairs={{0,1},{1,0},{2,3},{3,2},{4,5},{5,4},{6,7},{7,6},{8,9},{9,8},{10,11... | collective-permute-start | bytes 24584 | tf_op jit(solution)/shard_map/ppermute | solution.py:341
  96.6 8.2 %collective-permute-start.15 = (f32[40,128]{1,0:T(8,128)S(1)}, f32[40,128]{1,0:T(8,128)S(1)}, u32[]{:S(2)}, u32[]{:S(2)}) collective-permute-start(f32[40,128]{1,0:T(8,128)S(1)} %add_select_fusion.2), channel_id=1, source_target_pairs={{0,8},{4,12},{8,0},{12,4},{16,24},{20,28},{24,16},{28,20},{1,9},{5... | collective-permute-start | bytes 61448 | tf_op jit(solution)/shard_map/ppermute | solution.py:341
  99.4 6.9 %collective-permute-start.13 = (f32[4,512]{1,0:T(4,128)S(1)}, f32[4,512]{1,0:T(4,128)S(1)}, u32[]{:S(2)}, u32[]{:S(2)}) collective-permute-start(f32[4,512]{1,0:T(4,128)S(1)} %multiply_add_fusion.1), channel_id=1, source_target_pairs={{0,2},{1,3},{2,0},{3,1},{4,6},{5,7},{6,4},{7,5},{8,10},{9,11},{10,... | collective-permute-start | bytes 24584 | tf_op jit(solution)/shard_map/ppermute | solution.py:341
  104.8 3.8 %collective-permute-start.16 = (f32[40,128]{1,0:T(8,128)S(1)}, f32[40,128]{1,0:T(8,128)S(1)}, u32[]{:S(2)}, u32[]{:S(2)}) collective-permute-start(f32[40,128]{1,0:T(8,128)S(1)} %add_select_fusion.1), channel_id=1, source_target_pairs={{0,16},{4,20},{8,24},{12,28},{16,0},{20,4},{24,8},{28,12},{1,17},{... | collective-permute-start | bytes 61448 | tf_op jit(solution)/shard_map/ppermute | solution.py:341
  124.4 24.6 %collective-permute-start.17 = (bf16[528,1024]{1,0:T(8,128)(2,1)}, bf16[528,1024]{1,0:T(8,128)(2,1)S(1)}, u32[]{:S(2)}, u32[]{:S(2)}) collective-permute-start(bf16[528,1024]{1,0:T(8,128)(2,1)} %get-tuple-element.34), channel_id=1, source_target_pairs={{0,1},{3,2},{4,5},{7,6},{8,9},{11,10},{12,13},{15,14},{16,17},{19,... | collective-permute-start | bytes 3244040 | tf_op jit(solution)/shard_map/ppermute | solution.py:488
  127.5 26.5 %collective-permute-start.18 = (bf16[528,1024]{1,0:T(8,128)(2,1)}, bf16[528,1024]{1,0:T(8,128)(2,1)S(1)}, u32[]{:S(2)}, u32[]{:S(2)}) collective-permute-start(bf16[528,1024]{1,0:T(8,128)(2,1)} %get-tuple-element.35), channel_id=1, source_target_pairs={{2,0},{1,3},{6,4},{5,7},{10,8},{9,11},{14,12},{13,15},{18,16},{17,... | collective-permute-start | bytes 3244040 | tf_op jit(solution)/shard_map/ppermute | solution.py:488
  149.0 5.0 %copy-start.4 = (bf16[528,1024]{1,0:T(8,128)(2,1)}, bf16[528,1024]{1,0:T(8,128)(2,1)S(1)}, u32[]{:S(2)}) copy-start(bf16[528,1024]{1,0:T(8,128)(2,1)S(1)} %collective-permute-done.17) | copy-start | bytes 3244036
  154.0 66.7 %all-to-all-start.1 = ((bf16[8,272,1024]{2,1,0:T(8,128)(2,1)}), bf16[8,272,1024]{2,1,0:T(8,128)(2,1)}, u32[]{:S(2)}, u32[]{:S(2)}) async-start(bf16[8,272,1024]{2,1,0:T(8,128)(2,1)} %get-tuple-element.36), calls=%async_computation.1 | async-start | bytes 8912896 | tf_op jit(solution)/shard_map/all_to_all | solution.py:495
  158.7 56.9 %copy-start.2 = (bf16[528,1024]{1,0:T(8,128)(2,1)S(1)}, bf16[528,1024]{1,0:T(8,128)(2,1)}, u32[]{:S(2)}) copy-start(bf16[528,1024]{1,0:T(8,128)(2,1)} %get-tuple-element.38) | copy-start | bytes 3244036
  161.4 13.6 %collective-permute-start.19 = (bf16[528,1024]{1,0:T(8,128)(2,1)}, bf16[528,1024]{1,0:T(8,128)(2,1)S(1)}, u32[]{:S(2)}, u32[]{:S(2)}) collective-permute-start(bf16[528,1024]{1,0:T(8,128)(2,1)} %add_convert_fusion), channel_id=1, source_target_pairs={{2,1},{1,2},{6,5},{5,6},{10,9},{9,10},{14,13},{13,14},{18,17},{17,... | collective-permute-start | bytes 3244040 | tf_op jit(solution)/shard_map/ppermute | solution.py:488
  162.2 30.8 %collective-permute-start.20 = (bf16[528,1024]{1,0:T(8,128)(2,1)}, bf16[528,1024]{1,0:T(8,128)(2,1)}, u32[]{:S(2)}, u32[]{:S(2)}) collective-permute-start(bf16[528,1024]{1,0:T(8,128)(2,1)} %get-tuple-element.41), channel_id=1, source_target_pairs={{3,0},{0,3},{7,4},{4,7},{11,8},{8,11},{15,12},{12,15},{19,16},{16,... | collective-permute-start | bytes 3244040 | tf_op jit(solution)/shard_map/ppermute | solution.py:488
  166.5 49.1 %collective-permute-start.21 = (bf16[528,1024]{1,0:T(8,128)(2,1)}, bf16[528,1024]{1,0:T(8,128)(2,1)}, u32[]{:S(2)}, u32[]{:S(2)}) collective-permute-start(bf16[528,1024]{1,0:T(8,128)(2,1)} %get-tuple-element.43), channel_id=1, source_target_pairs={{1,0},{2,3},{5,4},{6,7},{9,8},{10,11},{13,12},{14,15},{17,16},{18,... | collective-permute-start | bytes 3244040 | tf_op jit(solution)/shard_map/ppermute | solution.py:488
  167.8 47.8 %collective-permute-start.22 = (bf16[528,1024]{1,0:T(8,128)(2,1)}, bf16[528,1024]{1,0:T(8,128)(2,1)}, u32[]{:S(2)}, u32[]{:S(2)}) collective-permute-start(bf16[528,1024]{1,0:T(8,128)(2,1)} %get-tuple-element.45), channel_id=1, source_target_pairs={{0,1},{3,2},{4,5},{7,6},{8,9},{11,10},{12,13},{15,14},{16,17},{19,... | collective-permute-start | bytes 3244040 | tf_op jit(solution)/shard_map/ppermute | solution.py:488
  (1 other events, 4.7 us)

commit v3 on v2

v3 whole, which is shorter than its diff:
```python
import functools
import math

import jax
import jax.numpy as jnp
from jax import lax
from jax.experimental import pallas as pl
from jax.experimental.pallas import tpu as pltpu
from jax.sharding import PartitionSpec as P

CAP = 2
NEG_FILL = -1e30
LOG2E = math.log2(math.e)
LN2 = math.log(2.0)
ANY = pl.BlockSpec(memory_space=pl.ANY)
SMEM = pl.BlockSpec(memory_space=pltpu.SMEM)
VMEM = pl.BlockSpec(memory_space=pltpu.VMEM)
EXTRA = 16
GROUPED = 3
MIB = 1024 * 1024


def slot_tables(neg_lists, groups, per_group, slot_depth):
    block_count = neg_lists.shape[0]
    block_ids = jnp.arange(block_count, dtype=jnp.int32)
    named = jnp.any(neg_lists[:, :, None] == block_ids[None, None, :], axis=1)
    present = jnp.any(named.reshape(groups, per_group, block_count), axis=1)
    present = present.reshape(groups, groups, per_group).astype(jnp.int32)
    slot_ranks = jnp.cumsum(present, axis=2) - 1
    slot_ids = jnp.arange(slot_depth, dtype=jnp.int32)
    hits = (present[..., None] == 1) & (slot_ranks[..., None] == slot_ids[None, None, None, :])
    local_ids = jnp.arange(per_group, dtype=jnp.int32)
    slot_block = jnp.sum(jnp.where(hits, local_ids[None, None, :, None], 0), axis=2)
    slot_live = jnp.any(hits, axis=2)
    return (slot_ranks, slot_block, slot_live)


def join_log2(a, b):
    return jnp.maximum(a, b) + jnp.log2(1.0 + jnp.exp2(-jnp.abs(a - b)))


def row_tile(rows):
    return math.gcd(rows, 256)


def dot_t(a, b):
    return lax.dot_general(a, b, (((1,), (1,)), ((), ())), preferred_element_type=jnp.float32)


def dot_n(a, b):
    return lax.dot_general(a, b, (((0,), (0,)), ((), ())), preferred_element_type=jnp.float32)


def cand_copy(own_p, far_p, slot_ref, picks, block, k, dst, sem):
    rows = own_p.shape[1]
    src = own_p.at[block] if k == 0 else far_p.at[slot_ref[block * picks + k - 1]]
    return pltpu.make_async_copy(src, dst.at[pl.ds(k * rows, rows)], sem)


def query_copies(block, chunk, pos, own_q, from_left, from_right, dst, sems, arrive):
    first, inner = chunk[0], len(from_left) + 1
    rows = own_q.shape[1]

    def piece(src, at, k):
        return pltpu.make_async_copy(src, dst.at[pl.ds(pl.multiple_of(at * rows, rows), rows)], sems.at[k])

    if arrive:
        for k in range(inner):
            piece(own_q.at[block], k, k).wait()
        return
    piece(own_q.at[block], pos, 0).start()
    for k in range(1, inner):
        @pl.when(pos >= k)
        def _():
            piece(from_left[k - 1].at[block - first], pos - k, k).start()

        @pl.when(pos < k)
        def _():
            piece(from_right[inner - k - 1].at[block - first], pos - k + inner, k).start()


def collect_kernel(picks, slot_ref, own_p, far_p, cands, sems):
    copies = [
        cand_copy(own_p, far_p, slot_ref, picks, b, k, cands.at[b], sems.at[b, k])
        for b in range(cands.shape[0])
        for k in range(picks + 1)
    ]
    for copy in copies:
        copy.start()
    for copy in copies:
        copy.wait()


def forward_kernel(chunk, inner, picks, scale, *refs):
    pos_ref, id_ref, own_q = refs[:3]
    from_left = refs[3:2 + inner]
    from_right = refs[2 + inner:1 + 2 * inner]
    cands, col_in, row_out, col_out, l_out, whole_q, q_sems = refs[1 + 2 * inner:]
    rows = own_q.shape[1]
    full = rows * inner
    tile = row_tile(full)
    pos = pos_ref[0]
    first, count = chunk

    def queries(b, arrive):
        query_copies(first + b, chunk, pos, own_q, from_left, from_right, whole_q.at[b], q_sems.at[b], arrive)

    for b in range(count):
        queries(b, False)
    col_out[...] = col_in[...]
    for b in range(count):
        queries(b, True)
        block_col = None
        for t in range(full // tile):
            logits = dot_t(whole_q[b, t * tile:(t + 1) * tile, :], cands[first + b]) * scale
            l_out[b, t * tile:(t + 1) * tile] = logits
            peak = jnp.max(logits, axis=1, keepdims=True)
            mass = jnp.sum(jnp.exp2(logits - peak), axis=1, keepdims=True)
            row_lse = jnp.broadcast_to(peak + jnp.log2(mass), (tile, 128))
            row_out[b:b + 1, t * tile:(t + 1) * tile] = row_lse.T[0:1, :]
            col_peak = jnp.max(logits, axis=0, keepdims=True)
            col_mass = jnp.sum(jnp.exp2(logits - col_peak), axis=0, keepdims=True)
            col_lse = col_peak + jnp.log2(col_mass)
            block_col = col_lse if block_col is None else join_log2(block_col, col_lse)
        for k in range(picks + 1):
            row = pl.ds(id_ref[(first + b) * (picks + 1) + k], 1)
            col_out[row, :] = join_log2(col_out[row, :], block_col[:, k * rows:(k + 1) * rows])


def scatter_plan(inner):
    if inner == 4:
        return [
            (((0, 1), (3, 2), (2, 0), (1, 3)), {0: 2, 3: 1, 2: 0, 1: 3}, None, (), (0, 3)),
            (((2, 1), (1, 2), (3, 0), (0, 3)), {2: 1, 1: 2, 3: 0, 0: 3}, (0, (1, 2)), (0,), (0, 1, 2, 3)),
            (((0, 1), (1, 0), (2, 3), (3, 2)), {0: 1, 1: 0, 2: 3, 3: 2}, None, (0,), (0, 1, 2, 3)),
        ]
    plan, place = [], {}
    for m in range(inner - 1):
        for t in range(inner - 1 - m):
            place[(t, m)] = len(plan)
            pairs = ((t, t + 1), (inner - 1 - t, inner - 2 - t))
            sends = {t: inner - 1 - m, inner - 1 - t: m}
            adds = (place[(t - 1, m)], tuple(sends)) if t else None
            plan.append((pairs, sends, adds, (), (t + 1, inner - 2 - t) if m == inner - 2 - t else ()))
    return plan


def one_of(pos, devices):
    return functools.reduce(jnp.logical_or, [pos == d for d in devices])


def slice_for(pos, sends):
    at = 0
    for device, target in sends.items():
        at = jnp.where(pos == device, target, at)
    return at


def in_pieces(value, width, lane):
    high = value.astype(jnp.bfloat16).astype(jnp.float32)
    mid = (value - high).astype(jnp.bfloat16).astype(jnp.float32)
    low = value - high - mid
    at = lax.broadcasted_iota(jnp.int32, (EXTRA, width), 1) - lane
    pieces = jnp.where(at == 0, high, jnp.where(at == 1, mid, jnp.where(at == 2, low, 0.0)))
    return pieces.astype(jnp.bfloat16)


def column_lse(b, picks, id_ref, col_lse):
    return jnp.concatenate(
        [col_lse[pl.ds(id_ref[b * (picks + 1) + k], 1), :] for k in range(picks + 1)], axis=1
    ) + 1.0


def block_weights(logits, row, col, first_row, rows, w_ref):
    probs = jnp.exp2(logits - row) + jnp.exp2(logits - col)
    r_id = lax.broadcasted_iota(jnp.int32, (logits.shape[0], rows), 0) + first_row
    c_id = lax.broadcasted_iota(jnp.int32, (logits.shape[0], rows), 1)
    target = jnp.where(r_id == c_id, 1.0, 0.0)
    w_ref[:, 0:rows] = (probs[:, 0:rows] - target).astype(jnp.bfloat16)
    w_ref[:, rows:] = probs[:, rows:].astype(jnp.bfloat16)


def loss_piece(blocks, pos, col_lse, width):
    value = jnp.sum(col_lse[0:blocks, :]) * LN2 - 2.0 * jnp.sum(col_lse[blocks:blocks + 1, 0:1])
    return in_pieces(value, width, 3 * pos)


def early_kernel(sends, chunks, blocks, inner, picks, *refs):
    pos_ref, id_ref, cands, row_lse, col_lse = refs[:5]
    l_refs = refs[5:5 + len(chunks)]
    out, w_buf, row_buf, dq_buf, sems = refs[5 + len(chunks):]
    per_group, full = row_lse.shape
    rows = full // inner
    width = out.shape[1]
    pos = pos_ref[0]
    at = slice_for(pos, sends)
    start = pl.multiple_of(at * rows, rows)
    home = {first + n: (c, n) for c, (first, size) in enumerate(chunks) for n in range(size)}
    dq_buf[per_group * rows:] = loss_piece(blocks, pos, col_lse, width)

    def copy(b):
        part = pl.ds(b * rows, rows if b < per_group else EXTRA)
        return pltpu.make_async_copy(dq_buf.at[part], out.at[part], sems.at[b])

    copy(per_group).start()
    for b in range(per_group):
        c, n = home[b]
        row_buf[...] = jnp.broadcast_to(row_lse[b:b + 1, :] + 1.0, (128, full)).T
        block_weights(
            l_refs[c][n, pl.ds(start, rows), :], row_buf[pl.ds(start, rows), 0:1],
            column_lse(b, picks, id_ref, col_lse), (at - pos) * rows, rows, w_buf.at[b],
        )
        grad = jnp.dot(w_buf[b], cands[b], preferred_element_type=jnp.float32)
        dq_buf[b * rows:(b + 1) * rows] = grad.astype(jnp.bfloat16)
        copy(b).start()
    for b in range(per_group + 1):
        copy(b).wait()


def query_kernel(out_slices, chunks, blocks, inner, picks, *refs):
    pos_ref, id_ref, cands, row_lse, col_lse = refs[:5]
    l_refs = refs[5:5 + len(chunks)]
    refs = refs[5 + len(chunks):]
    outs = refs[:len(out_slices)]
    w_buf, dq_buf, piece_buf, dq_sems = refs[len(out_slices):]
    per_group, full, width = dq_buf.shape
    rows = full // inner
    tile = row_tile(full)
    pos = pos_ref[0]
    home = {at + n: (c, n) for c, (at, size) in enumerate(chunks) for n in range(size)}

    def outgoing(b, act):
        for n, (out, sends) in enumerate(zip(outs, out_slices)):
            @pl.when(one_of(pos, sends))
            def _():
                if b < per_group:
                    at = pl.multiple_of(slice_for(pos, sends) * rows, rows)
                    src, dst = dq_buf.at[b, pl.ds(at, rows)], out.at[pl.ds(b * rows, rows)]
                else:
                    src, dst = piece_buf, out.at[pl.ds(per_group * rows, EXTRA)]
                copy = pltpu.make_async_copy(src, dst, dq_sems.at[b, n])
                copy.wait() if act == "wait" else copy.start()

    piece_buf[...] = loss_piece(blocks, pos, col_lse, width)
    outgoing(per_group, "start")
    for b in range(per_group):
        c, n = home[b]
        col = column_lse(b, picks, id_ref, col_lse)
        row = jnp.broadcast_to(row_lse[b:b + 1, :] + 1.0, (128, full)).T
        for t in range(full // tile):
            part = slice(t * tile, (t + 1) * tile)
            block_weights(
                l_refs[c][n, part, :], row[part, 0:1], col, t * tile - pos * rows, rows, w_buf.at[b, part]
            )
            grad = jnp.dot(w_buf[b, part, :], cands[b], preferred_element_type=jnp.float32)
            dq_buf[b, part] = grad.astype(jnp.bfloat16)
        outgoing(b, "start")
    for b in range(per_group + 1):
        outgoing(b, "wait")


def passage_kernel(chunks, picks, *refs):
    slot_ref, row_lse, weights = refs[:3]
    q_refs = refs[3:3 + len(chunks)]
    own_out, far_out, own_acc, far_acc, far_buf, far_sems = refs[3 + len(chunks):]
    per_group, rows, width = own_acc.shape
    groups, packed = far_buf.shape[:2]
    depth = packed // rows
    home = {at + n: (c, n) for c, (at, size) in enumerate(chunks) for n in range(size)}

    def own_copy(b):
        return pltpu.make_async_copy(own_acc.at[b], own_out.at[b], far_sems.at[groups + b])

    far_acc[...] = jnp.zeros_like(far_acc)
    for b in range(per_group):
        c, n = home[b]
        step = math.gcd(picks + 1, GROUPED)
        for k in range(0, picks + 1, step):
            parts = dot_n(weights[b, :, k * rows:(k + step) * rows], q_refs[c][n])
            for j in range(step):
                part = parts[j * rows:(j + 1) * rows]
                if k + j == 0:
                    own_acc[b] = part
                    own_copy(b).start()
                else:
                    slot = slot_ref[b * picks + k + j - 1]
                    far_acc[slot] = far_acc[slot] + part
    row_pieces = in_pieces(jnp.sum(row_lse[0:per_group, :]) * LN2, width, 0)
    for g in range(groups):
        for c in range(depth):
            far_buf[g, c * rows:(c + 1) * rows] = far_acc[g * depth + c].astype(jnp.bfloat16)
        far_buf[g, depth * rows:] = row_pieces
        pltpu.make_async_copy(far_buf.at[g], far_out.at[g], far_sems.at[g]).start()
    for g in range(groups):
        pltpu.make_async_copy(far_buf.at[g], far_out.at[g], far_sems.at[g]).wait()
    for b in range(per_group):
        own_copy(b).wait()


def finish_kernel(depth, inner, finals, pos_ref, dest_ref, mine_ref, own_ref, far_ref, *refs):
    moved = refs[:len(finals)]
    q_out, p_out, loss_ref, acc, got, q_got, sems, q_sems = refs[len(finals):]
    groups = far_ref.shape[0]
    per_group, rows, _ = p_out.shape
    pos = pos_ref[0]

    def far_copy(g):
        return pltpu.make_async_copy(far_ref.at[g], got.at[g], sems.at[g])

    def moved_copy(n):
        return pltpu.make_async_copy(moved[n], q_got.at[n], q_sems.at[n])

    for n, devices in enumerate(finals):
        @pl.when(one_of(pos, devices))
        def _():
            moved_copy(n).start()
    for g in range(groups):
        far_copy(g).start()
    ends = {}
    for d in range(inner):
        ends.setdefault(tuple(n for n, devices in enumerate(finals) if d in devices), []).append(d)
    lane = lax.broadcasted_iota(jnp.int32, (8, 128), 1)
    for which, devices in ends.items():
        @pl.when(one_of(pos, devices))
        def _():
            for n in which:
                moved_copy(n).wait()
            for b in range(per_group):
                part = slice(b * rows, (b + 1) * rows)
                value = mine_ref[part, :].astype(jnp.float32)
                for n in which:
                    value = value + q_got[n, part, :].astype(jnp.float32)
                q_out[b] = value.astype(jnp.bfloat16)
            piece = mine_ref[per_group * rows:, 0:128].astype(jnp.float32)
            for n in which:
                piece = piece + q_got[n, per_group * rows:, 0:128].astype(jnp.float32)
            loss_ref[...] = jnp.where(lane < 3 * inner, piece[0:8], 0.0)
    acc[0:per_group] = own_ref[...]
    pieces = loss_ref[...]
    for g in range(groups):
        far_copy(g).wait()
        for c in range(depth):
            dest = dest_ref[g * depth + c]
            acc[dest] = acc[dest] + got[g, c * rows:(c + 1) * rows].astype(jnp.float32)
        pieces = pieces + got[g, depth * rows:, 0:128].astype(jnp.float32)[0:8]
    loss_ref[...] = jnp.sum(pieces, axis=1, keepdims=True) + jnp.zeros((8, 128), jnp.float32)
    p_out[...] = acc[0:per_group].astype(jnp.bfloat16)


def after(value, *events):
    return lax.optimization_barrier((value, *events))[0]


def doublings(size):
    return [1 << n for n in range(size.bit_length() - 1)]


def butterfly(value, axis, size, join):
    for step in doublings(size):
        other = lax.ppermute(value, axis, [(i, i ^ step) for i in range(size)])
        value = join(value, other)
    return value


def body(queries, passages, neg_lists):
    per_group, rows, width = queries.shape
    picks = neg_lists.shape[1]
    blocks = neg_lists.shape[0]
    groups = lax.axis_size("dp")
    inner = lax.axis_size("inner")
    full = rows * inner
    cand_rows = (picks + 1) * rows
    slot_count = groups * CAP
    scale = 1.0 / math.sqrt(width)
    my_group = lax.axis_index("dp")
    pos = lax.axis_index("inner")
    f32, bf16 = jnp.float32, jnp.bfloat16

    def params(mib):
        return pltpu.CompilerParams(vmem_limit_bytes=mib * MIB)

    def in_hbm(*shape):
        return pltpu.HBM(shape, bf16)

    def resident(value):
        return pltpu.with_memory_space_constraint(value, pltpu.VMEM)

    block_flops = 2 * full * cand_rows * width
    block_bytes = 2 * (full + cand_rows) * width

    def cost(blocks, products):
        return pl.CostEstimate(
            flops=blocks * products * block_flops, bytes_accessed=blocks * products * block_bytes, transcendentals=0
        )

    half = per_group // 2
    chunks = [(0, half), (half, per_group - half)]
    lefts = [[] for _ in chunks]
    rights = [[] for _ in chunks]
    moving = [[queries[at:at + size]] * 2 for at, size in chunks]
    for s in range(1, inner):
        for c in range(len(chunks)):
            moving[c] = [
                lax.ppermute(moving[c][0], "inner", [(i, i + 1) for i in range(s - 1, inner - 1)]),
                lax.ppermute(moving[c][1], "inner", [(i, i - 1) for i in range(inner - s, 0, -1)]),
            ]
            lefts[c].append(moving[c][0])
            rights[c].append(moving[c][1])

    slot_ranks, slot_block, slot_live = slot_tables(neg_lists, groups, per_group, CAP)
    listed = lax.dynamic_slice_in_dim(neg_lists, my_group * per_group, per_group, 0)
    my_ranks = lax.dynamic_index_in_dim(slot_ranks, my_group, 0, keepdims=False)
    slot_of = (listed // per_group) * CAP + my_ranks[listed // per_group, listed % per_group]
    slot_flat = slot_of.reshape(-1)
    own_ids = my_group * per_group + jnp.arange(per_group, dtype=jnp.int32)
    id_flat = jnp.concatenate([own_ids[:, None], listed], axis=1).reshape(-1)
    pos_arr = pos.reshape(1)
    sends_for = lax.dynamic_index_in_dim(slot_block, my_group, 1, keepdims=False)
    live_for = lax.dynamic_index_in_dim(slot_live, my_group, 1, keepdims=False)
    outgoing = passages[sends_for]
    arrived = lax.all_to_all(outgoing, "dp", split_axis=0, concat_axis=0, tiled=True)
    arrived = arrived.reshape(slot_count, rows, width)

    own_sum = jnp.sum(queries.astype(f32) * passages.astype(f32)) * scale
    col = jnp.concatenate([jnp.full((blocks, rows), NEG_FILL, f32), jnp.broadcast_to(own_sum, (8, rows))])
    cands = pl.pallas_call(
        functools.partial(collect_kernel, picks),
        out_shape=pltpu.VMEM((per_group, cand_rows, width), bf16),
        in_specs=[SMEM, ANY, ANY],
        out_specs=VMEM,
        scratch_shapes=[pltpu.SemaphoreType.DMA((per_group, picks + 1))],
        compiler_params=params(2),
        name="collect",
    )(slot_flat, passages, arrived)
    cands = resident(cands)
    row_parts, logits, wholes = [], [], []
    for c, chunk in enumerate(chunks):
        row_part, col, logit, whole = pl.pallas_call(
            functools.partial(forward_kernel, chunk, inner, picks, scale * LOG2E),
            out_shape=(
                jax.ShapeDtypeStruct((chunk[1], full), f32),
                jax.ShapeDtypeStruct(col.shape, f32),
                pltpu.VMEM((chunk[1], full, cand_rows), f32),
                pltpu.VMEM((chunk[1], full, width), bf16),
            ),
            in_specs=[SMEM] * 2 + [ANY] * (2 * inner - 1) + [VMEM] * 2,
            out_specs=(VMEM,) * 4,
            scratch_shapes=[pltpu.SemaphoreType.DMA((chunk[1], inner))],
            compiler_params=params(12),
            cost_estimate=cost(chunk[1], 1),
            name=f"forward_{c}",
        )(pos_arr, id_flat, queries, *lefts[c], *rights[c], cands, col)
        row_parts.append(row_part)
        logits.append(resident(logit))
        wholes.append(resident(whole))
    row = jnp.concatenate(row_parts, axis=0)
    is_lse = jnp.arange(blocks + 8)[:, None] < blocks
    col_lse = butterfly(col, "dp", groups, lambda a, b: jnp.where(is_lse, join_log2(a, b), a + b))
    row_lse = butterfly(row, "inner", inner, join_log2)

    packed = CAP * rows + EXTRA
    flat = per_group * rows + EXTRA
    plan = scatter_plan(inner)
    first = pl.pallas_call(
        functools.partial(early_kernel, plan[0][1], chunks, blocks, inner, picks),
        out_shape=in_hbm(flat, width),
        in_specs=[SMEM] * 2 + [VMEM] * (3 + len(chunks)),
        out_specs=ANY,
        scratch_shapes=[
            pltpu.VMEM((per_group, rows, cand_rows), bf16),
            pltpu.VMEM((full, 128), f32),
            pltpu.VMEM((flat, width), bf16),
            pltpu.SemaphoreType.DMA((per_group + 1,)),
        ],
        compiler_params=params(12),
        cost_estimate=cost(1, 1),
        name="early",
    )(pos_arr, id_flat, cands, row_lse, col_lse, *logits)
    own_slice = {d: d for d in range(inner)}
    out_slices = [sends for _, sends, _, _, _ in plan[1:]] + [own_slice]
    *parts, mine, weights = pl.pallas_call(
        functools.partial(query_kernel, out_slices, chunks, blocks, inner, picks),
        out_shape=(in_hbm(flat, width),) * len(out_slices) + (pltpu.VMEM((per_group, full, cand_rows), bf16),),
        in_specs=[SMEM] * 2 + [VMEM] * (3 + len(chunks)),
        out_specs=(ANY,) * len(out_slices) + (VMEM,),
        scratch_shapes=[
            pltpu.VMEM((per_group, full, width), bf16),
            pltpu.VMEM((EXTRA, width), bf16),
            pltpu.SemaphoreType.DMA((per_group + 1, len(out_slices))),
        ],
        compiler_params=params(14),
        cost_estimate=cost(per_group, 1),
        name="query",
    )(pos_arr, id_flat, cands, row_lse, col_lse, *logits)
    parts = [first] + parts

    own_grad, far_grad = pl.pallas_call(
        functools.partial(passage_kernel, chunks, picks),
        out_shape=(
            jax.ShapeDtypeStruct((per_group, rows, width), f32),
            in_hbm(groups, packed, width),
        ),
        in_specs=[SMEM] + [VMEM] * (2 + len(chunks)),
        out_specs=(ANY, ANY),
        scratch_shapes=[
            pltpu.VMEM((per_group, rows, width), f32),
            pltpu.VMEM((slot_count, rows, width), f32),
            pltpu.VMEM((groups, packed, width), bf16),
            pltpu.SemaphoreType.DMA((groups + per_group,)),
        ],
        compiler_params=params(28),
        cost_estimate=cost(per_group, 1),
        name="passage",
    )(slot_flat, row_lse, resident(weights), *wholes)

    sums = []
    for (pairs, _, adds, gates, _), out in zip(plan, parts):
        if adds is not None:
            arrived_sum = jnp.where(one_of(pos, adds[1]), sums[adds[0]].astype(f32), 0.0)
            out = (out.astype(f32) + arrived_sum).astype(bf16)
        if gates:
            out = after(out, *[sums[g] for g in gates])
        sums.append(lax.ppermute(out, "inner", pairs))
    finals = [(devices, value) for (_, _, _, _, devices), value in zip(plan, sums) if devices]

    far_grad = after(far_grad, sums[0])
    returned = lax.all_to_all(far_grad, "dp", split_axis=0, concat_axis=0, tiled=True)
    dest = jnp.where(live_for, sends_for, per_group).reshape(-1)
    query_grad, passage_grad, total = pl.pallas_call(
        functools.partial(finish_kernel, CAP, inner, [devices for devices, _ in finals]),
        out_shape=(
            jax.ShapeDtypeStruct((per_group, rows, width), bf16),
            jax.ShapeDtypeStruct((per_group, rows, width), bf16),
            jax.ShapeDtypeStruct((8, 128), f32),
        ),
        in_specs=[SMEM] * 2 + [VMEM] * 2 + [ANY] * (1 + len(finals)),
        out_specs=(VMEM,) * 3,
        scratch_shapes=[
            pltpu.VMEM((per_group + 1, rows, width), f32),
            pltpu.VMEM((groups, packed, width), bf16),
            pltpu.VMEM((len(finals), flat, width), bf16),
            pltpu.SemaphoreType.DMA((groups,)),
            pltpu.SemaphoreType.DMA((len(finals),)),
        ],
        compiler_params=params(28),
        name="finish",
    )(pos_arr, dest, mine, own_grad, returned, *[value for _, value in finals])
    mean_loss = total[0, 0] / (2.0 * groups * per_group * full)
    return (mean_loss, query_grad, passage_grad)


def solution(mesh):
    in_specs = (P("dp", "inner", None), P("dp", "inner", None), P())
    out_specs = (P(), P("dp", "inner", None), P("dp", "inner", None))
    return jax.shard_map(body, mesh=mesh, in_specs=in_specs, out_specs=out_specs, check_vma=False)
```

time: 230 us -> 202 us (0.88)
  starting transfers between devices: 59.8 us -> 47 us
  other arithmetic: 12 us -> 4.74 us
  Pallas kernels: 48.4 us -> 44.9 us
  local copies, waits for them, and re-layouts: 12.2 us -> 9.41 us
    ppermute x6 -> x3, starting transfers between devices: 17.3 us -> 4.13 us  [body(): sums.append(lax.ppermute(out, 'inner', pairs))]
    pallas_call x2, Pallas kernels: 17.5 us -> 12.1 us  [body(): pl.pallas_call(functools.partial(forward_kernel, chunk, inner, picks, sca...]
    add x1 -> x0, other arithmetic: 3.31 us -> none  [body(): query_sum = query_sum + sums[-1]]
    ppermute x6 -> x3, waiting for transfers between devices: 54.7 us -> 52.7 us  [body(): sums.append(lax.ppermute(out, 'inner', pairs))]
    pallas_call x3 -> x5, Pallas kernels: 30.8 us -> 32.8 us  [the longest x1 9.88 us: body(): pl.pallas_call(functools.partial(passage_kernel, chunks, picks), out_shap...]
  transfers between devices with their start and end apart: 25 -> 22, of which waited for: 14 -> 12; matrix products, arithmetic and copies ran while one was open for 7% -> 3% of each run, Pallas kernels for 9% -> 14%
where the time goes in v3:
time: 202 us; the launch traced here: 201 us
  waiting for transfers between devices  91.9 us (45%)
  starting transfers between devices  47 us (23%)
  Pallas kernels  44.9 us (22%)
  local copies, waits for them, and re-layouts  9.41 us (5%)
  other arithmetic  4.74 us (2%)
  between operations  3.36 us (2%)
    ppermute x3, waiting for transfers between devices, body(): sums.append(lax.ppermute(out, 'inner', pairs))  52.7 us
    ppermute x6, waiting for transfers between devices, body(): lax.ppermute(moving[c][1], 'inner', [(i, i - 1) for i in range(inner - s,...  35 us
    ppermute x6, starting transfers between devices, body(): lax.ppermute(moving[c][0], 'inner', [(i, i + 1) for i in range(s - 1, inn...  16.2 us
    pallas_call x2, Pallas kernels, body(): pl.pallas_call(functools.partial(forward_kernel, chunk, inner, picks, sca...  12.1 us
    pallas_call x1, Pallas kernels, body(): pl.pallas_call(functools.partial(passage_kernel, chunks, picks), out_shap...  9.88 us
    ppermute x5, starting transfers between devices, butterfly(): other = lax.ppermute(value, axis, [(i, i ^ step) for i in range(size)])  8.81 us
    pallas_call x1, Pallas kernels, body(): pl.pallas_call(functools.partial(query_kernel, out_slices, chunks, blocks...  8.58 us
    ppermute x6, starting transfers between devices, body(): lax.ppermute(moving[c][1], 'inner', [(i, i - 1) for i in range(inner - s,...  7.68 us
  transfers between devices with their start and end apart: 22, of which 12 were waited for; matrix products, arithmetic and copies ran while one was open for 3% of the time, Pallas kernels for 14%

profile of v3, /device:TPU:0, one launch (start us, length us, event | category | flops | bytes accessed | tf_op | source)
XLA Modules:
  0.0 201.3 jit_solution(1698175681762327530)
XLA Ops:
  2.3 4.0 %gather_fusion.1 = bf16[16,128,1024]{2,1,0:T(8,128)(2,1)} fusion(bf16[4,128,1024]{2,1,0:T(8,128)(2,1)} %own_p.1, s32[1024]{0:T(1024)S(1)} %pad_clamp_fusion), kind=kCustom, calls=%fused_computation.1 | custom fusion | bytes 8388672 | tf_op jit(solution)/shard_map/gather | solution.py:420
  6.3 5.3 %all-to-all-start = ((bf16[8,2,128,1024]{3,2,1,0:T(8,128)(2,1)}), bf16[8,2,128,1024]{3,2,1,0:T(8,128)(2,1)}, u32[]{:S(2)}, u32[]{:S(2)}) async-start(bf16[8,2,128,1024]{3,2,1,0:T(8,128)(2,1)} %bitcast.14), calls=%async_computation | async-start | bytes 8388608 | tf_op jit(solution)/shard_map/all_to_all | solution.py:421
  13.8 5.8 %collective-permute-start = (bf16[2,128,1024]{2,1,0:T(8,128)(2,1)S(1)}, bf16[2,128,1024]{2,1,0:T(8,128)(2,1)}, u32[]{:S(2)}, u32[]{:S(2)}) collective-permute-start(bf16[2,128,1024]{2,1,0:T(8,128)(2,1)S(1)} %get-tuple-element.45), channel_id=1, source_target_pairs={{0,1},{1,2},{2,3},{4,5},{5,6},{6,7},{8,9},{9,10},{10,11},{12,13},{... | collective-permute-start | bytes 1572872 | tf_op jit(solution)/shard_map/ppermute | solution.py:404
  20.9 4.6 %collective-permute-start.6 = (bf16[2,128,1024]{2,1,0:T(8,128)(2,1)}, bf16[2,128,1024]{2,1,0:T(8,128)(2,1)S(1)}, u32[]{:S(2)}, u32[]{:S(2)}) collective-permute-start(bf16[2,128,1024]{2,1,0:T(8,128)(2,1)} %get-tuple-element.46), channel_id=1, source_target_pairs={{0,1},{1,2},{2,3},{4,5},{5,6},{6,7},{8,9},{9,10},{10,11},{12,13},{... | collective-permute-start | bytes 1572872 | tf_op jit(solution)/shard_map/ppermute | solution.py:404
  25.5 4.3 %collective-permute-done.3.refs_6_ = bf16[2,128,1024]{2,1,0:T(8,128)(2,1)} collective-permute-done((bf16[2,128,1024]{2,1,0:T(8,128)(2,1)S(1)}, bf16[2,128,1024]{2,1,0:T(8,128)(2,1)}, u32[]{:S(2)}, u32[]{:S(2)}) %collective-permute-start.3) | collective-permute-done | bytes 524320 | tf_op jit(solution)/shard_map/ppermute | solution.py:405
  31.1 1.4 collective-permute-start.1
  32.6 8.3 %collective-permute-done.9.refs_6_ = bf16[2,128,1024]{2,1,0:T(8,128)(2,1)S(1)} collective-permute-done((bf16[2,128,1024]{2,1,0:T(8,128)(2,1)}, bf16[2,128,1024]{2,1,0:T(8,128)(2,1)S(1)}, u32[]{:S(2)}, u32[]{:S(2)}) %collective-permute-start.9) | collective-permute-done | bytes 524320 | tf_op jit(solution)/shard_map/ppermute | solution.py:405
  42.2 1.5 collective-permute-start.7
  44.8 7.4 %collective-permute-done.4.refs_7_ = bf16[2,128,1024]{2,1,0:T(8,128)(2,1)} collective-permute-done((bf16[2,128,1024]{2,1,0:T(8,128)(2,1)}, bf16[2,128,1024]{2,1,0:T(8,128)(2,1)}, u32[]{:S(2)}, u32[]{:S(2)}) %collective-permute-start.4) | collective-permute-done | bytes 524320 | tf_op jit(solution)/shard_map/ppermute | solution.py:405
  53.5 1.5 collective-permute-start.2
  55.1 8.4 %collective-permute-done.10.refs_7_ = bf16[2,128,1024]{2,1,0:T(8,128)(2,1)} collective-permute-done((bf16[2,128,1024]{2,1,0:T(8,128)(2,1)S(1)}, bf16[2,128,1024]{2,1,0:T(8,128)(2,1)}, u32[]{:S(2)}, u32[]{:S(2)}) %collective-permute-start.10) | collective-permute-done | bytes 524320 | tf_op jit(solution)/shard_map/ppermute | solution.py:405
  64.7 1.5 collective-permute-start.8
  68.1 4.4 %collect.1.refs_9_.refs_2_ = bf16[4,1152,1024]{2,1,0:T(8,128)(2,1)S(1)} custom-call(s32[32]{0:T(128)S(1)} %reshape.85.slot_ref.refs_0_, bf16[4,128,1024]{2,1,0:T(8,128)(2,1)S(1)} %copy-done, bf16[16,128,1024]{2,1,0:T(8,128)(2,1)} %bitcast.5.far_p), custom_call_target="tpu_custom_call" | custom-call | tf_op jit(solution)/shard_map/collect/pallas_call | solution.py:426
  72.5 2.1 %collective-permute-done.5.refs_8_ = bf16[2,128,1024]{2,1,0:T(8,128)(2,1)} collective-permute-done((bf16[2,128,1024]{2,1,0:T(8,128)(2,1)}, bf16[2,128,1024]{2,1,0:T(8,128)(2,1)}, u32[]{:S(2)}, u32[]{:S(2)}) %collective-permute-start.5) | collective-permute-done | bytes 524320 | tf_op jit(solution)/shard_map/ppermute | solution.py:405
  74.7 6.1 %forward_0.1 = (f32[2,512]{1,0:T(2,128)S(1)}, f32[40,128]{1,0:T(8,128)S(1)}, f32[2,512,1152]{2,1,0:T(8,128)S(1)}, bf16[2,512,1024]{2,1,0:T(8,128)(2,1)S(1)}) custom-call(s32[1]{0:T(128)} %bitcast.refs_0_.pos_ref, s32[36]{0:T(128)S(1)} %reshape.84.refs_1_, bf16[4,128,1024]{2,1,0:T(8,128)(2,1)S(1)} %copy-done.1, ...), custom_call_target="tpu_custom_call" | custom-call | flops 2415919104 | bytes 6815744 | tf_op jit(solution)/shard_map/forward_0/pallas_call | solution.py:438
  80.9 4.7 %collective-permute-done.11.refs_8_ = bf16[2,128,1024]{2,1,0:T(8,128)(2,1)} collective-permute-done((bf16[2,128,1024]{2,1,0:T(8,128)(2,1)}, bf16[2,128,1024]{2,1,0:T(8,128)(2,1)}, u32[]{:S(2)}, u32[]{:S(2)}) %collective-permute-start.11) | collective-permute-done | bytes 524320 | tf_op jit(solution)/shard_map/ppermute | solution.py:405
  85.6 6.0 %forward_1.1 = (f32[2,512]{1,0:T(2,128)S(1)}, f32[40,128]{1,0:T(8,128)S(1)}, f32[2,512,1152]{2,1,0:T(8,128)S(1)}, bf16[2,512,1024]{2,1,0:T(8,128)(2,1)S(1)}) custom-call(s32[1]{0:T(128)} %bitcast.refs_0_.pos_ref, s32[36]{0:T(128)S(1)} %reshape.84.refs_1_, bf16[4,128,1024]{2,1,0:T(8,128)(2,1)S(1)} %copy-done.1, ...), custom_call_target="tpu_custom_call" | custom-call | flops 2415919104 | bytes 6815744 | tf_op jit(solution)/shard_map/forward_1/pallas_call | solution.py:438
  92.9 1.7 collective-permute-start.15
  95.5 5.4 %collective-permute-start.13 = (f32[4,512]{1,0:T(4,128)S(1)}, f32[4,512]{1,0:T(4,128)S(1)}, u32[]{:S(2)}, u32[]{:S(2)}) collective-permute-start(f32[4,512]{1,0:T(4,128)S(1)} %multiply_add_fusion.1), channel_id=1, source_target_pairs={{0,2},{1,3},{2,0},{3,1},{4,6},{5,7},{6,4},{7,5},{8,10},{9,11},{10,... | collective-permute-start | bytes 24584 | tf_op jit(solution)/shard_map/ppermute | solution.py:360
  100.9 1.6 collective-permute-start.16
  102.5 2.2 %collective-permute-done.16 = f32[40,128]{1,0:T(8,128)S(1)} collective-permute-done((f32[40,128]{1,0:T(8,128)S(1)}, f32[40,128]{1,0:T(8,128)S(1)}, u32[]{:S(2)}, u32[]{:S(2)}) %collective-permute-start.16) | collective-permute-done | bytes 20512 | tf_op jit(solution)/shard_map/ppermute | solution.py:360
  104.8 3.5 %early.1 = bf16[528,1024]{1,0:T(8,128)(2,1)} custom-call(s32[1]{0:T(128)} %bitcast.refs_0_.pos_ref, s32[36]{0:T(128)S(1)} %reshape.84.refs_1_, bf16[4,1152,1024]{2,1,0:T(8,128)(2,1)S(1)} %collect.1.refs_9_.refs_2_, f32[4,512]{1,0:T(4,128)S(1)} %multiply_add_fusion.refs_3_.refs_1_, f32[40,128]{1,0:T(8,128)S(1)} %add_select_fusion.refs_4_, ...), custom_call_target="tpu_custom_call" | custom-call | flops 1207959552 | bytes 3407872 | tf_op jit(solution)/shard_map/early/pallas_call | solution.py:464
  108.3 2.1 %collective-permute-start.17 = (bf16[528,1024]{1,0:T(8,128)(2,1)}, bf16[528,1024]{1,0:T(8,128)(2,1)S(1)}, u32[]{:S(2)}, u32[]{:S(2)}) collective-permute-start(bf16[528,1024]{1,0:T(8,128)(2,1)} %early.1), channel_id=1, source_target_pairs={{0,1},{3,2},{2,0},{1,3},{4,5},{7,6},{6,4},{5,7},{8,9},{11,10},{10,... | collective-permute-start | bytes 3244040 | tf_op jit(solution)/shard_map/ppermute | solution.py:523
  110.4 8.6 %query.1 = (bf16[528,1024]{1,0:T(8,128)(2,1)}, bf16[528,1024]{1,0:T(8,128)(2,1)}, bf16[528,1024]{1,0:T(8,128)(2,1)}, bf16[4,512,1152]{2,1,0:T(8,128)(2,1)S(1)}) custom-call(s32[1]{0:T(128)} %bitcast.refs_0_.pos_ref, s32[36]{0:T(128)S(1)} %reshape.84.refs_1_, bf16[4,1152,1024]{2,1,0:T(8,128)(2,1)S(1)} %collect.1.refs_9_.refs_2_, ...), custom_call_target="tpu_custom_call" | custom-call | flops 4831838208 | bytes 13631488 | tf_op jit(solution)/shard_map/query/pallas_call | solution.py:481
  119.0 9.9 %passage.1 = (f32[4,128,1024]{2,1,0:T(8,128)S(1)}, bf16[8,272,1024]{2,1,0:T(8,128)(2,1)}) custom-call(s32[32]{0:T(128)S(1)} %reshape.85.slot_ref.refs_0_, f32[4,512]{1,0:T(4,128)S(1)} %multiply_add_fusion.refs_3_.refs_1_, bf16[4,512,1152]{2,1,0:T(8,128)(2,1)S(1)} %get-tuple-element.30.refs_2_, bf16[2,512,1024]{2,1,0:T(8,128)(2,1)S(1)} %get-tuple-element.31.refs_3_, ...), custom_call_target="tpu_custom_call" | custom-call | flops 4831838208 | bytes 13631488 | tf_op jit(solution)/shard_map/passage/pallas_call | solution.py:497
  128.9 5.0 %collective-permute-done.17.refs_0_ = bf16[528,1024]{1,0:T(8,128)(2,1)S(1)} collective-permute-done((bf16[528,1024]{1,0:T(8,128)(2,1)}, bf16[528,1024]{1,0:T(8,128)(2,1)S(1)}, u32[]{:S(2)}, u32[]{:S(2)}) %collective-permute-start.17) | collective-permute-done | bytes 1081376 | tf_op jit(solution)/shard_map/ppermute | solution.py:523
  133.9 4.8 %all-to-all-start.1 = ((bf16[8,272,1024]{2,1,0:T(8,128)(2,1)}), bf16[8,272,1024]{2,1,0:T(8,128)(2,1)}, u32[]{:S(2)}, u32[]{:S(2)}) async-start(bf16[8,272,1024]{2,1,0:T(8,128)(2,1)} %get-tuple-element.35), calls=%async_computation.1 | async-start | bytes 8912896 | tf_op jit(solution)/shard_map/all_to_all | solution.py:527
  138.8 2.7 %add_convert_fusion = bf16[528,1024]{1,0:T(8,128)(2,1)} fusion(bf16[528,1024]{1,0:T(8,128)(2,1)S(1)} %collective-permute-done.17.refs_0_, bf16[528,1024]{1,0:T(8,128)(2,1)} %get-tuple-element.36, pred[]{:T(512)S(6)} %or.3), kind=kLoop, calls=%fused_computation.2 | loop fusion | flops 2703360 | bytes 3244033 | tf_op jit(solution)/shard_map/convert_element_type | solution.py:520
  141.8 1.6 collective-permute-start.18
  143.6 24.4 %collective-permute-done.19.refs_2_ = bf16[528,1024]{1,0:T(8,128)(2,1)} collective-permute-done((bf16[528,1024]{1,0:T(8,128)(2,1)}, bf16[528,1024]{1,0:T(8,128)(2,1)}, u32[]{:S(2)}, u32[]{:S(2)}) %collective-permute-start.19) | collective-permute-done | bytes 1081376 | tf_op jit(solution)/shard_map/ppermute | solution.py:523
  168.0 23.3 %collective-permute-done.18.refs_1_ = bf16[528,1024]{1,0:T(8,128)(2,1)} collective-permute-done((bf16[528,1024]{1,0:T(8,128)(2,1)}, bf16[528,1024]{1,0:T(8,128)(2,1)}, u32[]{:S(2)}, u32[]{:S(2)}) %collective-permute-start.18) | collective-permute-done | bytes 1081376 | tf_op jit(solution)/shard_map/ppermute | solution.py:523
  192.6 6.5 %finish.1 = (bf16[4,128,1024]{2,1,0:T(8,128)(2,1)}, bf16[4,128,1024]{2,1,0:T(8,128)(2,1)}, f32[8,128]{1,0:T(8,128)S(1)}) custom-call(s32[1]{0:T(128)} %bitcast.refs_0_.pos_ref, s32[16]{0:T(128)S(1)} %select_n.73.dest_ref, bf16[528,1024]{1,0:T(8,128)(2,1)S(1)} %copy-done.2, f32[4,128,1024]{2,1,0:T(8,128)S(1)} %get-tuple-element.33.own_ref, ...), custom_call_target="tpu_custom_call" | custom-call | tf_op jit(solution)/shard_map/finish/pallas_call | solution.py:529
  (70 shorter events, 17.7 us)
Async XLA Ops:
  6.3 5.3 %copy-start.1 = (bf16[4,128,1024]{2,1,0:T(8,128)(2,1)S(1)}, bf16[4,128,1024]{2,1,0:T(8,128)(2,1)}, u32[]{:S(2)}) copy-start(bf16[4,128,1024]{2,1,0:T(8,128)(2,1)} %refs_2_.3) | copy-start | bytes 3145732
  6.3 61.8 %all-to-all-start = ((bf16[8,2,128,1024]{3,2,1,0:T(8,128)(2,1)}), bf16[8,2,128,1024]{3,2,1,0:T(8,128)(2,1)}, u32[]{:S(2)}, u32[]{:S(2)}) async-start(bf16[8,2,128,1024]{3,2,1,0:T(8,128)(2,1)} %bitcast.14), calls=%async_computation | async-start | bytes 8388608 | tf_op jit(solution)/shard_map/all_to_all | solution.py:421
  11.6 54.6 %copy-start = (bf16[4,128,1024]{2,1,0:T(8,128)(2,1)S(1)}, bf16[4,128,1024]{2,1,0:T(8,128)(2,1)}, u32[]{:S(2)}) copy-start(bf16[4,128,1024]{2,1,0:T(8,128)(2,1)} %own_p.1) | copy-start | bytes 3145732
  12.6 17.2 %collective-permute-start.3 = (bf16[2,128,1024]{2,1,0:T(8,128)(2,1)S(1)}, bf16[2,128,1024]{2,1,0:T(8,128)(2,1)}, u32[]{:S(2)}, u32[]{:S(2)}) collective-permute-start(bf16[2,128,1024]{2,1,0:T(8,128)(2,1)S(1)} %get-tuple-element.45), channel_id=1, source_target_pairs={{3,2},{2,1},{1,0},{7,6},{6,5},{5,4},{11,10},{10,9},{9,8},{15,14},{... | collective-permute-start | bytes 1572872 | tf_op jit(solution)/shard_map/ppermute | solution.py:405
  13.8 17.2 %collective-permute-start = (bf16[2,128,1024]{2,1,0:T(8,128)(2,1)S(1)}, bf16[2,128,1024]{2,1,0:T(8,128)(2,1)}, u32[]{:S(2)}, u32[]{:S(2)}) collective-permute-start(bf16[2,128,1024]{2,1,0:T(8,128)(2,1)S(1)} %get-tuple-element.45), channel_id=1, source_target_pairs={{0,1},{1,2},{2,3},{4,5},{5,6},{6,7},{8,9},{9,10},{10,11},{12,13},{... | collective-permute-start | bytes 1572872 | tf_op jit(solution)/shard_map/ppermute | solution.py:404
  19.6 21.3 %collective-permute-start.9 = (bf16[2,128,1024]{2,1,0:T(8,128)(2,1)}, bf16[2,128,1024]{2,1,0:T(8,128)(2,1)S(1)}, u32[]{:S(2)}, u32[]{:S(2)}) collective-permute-start(bf16[2,128,1024]{2,1,0:T(8,128)(2,1)} %get-tuple-element.46), channel_id=1, source_target_pairs={{3,2},{2,1},{1,0},{7,6},{6,5},{5,4},{11,10},{10,9},{9,8},{15,14},{... | collective-permute-start | bytes 1572872 | tf_op jit(solution)/shard_map/ppermute | solution.py:405
  20.9 21.3 %collective-permute-start.6 = (bf16[2,128,1024]{2,1,0:T(8,128)(2,1)}, bf16[2,128,1024]{2,1,0:T(8,128)(2,1)S(1)}, u32[]{:S(2)}, u32[]{:S(2)}) collective-permute-start(bf16[2,128,1024]{2,1,0:T(8,128)(2,1)} %get-tuple-element.46), channel_id=1, source_target_pairs={{0,1},{1,2},{2,3},{4,5},{5,6},{6,7},{8,9},{9,10},{10,11},{12,13},{... | collective-permute-start | bytes 1572872 | tf_op jit(solution)/shard_map/ppermute | solution.py:404
  29.7 22.5 %collective-permute-start.4 = (bf16[2,128,1024]{2,1,0:T(8,128)(2,1)}, bf16[2,128,1024]{2,1,0:T(8,128)(2,1)}, u32[]{:S(2)}, u32[]{:S(2)}) collective-permute-start(bf16[2,128,1024]{2,1,0:T(8,128)(2,1)} %collective-permute-done.3.refs_6_), channel_id=1, source_target_pairs={{2,1},{1,0},{6,5},{5,4},{10,9},{9,8},{14,13},{13,12},{18,17},{17,1... | collective-permute-start | bytes 1572872 | tf_op jit(solution)/shard_map/ppermute | solution.py:405
  31.1 22.4 %collective-permute-start.1 = (bf16[2,128,1024]{2,1,0:T(8,128)(2,1)}, bf16[2,128,1024]{2,1,0:T(8,128)(2,1)}, u32[]{:S(2)}, u32[]{:S(2)}) collective-permute-start(bf16[2,128,1024]{2,1,0:T(8,128)(2,1)} %collective-permute-done.refs_3_), channel_id=1, source_target_pairs={{1,2},{2,3},{5,6},{6,7},{9,10},{10,11},{13,14},{14,15},{17,18},{18... | collective-permute-start | bytes 1572872 | tf_op jit(solution)/shard_map/ppermute | solution.py:404
  40.9 22.6 %collective-permute-start.10 = (bf16[2,128,1024]{2,1,0:T(8,128)(2,1)S(1)}, bf16[2,128,1024]{2,1,0:T(8,128)(2,1)}, u32[]{:S(2)}, u32[]{:S(2)}) collective-permute-start(bf16[2,128,1024]{2,1,0:T(8,128)(2,1)S(1)} %collective-permute-done.9.refs_6_), channel_id=1, source_target_pairs={{2,1},{1,0},{6,5},{5,4},{10,9},{9,8},{14,13},{13,12},{18,17},{17,1... | collective-permute-start | bytes 1572872 | tf_op jit(solution)/shard_map/ppermute | solution.py:405
  42.2 22.6 %collective-permute-start.7 = (bf16[2,128,1024]{2,1,0:T(8,128)(2,1)S(1)}, bf16[2,128,1024]{2,1,0:T(8,128)(2,1)}, u32[]{:S(2)}, u32[]{:S(2)}) collective-permute-start(bf16[2,128,1024]{2,1,0:T(8,128)(2,1)S(1)} %collective-permute-done.6.refs_3_), channel_id=1, source_target_pairs={{1,2},{2,3},{5,6},{6,7},{9,10},{10,11},{13,14},{14,15},{17,18},{18... | collective-permute-start | bytes 1572872 | tf_op jit(solution)/shard_map/ppermute | solution.py:404
  52.2 22.5 %collective-permute-start.5 = (bf16[2,128,1024]{2,1,0:T(8,128)(2,1)}, bf16[2,128,1024]{2,1,0:T(8,128)(2,1)}, u32[]{:S(2)}, u32[]{:S(2)}) collective-permute-start(bf16[2,128,1024]{2,1,0:T(8,128)(2,1)} %collective-permute-done.4.refs_7_), channel_id=1, source_target_pairs={{1,0},{5,4},{9,8},{13,12},{17,16},{21,20},{25,24},{29,28}} | collective-permute-start | bytes 1572872 | tf_op jit(solution)/shard_map/ppermute | solution.py:405
  53.5 21.2 %collective-permute-start.2 = (bf16[2,128,1024]{2,1,0:T(8,128)(2,1)}, bf16[2,128,1024]{2,1,0:T(8,128)(2,1)}, u32[]{:S(2)}, u32[]{:S(2)}) collective-permute-start(bf16[2,128,1024]{2,1,0:T(8,128)(2,1)} %collective-permute-done.1.refs_4_), channel_id=1, source_target_pairs={{2,3},{6,7},{10,11},{14,15},{18,19},{22,23},{26,27},{30,31}} | collective-permute-start | bytes 1572872 | tf_op jit(solution)/shard_map/ppermute | solution.py:404
  63.4 22.1 %collective-permute-start.11 = (bf16[2,128,1024]{2,1,0:T(8,128)(2,1)}, bf16[2,128,1024]{2,1,0:T(8,128)(2,1)}, u32[]{:S(2)}, u32[]{:S(2)}) collective-permute-start(bf16[2,128,1024]{2,1,0:T(8,128)(2,1)} %collective-permute-done.10.refs_7_), channel_id=1, source_target_pairs={{1,0},{5,4},{9,8},{13,12},{17,16},{21,20},{25,24},{29,28}} | collective-permute-start | bytes 1572872 | tf_op jit(solution)/shard_map/ppermute | solution.py:405
  64.7 20.8 %collective-permute-start.8 = (bf16[2,128,1024]{2,1,0:T(8,128)(2,1)}, bf16[2,128,1024]{2,1,0:T(8,128)(2,1)}, u32[]{:S(2)}, u32[]{:S(2)}) collective-permute-start(bf16[2,128,1024]{2,1,0:T(8,128)(2,1)} %collective-permute-done.7.refs_4_), channel_id=1, source_target_pairs={{2,3},{6,7},{10,11},{14,15},{18,19},{22,23},{26,27},{30,31}} | collective-permute-start | bytes 1572872 | tf_op jit(solution)/shard_map/ppermute | solution.py:404
  91.6 1.3 collective-permute-start.14
  91.7 3.7 %collective-permute-start.12 = (f32[4,512]{1,0:T(4,128)S(1)}, f32[4,512]{1,0:T(4,128)S(1)}, u32[]{:S(2)}, u32[]{:S(2)}) collective-permute-start(f32[4,512]{1,0:T(4,128)S(1)} %pad_maximum_fusion), channel_id=1, source_target_pairs={{0,1},{1,0},{2,3},{3,2},{4,5},{5,4},{6,7},{7,6},{8,9},{9,8},{10,11... | collective-permute-start | bytes 24584 | tf_op jit(solution)/shard_map/ppermute | solution.py:360
  92.9 7.9 %collective-permute-start.15 = (f32[40,128]{1,0:T(8,128)S(1)}, f32[40,128]{1,0:T(8,128)S(1)}, u32[]{:S(2)}, u32[]{:S(2)}) collective-permute-start(f32[40,128]{1,0:T(8,128)S(1)} %add_select_fusion.2), channel_id=1, source_target_pairs={{0,8},{4,12},{8,0},{12,4},{16,24},{20,28},{24,16},{28,20},{1,9},{5... | collective-permute-start | bytes 61448 | tf_op jit(solution)/shard_map/ppermute | solution.py:360
  95.5 7.1 %collective-permute-start.13 = (f32[4,512]{1,0:T(4,128)S(1)}, f32[4,512]{1,0:T(4,128)S(1)}, u32[]{:S(2)}, u32[]{:S(2)}) collective-permute-start(f32[4,512]{1,0:T(4,128)S(1)} %multiply_add_fusion.1), channel_id=1, source_target_pairs={{0,2},{1,3},{2,0},{3,1},{4,6},{5,7},{6,4},{7,5},{8,10},{9,11},{10,... | collective-permute-start | bytes 24584 | tf_op jit(solution)/shard_map/ppermute | solution.py:360
  100.9 3.8 %collective-permute-start.16 = (f32[40,128]{1,0:T(8,128)S(1)}, f32[40,128]{1,0:T(8,128)S(1)}, u32[]{:S(2)}, u32[]{:S(2)}) collective-permute-start(f32[40,128]{1,0:T(8,128)S(1)} %add_select_fusion.1), channel_id=1, source_target_pairs={{0,16},{4,20},{8,24},{12,28},{16,0},{20,4},{24,8},{28,12},{1,17},{... | collective-permute-start | bytes 61448 | tf_op jit(solution)/shard_map/ppermute | solution.py:360
  108.3 25.6 %collective-permute-start.17 = (bf16[528,1024]{1,0:T(8,128)(2,1)}, bf16[528,1024]{1,0:T(8,128)(2,1)S(1)}, u32[]{:S(2)}, u32[]{:S(2)}) collective-permute-start(bf16[528,1024]{1,0:T(8,128)(2,1)} %early.1), channel_id=1, source_target_pairs={{0,1},{3,2},{2,0},{1,3},{4,5},{7,6},{6,4},{5,7},{8,9},{11,10},{10,... | collective-permute-start | bytes 3244040 | tf_op jit(solution)/shard_map/ppermute | solution.py:523
  133.9 57.4 %all-to-all-start.1 = ((bf16[8,272,1024]{2,1,0:T(8,128)(2,1)}), bf16[8,272,1024]{2,1,0:T(8,128)(2,1)}, u32[]{:S(2)}, u32[]{:S(2)}) async-start(bf16[8,272,1024]{2,1,0:T(8,128)(2,1)} %get-tuple-element.35), calls=%async_computation.1 | async-start | bytes 8912896 | tf_op jit(solution)/shard_map/all_to_all | solution.py:527
  141.4 26.6 %collective-permute-start.19 = (bf16[528,1024]{1,0:T(8,128)(2,1)}, bf16[528,1024]{1,0:T(8,128)(2,1)}, u32[]{:S(2)}, u32[]{:S(2)}) collective-permute-start(bf16[528,1024]{1,0:T(8,128)(2,1)} %get-tuple-element.39), channel_id=1, source_target_pairs={{0,1},{1,0},{2,3},{3,2},{4,5},{5,4},{6,7},{7,6},{8,9},{9,8},{10,11... | collective-permute-start | bytes 3244040 | tf_op jit(solution)/shard_map/ppermute | solution.py:523
  141.8 49.5 %collective-permute-start.18 = (bf16[528,1024]{1,0:T(8,128)(2,1)}, bf16[528,1024]{1,0:T(8,128)(2,1)}, u32[]{:S(2)}, u32[]{:S(2)}) collective-permute-start(bf16[528,1024]{1,0:T(8,128)(2,1)} %add_convert_fusion), channel_id=1, source_target_pairs={{2,1},{1,2},{3,0},{0,3},{6,5},{5,6},{7,4},{4,7},{10,9},{9,10},{11,... | collective-permute-start | bytes 3244040 | tf_op jit(solution)/shard_map/ppermute | solution.py:523
  191.3 1.2 copy-start.2

commit v4 on v3

--- a/solution.py
+++ b/solution.py
@@ -18,6 +18,7 @@
 EXTRA = 16
 GROUPED = 3
 MIB = 1024 * 1024
+MARK = 60_000_000_000
 
 
 def slot_tables(neg_lists, groups, per_group, slot_depth):
@@ -262,14 +263,11 @@
 def passage_kernel(chunks, picks, *refs):
     slot_ref, row_lse, weights = refs[:3]
     q_refs = refs[3:3 + len(chunks)]
-    own_out, far_out, own_acc, far_acc, far_buf, far_sems = refs[3 + len(chunks):]
-    per_group, rows, width = own_acc.shape
+    own_out, far_out, far_acc, far_buf, far_sems = refs[3 + len(chunks):]
+    per_group, rows, width = own_out.shape
     groups, packed = far_buf.shape[:2]
     depth = packed // rows
     home = {at + n: (c, n) for c, (at, size) in enumerate(chunks) for n in range(size)}
-
-    def own_copy(b):
-        return pltpu.make_async_copy(own_acc.at[b], own_out.at[b], far_sems.at[groups + b])
 
     far_acc[...] = jnp.zeros_like(far_acc)
     for b in range(per_group):
@@ -280,8 +278,7 @@
             for j in range(step):
                 part = parts[j * rows:(j + 1) * rows]
                 if k + j == 0:
-                    own_acc[b] = part
-                    own_copy(b).start()
+                    own_out[b] = part
                 else:
                     slot = slot_ref[b * picks + k + j - 1]
                     far_acc[slot] = far_acc[slot] + part
@@ -293,13 +290,11 @@
         pltpu.make_async_copy(far_buf.at[g], far_out.at[g], far_sems.at[g]).start()
     for g in range(groups):
         pltpu.make_async_copy(far_buf.at[g], far_out.at[g], far_sems.at[g]).wait()
-    for b in range(per_group):
-        own_copy(b).wait()
 
 
 def finish_kernel(depth, inner, finals, pos_ref, dest_ref, mine_ref, own_ref, far_ref, *refs):
     moved = refs[:len(finals)]
-    q_out, p_out, loss_ref, acc, got, q_got, sems, q_sems = refs[len(finals):]
+    q_out, p_out, loss_ref, acc, got, q_got, q_buf, p_buf, sems, q_sems, out_sems = refs[len(finals):]
     groups = far_ref.shape[0]
     per_group, rows, _ = p_out.shape
     pos = pos_ref[0]
@@ -307,35 +302,44 @@
     def far_copy(g):
         return pltpu.make_async_copy(far_ref.at[g], got.at[g], sems.at[g])
 
-    def moved_copy(n):
-        return pltpu.make_async_copy(moved[n], q_got.at[n], q_sems.at[n])
-
-    for n, devices in enumerate(finals):
-        @pl.when(one_of(pos, devices))
-        def _():
-            moved_copy(n).start()
+    def moved_copy(n, b):
+        part = pl.ds(b * rows, rows if b < per_group else EXTRA)
+        return pltpu.make_async_copy(moved[n].at[part], q_got.at[n, part], q_sems.at[n, b])
+
+    def q_copy(b):
+        return pltpu.make_async_copy(q_buf.at[b], q_out.at[b], out_sems.at[0, b])
+
+    def p_copy(b):
+        return pltpu.make_async_copy(p_buf.at[b], p_out.at[b], out_sems.at[1, b])
+
+    for b in range(per_group + 1):
+        for n, devices in enumerate(finals):
+            @pl.when(one_of(pos, devices))
+            def _():
+                moved_copy(n, b).start()
     for g in range(groups):
         far_copy(g).start()
     ends = {}
     for d in range(inner):
         ends.setdefault(tuple(n for n, devices in enumerate(finals) if d in devices), []).append(d)
     lane = lax.broadcasted_iota(jnp.int32, (8, 128), 1)
+    acc[0:per_group] = own_ref[...]
     for which, devices in ends.items():
         @pl.when(one_of(pos, devices))
         def _():
-            for n in which:
-                moved_copy(n).wait()
             for b in range(per_group):
                 part = slice(b * rows, (b + 1) * rows)
                 value = mine_ref[part, :].astype(jnp.float32)
                 for n in which:
+                    moved_copy(n, b).wait()
                     value = value + q_got[n, part, :].astype(jnp.float32)
-                q_out[b] = value.astype(jnp.bfloat16)
+                q_buf[b] = value.astype(jnp.bfloat16)
+                q_copy(b).start()
             piece = mine_ref[per_group * rows:, 0:128].astype(jnp.float32)
             for n in which:
+                moved_copy(n, per_group).wait()
                 piece = piece + q_got[n, per_group * rows:, 0:128].astype(jnp.float32)
             loss_ref[...] = jnp.where(lane < 3 * inner, piece[0:8], 0.0)
-    acc[0:per_group] = own_ref[...]
     pieces = loss_ref[...]
     for g in range(groups):
         far_copy(g).wait()
@@ -343,8 +347,19 @@
             dest = dest_ref[g * depth + c]
             acc[dest] = acc[dest] + got[g, c * rows:(c + 1) * rows].astype(jnp.float32)
         pieces = pieces + got[g, depth * rows:, 0:128].astype(jnp.float32)[0:8]
-    loss_ref[...] = jnp.sum(pieces, axis=1, keepdims=True) + jnp.zeros((8, 128), jnp.float32)
-    p_out[...] = acc[0:per_group].astype(jnp.bfloat16)
+    for b in range(per_group):
+        p_buf[b] = acc[b].astype(jnp.bfloat16)
+        p_copy(b).start()
+    total = jnp.sum(pieces, axis=1, keepdims=True) * (0.5 / (groups * per_group * rows * inner))
+    loss_ref[...] = total + jnp.zeros((8, 128), jnp.float32)
+    for b in range(per_group):
+        q_copy(b).wait()
+        p_copy(b).wait()
+
+
+def mark_kernel(a_ref, b_ref, out_ref):
+    del a_ref, b_ref
+    out_ref[...] = jnp.zeros_like(out_ref)
 
 
 def after(value, *events):
@@ -406,6 +421,17 @@
             ]
             lefts[c].append(moving[c][0])
             rights[c].append(moving[c][1])
+            if s == 1:
+                mark = pl.pallas_call(
+                    mark_kernel,
+                    out_shape=jax.ShapeDtypeStruct((8, 128), f32),
+                    in_specs=[ANY, ANY],
+                    out_specs=VMEM,
+                    compiler_params=params(1),
+                    cost_estimate=pl.CostEstimate(flops=MARK, bytes_accessed=0, transcendentals=0),
+                    name="mark",
+                )(*moving[c])
+                moving[c] = [after(value, mark) for value in moving[c]]
 
     slot_ranks, slot_block, slot_live = slot_tables(neg_lists, groups, per_group, CAP)
     listed = lax.dynamic_slice_in_dim(neg_lists, my_group * per_group, per_group, 0)
@@ -480,9 +506,10 @@
     out_slices = [sends for _, sends, _, _, _ in plan[1:]] + [own_slice]
     *parts, mine, weights = pl.pallas_call(
         functools.partial(query_kernel, out_slices, chunks, blocks, inner, picks),
-        out_shape=(in_hbm(flat, width),) * len(out_slices) + (pltpu.VMEM((per_group, full, cand_rows), bf16),),
+        out_shape=(in_hbm(flat, width),) * (len(out_slices) - 1)
+        + (pltpu.VMEM((flat, width), bf16), pltpu.VMEM((per_group, full, cand_rows), bf16)),
         in_specs=[SMEM] * 2 + [VMEM] * (3 + len(chunks)),
-        out_specs=(ANY,) * len(out_slices) + (VMEM,),
+        out_specs=(ANY,) * (len(out_slices) - 1) + (VMEM, VMEM),
         scratch_shapes=[
             pltpu.VMEM((per_group, full, width), bf16),
             pltpu.VMEM((EXTRA, width), bf16),
@@ -497,16 +524,15 @@
     own_grad, far_grad = pl.pallas_call(
         functools.partial(passage_kernel, chunks, picks),
         out_shape=(
-            jax.ShapeDtypeStruct((per_group, rows, width), f32),
+            pltpu.VMEM((per_group, rows, width), f32),
             in_hbm(groups, packed, width),
         ),
         in_specs=[SMEM] + [VMEM] * (2 + len(chunks)),
-        out_specs=(ANY, ANY),
+        out_specs=(VMEM, ANY),
         scratch_shapes=[
-            pltpu.VMEM((per_group, rows, width), f32),
             pltpu.VMEM((slot_count, rows, width), f32),
             pltpu.VMEM((groups, packed, width), bf16),
-            pltpu.SemaphoreType.DMA((groups + per_group,)),
+            pltpu.SemaphoreType.DMA((groups,)),
         ],
         compiler_params=params(28),
         cost_estimate=cost(per_group, 1),
@@ -534,19 +560,21 @@
             jax.ShapeDtypeStruct((8, 128), f32),
         ),
         in_specs=[SMEM] * 2 + [VMEM] * 2 + [ANY] * (1 + len(finals)),
-        out_specs=(VMEM,) * 3,
+        out_specs=(ANY, ANY, VMEM),
         scratch_shapes=[
             pltpu.VMEM((per_group + 1, rows, width), f32),
             pltpu.VMEM((groups, packed, width), bf16),
             pltpu.VMEM((len(finals), flat, width), bf16),
+            pltpu.VMEM((per_group, rows, width), bf16),
+            pltpu.VMEM((per_group, rows, width), bf16),
             pltpu.SemaphoreType.DMA((groups,)),
-            pltpu.SemaphoreType.DMA((len(finals),)),
+            pltpu.SemaphoreType.DMA((len(finals), per_group + 1)),
+            pltpu.SemaphoreType.DMA((2, per_group)),
         ],
         compiler_params=params(28),
         name="finish",
-    )(pos_arr, dest, mine, own_grad, returned, *[value for _, value in finals])
-    mean_loss = total[0, 0] / (2.0 * groups * per_group * full)
-    return (mean_loss, query_grad, passage_grad)
+    )(pos_arr, dest, resident(mine), resident(own_grad), returned, *[value for _, value in finals])
+    return (total[0, 0], query_grad, passage_grad)
 
 
 def solution(mesh):

time: 202 us -> 195 us (0.965)
  starting transfers between devices: 47 us -> 41.5 us
    ppermute x6, waiting for transfers between devices: 35 us -> 20.1 us  [body(): lax.ppermute(moving[c][1], 'inner', [(i, i - 1) for i in range(inner - s,...]
    all_to_all x1, waiting for transfers between devices: 0.01 us -> 13.1 us  [body(): lax.all_to_all(outgoing, 'dp', split_axis=0, concat_axis=0, tiled=True)]
    ppermute x5, starting transfers between devices: 8.81 us -> 5.73 us  [butterfly(): other = lax.ppermute(value, axis, [(i, i ^ step) for i in range(size)])]
    ppermute x3, starting transfers between devices: 4.13 us -> 1.98 us  [body(): sums.append(lax.ppermute(out, 'inner', pairs))]
  transfers between devices with their start and end apart: 22 -> 22, of which waited for: 12 -> 11; matrix products, arithmetic and copies ran while one was open for 3% -> 5% of each run, Pallas kernels for 14% -> 15%
where the time goes in v4:
time: 195 us
  waiting for transfers between devices  92.3 us (47%)
  Pallas kernels  44.5 us (23%)
  starting transfers between devices  41.5 us (21%)
  local copies, waits for them, and re-layouts  9.92 us (5%)
  other arithmetic  4.75 us (2%)
    ppermute x3, waiting for transfers between devices, body(): sums.append(lax.ppermute(out, 'inner', pairs))  52.9 us
    ppermute x6, waiting for transfers between devices, body(): lax.ppermute(moving[c][1], 'inner', [(i, i - 1) for i in range(inner - s,...  20.1 us
    ppermute x6, starting transfers between devices, body(): lax.ppermute(moving[c][0], 'inner', [(i, i + 1) for i in range(s - 1, inn...  17 us
    all_to_all x1, waiting for transfers between devices, body(): lax.all_to_all(outgoing, 'dp', split_axis=0, concat_axis=0, tiled=True)  13.1 us
    pallas_call x2, Pallas kernels, body(): pl.pallas_call(functools.partial(forward_kernel, chunk, inner, picks, sca...  12.2 us
    pallas_call x1, Pallas kernels, body(): pl.pallas_call(functools.partial(query_kernel, out_slices, chunks, blocks...  9.75 us
    pallas_call x1, Pallas kernels, body(): pl.pallas_call(functools.partial(passage_kernel, chunks, picks), out_shap...  8.84 us
    ppermute x6, starting transfers between devices, body(): lax.ppermute(moving[c][1], 'inner', [(i, i - 1) for i in range(inner - s,...  7.68 us
  transfers between devices with their start and end apart: 22, of which 11 were waited for; matrix products, arithmetic and copies ran while one was open for 5% of the time, Pallas kernels for 15%

profile of v4, /device:TPU:0, one launch (start us, length us, event | category | flops | bytes accessed | tf_op | source)
XLA Modules:
  0.0 194.6 jit_solution(5142256810586126469)
XLA Ops:
  0.7 2.3 %fusion.9 = (bf16[2,128,1024]{2,1,0:T(8,128)(2,1)}, bf16[2,128,1024]{2,1,0:T(8,128)(2,1)}) fusion(bf16[4,128,1024]{2,1,0:T(8,128)(2,1)} %refs_2_.3), kind=kLoop, calls=%fused_computation.43 | loop fusion | bytes 2097152 | tf_op jit(solution)/shard_map/slice | solution.py:415
  4.3 6.4 %collective-permute-start = (bf16[2,128,1024]{2,1,0:T(8,128)(2,1)}, bf16[2,128,1024]{2,1,0:T(8,128)(2,1)}, u32[]{:S(2)}, u32[]{:S(2)}) collective-permute-start(bf16[2,128,1024]{2,1,0:T(8,128)(2,1)} %get-tuple-element.53), channel_id=1, source_target_pairs={{0,1},{1,2},{2,3},{4,5},{5,6},{6,7},{8,9},{9,10},{10,11},{12,13},{... | collective-permute-start | bytes 1572872 | tf_op jit(solution)/shard_map/ppermute | solution.py:419
  11.9 4.6 %collective-permute-start.6 = (bf16[2,128,1024]{2,1,0:T(8,128)(2,1)}, bf16[2,128,1024]{2,1,0:T(8,128)(2,1)S(1)}, u32[]{:S(2)}, u32[]{:S(2)}) collective-permute-start(bf16[2,128,1024]{2,1,0:T(8,128)(2,1)} %get-tuple-element.54), channel_id=1, source_target_pairs={{0,1},{1,2},{2,3},{4,5},{5,6},{6,7},{8,9},{9,10},{10,11},{12,13},{... | collective-permute-start | bytes 1572872 | tf_op jit(solution)/shard_map/ppermute | solution.py:419
  17.5 2.8 %gather_fusion.1 = bf16[16,128,1024]{2,1,0:T(8,128)(2,1)} fusion(bf16[4,128,1024]{2,1,0:T(8,128)(2,1)S(1)} %copy-done, s32[1024]{0:T(1024)S(1)} %pad_clamp_fusion), kind=kCustom, calls=%fused_computation.1 | custom fusion | bytes 8388672 | tf_op jit(solution)/shard_map/gather | solution.py:446
  20.3 4.5 %all-to-all-start = ((bf16[8,2,128,1024]{3,2,1,0:T(8,128)(2,1)}), bf16[8,2,128,1024]{3,2,1,0:T(8,128)(2,1)}, u32[]{:S(2)}, u32[]{:S(2)}) async-start(bf16[8,2,128,1024]{3,2,1,0:T(8,128)(2,1)} %bitcast.14), calls=%async_computation | async-start | bytes 8388608 | tf_op jit(solution)/shard_map/all_to_all | solution.py:447
  25.0 1.6 collective-permute-start.2
  27.9 3.3 %collective-permute-done.7.refs_6_ = bf16[2,128,1024]{2,1,0:T(8,128)(2,1)S(1)} collective-permute-done((bf16[2,128,1024]{2,1,0:T(8,128)(2,1)}, bf16[2,128,1024]{2,1,0:T(8,128)(2,1)S(1)}, u32[]{:S(2)}, u32[]{:S(2)}) %collective-permute-start.7) | collective-permute-done | bytes 524320 | tf_op jit(solution)/shard_map/ppermute | solution.py:420
  31.3 1.3 collective-permute-done.6.refs_3_
  32.5 1.5 collective-permute-start.8
  36.5 1.5 collective-permute-start.3
  38.0 8.4 %collective-permute-done.4.refs_7_ = bf16[2,128,1024]{2,1,0:T(8,128)(2,1)} collective-permute-done((bf16[2,128,1024]{2,1,0:T(8,128)(2,1)}, bf16[2,128,1024]{2,1,0:T(8,128)(2,1)}, u32[]{:S(2)}, u32[]{:S(2)}) %collective-permute-start.4) | collective-permute-done | bytes 524320 | tf_op jit(solution)/shard_map/ppermute | solution.py:420
  47.8 1.5 collective-permute-start.9
  49.3 8.4 %collective-permute-done.10.refs_7_ = bf16[2,128,1024]{2,1,0:T(8,128)(2,1)} collective-permute-done((bf16[2,128,1024]{2,1,0:T(8,128)(2,1)S(1)}, bf16[2,128,1024]{2,1,0:T(8,128)(2,1)}, u32[]{:S(2)}, u32[]{:S(2)}) %collective-permute-start.10) | collective-permute-done | bytes 524320 | tf_op jit(solution)/shard_map/ppermute | solution.py:420
  57.6 1.3 collective-permute-start.11
  60.9 13.1 %all-to-all-done = bf16[8,2,128,1024]{3,2,1,0:T(8,128)(2,1)} async-done(((bf16[8,2,128,1024]{3,2,1,0:T(8,128)(2,1)}), bf16[8,2,128,1024]{3,2,1,0:T(8,128)(2,1)}, u32[]{:S(2)}, u32[]{:S(2)}) %all-to-all-start) | async-done | bytes 4194336 | tf_op jit(solution)/shard_map/all_to_all | solution.py:447
  74.0 4.4 %collect.1.refs_9_.refs_2_ = bf16[4,1152,1024]{2,1,0:T(8,128)(2,1)S(1)} custom-call(s32[32]{0:T(128)S(1)} %reshape.83.slot_ref.refs_0_, bf16[4,128,1024]{2,1,0:T(8,128)(2,1)S(1)} %copy-done, bf16[16,128,1024]{2,1,0:T(8,128)(2,1)} %bitcast.5.far_p), custom_call_target="tpu_custom_call" | custom-call | tf_op jit(solution)/shard_map/collect/pallas_call | solution.py:452
  78.5 6.1 %forward_0.1 = (f32[2,512]{1,0:T(2,128)S(1)}, f32[40,128]{1,0:T(8,128)S(1)}, f32[2,512,1152]{2,1,0:T(8,128)S(1)}, bf16[2,512,1024]{2,1,0:T(8,128)(2,1)S(1)}) custom-call(s32[1]{0:T(128)} %bitcast.refs_0_.pos_ref, s32[36]{0:T(128)S(1)} %reshape.82.refs_1_, bf16[4,128,1024]{2,1,0:T(8,128)(2,1)S(1)} %copy-done.1, ...), custom_call_target="tpu_custom_call" | custom-call | flops 2415919104 | bytes 6815744 | tf_op jit(solution)/shard_map/forward_0/pallas_call | solution.py:464
  84.6 6.0 %forward_1.1 = (f32[2,512]{1,0:T(2,128)S(1)}, f32[40,128]{1,0:T(8,128)S(1)}, f32[2,512,1152]{2,1,0:T(8,128)S(1)}, bf16[2,512,1024]{2,1,0:T(8,128)(2,1)S(1)}) custom-call(s32[1]{0:T(128)} %bitcast.refs_0_.pos_ref, s32[36]{0:T(128)S(1)} %reshape.82.refs_1_, bf16[4,128,1024]{2,1,0:T(8,128)(2,1)S(1)} %copy-done.1, ...), custom_call_target="tpu_custom_call" | custom-call | flops 2415919104 | bytes 6815744 | tf_op jit(solution)/shard_map/forward_1/pallas_call | solution.py:464
  90.8 1.6 collective-permute-start.12
  93.0 1.5 collective-permute-done.12
  94.5 3.0 %collective-permute-start.13 = (f32[4,512]{1,0:T(4,128)S(1)}, f32[4,512]{1,0:T(4,128)S(1)}, u32[]{:S(2)}, u32[]{:S(2)}) collective-permute-start(f32[4,512]{1,0:T(4,128)S(1)} %multiply_add_fusion.1), channel_id=1, source_target_pairs={{0,2},{1,3},{2,0},{3,1},{4,6},{5,7},{6,4},{7,5},{8,10},{9,11},{10,... | collective-permute-start | bytes 24584 | tf_op jit(solution)/shard_map/ppermute | solution.py:375
  99.2 2.2 %collective-permute-done.16 = f32[40,128]{1,0:T(8,128)S(1)} collective-permute-done((f32[40,128]{1,0:T(8,128)S(1)}, f32[40,128]{1,0:T(8,128)S(1)}, u32[]{:S(2)}, u32[]{:S(2)}) %collective-permute-start.16) | collective-permute-done | bytes 20512 | tf_op jit(solution)/shard_map/ppermute | solution.py:375
  101.5 3.4 %early.1 = bf16[528,1024]{1,0:T(8,128)(2,1)} custom-call(s32[1]{0:T(128)} %bitcast.refs_0_.pos_ref, s32[36]{0:T(128)S(1)} %reshape.82.refs_1_, bf16[4,1152,1024]{2,1,0:T(8,128)(2,1)S(1)} %collect.1.refs_9_.refs_2_, f32[4,512]{1,0:T(4,128)S(1)} %multiply_add_fusion.refs_3_.refs_1_, f32[40,128]{1,0:T(8,128)S(1)} %add_select_fusion.refs_4_, ...), custom_call_target="tpu_custom_call" | custom-call | flops 1207959552 | bytes 3407872 | tf_op jit(solution)/shard_map/early/pallas_call | solution.py:490
  105.0 9.8 %query.1 = (bf16[528,1024]{1,0:T(8,128)(2,1)}, bf16[528,1024]{1,0:T(8,128)(2,1)}, bf16[528,1024]{1,0:T(8,128)(2,1)S(1)}, bf16[4,512,1152]{2,1,0:T(8,128)(2,1)S(1)}) custom-call(s32[1]{0:T(128)} %bitcast.refs_0_.pos_ref, s32[36]{0:T(128)S(1)} %reshape.82.refs_1_, bf16[4,1152,1024]{2,1,0:T(8,128)(2,1)S(1)} %collect.1.refs_9_.refs_2_, ...), custom_call_target="tpu_custom_call" | custom-call | flops 4831838208 | bytes 13631488 | tf_op jit(solution)/shard_map/query/pallas_call | solution.py:507
  115.8 8.8 %passage.1 = (f32[4,128,1024]{2,1,0:T(8,128)S(1)}, bf16[8,272,1024]{2,1,0:T(8,128)(2,1)}) custom-call(s32[32]{0:T(128)S(1)} %reshape.83.slot_ref.refs_0_, f32[4,512]{1,0:T(4,128)S(1)} %multiply_add_fusion.refs_3_.refs_1_, bf16[4,512,1152]{2,1,0:T(8,128)(2,1)S(1)} %get-tuple-element.38.refs_2_, bf16[2,512,1024]{2,1,0:T(8,128)(2,1)S(1)} %get-tuple-element.39.refs_3_, ...), custom_call_target="tpu_custom_call" | custom-call | flops 4831838208 | bytes 13631488 | tf_op jit(solution)/shard_map/passage/pallas_call | solution.py:524
  124.6 5.2 %collective-permute-done.17.refs_0_ = bf16[528,1024]{1,0:T(8,128)(2,1)S(1)} collective-permute-done((bf16[528,1024]{1,0:T(8,128)(2,1)}, bf16[528,1024]{1,0:T(8,128)(2,1)S(1)}, u32[]{:S(2)}, u32[]{:S(2)}) %collective-permute-start.17) | collective-permute-done | bytes 1081376 | tf_op jit(solution)/shard_map/ppermute | solution.py:549
  129.8 4.6 %all-to-all-start.1 = ((bf16[8,272,1024]{2,1,0:T(8,128)(2,1)}), bf16[8,272,1024]{2,1,0:T(8,128)(2,1)}, u32[]{:S(2)}, u32[]{:S(2)}) async-start(bf16[8,272,1024]{2,1,0:T(8,128)(2,1)} %get-tuple-element.43), calls=%async_computation.1 | async-start | bytes 8912896 | tf_op jit(solution)/shard_map/all_to_all | solution.py:553
  134.4 2.7 %add_convert_fusion = bf16[528,1024]{1,0:T(8,128)(2,1)} fusion(bf16[528,1024]{1,0:T(8,128)(2,1)S(1)} %collective-permute-done.17.refs_0_, bf16[528,1024]{1,0:T(8,128)(2,1)} %get-tuple-element.44, pred[]{:T(512)S(6)} %or.3), kind=kLoop, calls=%fused_computation.2 | loop fusion | flops 2703360 | bytes 3244033 | tf_op jit(solution)/shard_map/convert_element_type | solution.py:546
  137.1 1.9 collective-permute-start.18
  139.2 24.5 %collective-permute-done.19.refs_2_ = bf16[528,1024]{1,0:T(8,128)(2,1)} collective-permute-done((bf16[528,1024]{1,0:T(8,128)(2,1)}, bf16[528,1024]{1,0:T(8,128)(2,1)}, u32[]{:S(2)}, u32[]{:S(2)}) %collective-permute-start.19) | collective-permute-done | bytes 1081376 | tf_op jit(solution)/shard_map/ppermute | solution.py:549
  163.7 23.3 %collective-permute-done.18.refs_1_ = bf16[528,1024]{1,0:T(8,128)(2,1)} collective-permute-done((bf16[528,1024]{1,0:T(8,128)(2,1)}, bf16[528,1024]{1,0:T(8,128)(2,1)}, u32[]{:S(2)}, u32[]{:S(2)}) %collective-permute-start.18) | collective-permute-done | bytes 1081376 | tf_op jit(solution)/shard_map/ppermute | solution.py:549
  188.2 5.9 %finish.1 = (bf16[4,128,1024]{2,1,0:T(8,128)(2,1)}, bf16[4,128,1024]{2,1,0:T(8,128)(2,1)}, f32[8,128]{1,0:T(8,128)S(1)}) custom-call(s32[1]{0:T(128)} %bitcast.refs_0_.pos_ref, s32[16]{0:T(128)S(1)} %select_n.73.dest_ref, bf16[528,1024]{1,0:T(8,128)(2,1)S(1)} %copy-done.3, f32[4,128,1024]{2,1,0:T(8,128)S(1)} %get-tuple-element.41.own_ref, ...), custom_call_target="tpu_custom_call" | custom-call | tf_op jit(solution)/shard_map/finish/pallas_call | solution.py:555
  (74 shorter events, 15.6 us)
Async XLA Ops:
  0.6 15.9 %copy-start.4 = (s32[32,8]{0,1:T(8,128)S(1)}, s32[32,8]{0,1:T(8,128)}, u32[]{:S(2)}) copy-start(s32[32,8]{0,1:T(8,128)} %param.5) | copy-start | bytes 3076
  0.6 16.9 %copy-start = (bf16[4,128,1024]{2,1,0:T(8,128)(2,1)S(1)}, bf16[4,128,1024]{2,1,0:T(8,128)(2,1)}, u32[]{:S(2)}) copy-start(bf16[4,128,1024]{2,1,0:T(8,128)(2,1)} %own_p.1) | copy-start | bytes 3145732
  3.0 22.0 %collective-permute-start.1 = (bf16[2,128,1024]{2,1,0:T(8,128)(2,1)}, bf16[2,128,1024]{2,1,0:T(8,128)(2,1)}, u32[]{:S(2)}, u32[]{:S(2)}) collective-permute-start(bf16[2,128,1024]{2,1,0:T(8,128)(2,1)} %get-tuple-element.53), channel_id=1, source_target_pairs={{3,2},{2,1},{1,0},{7,6},{6,5},{5,4},{11,10},{10,9},{9,8},{15,14},{... | collective-permute-start | bytes 1572872 | tf_op jit(solution)/shard_map/ppermute | solution.py:420
  4.3 20.8 %collective-permute-start = (bf16[2,128,1024]{2,1,0:T(8,128)(2,1)}, bf16[2,128,1024]{2,1,0:T(8,128)(2,1)}, u32[]{:S(2)}, u32[]{:S(2)}) collective-permute-start(bf16[2,128,1024]{2,1,0:T(8,128)(2,1)} %get-tuple-element.53), channel_id=1, source_target_pairs={{0,1},{1,2},{2,3},{4,5},{5,6},{6,7},{8,9},{9,10},{10,11},{12,13},{... | collective-permute-start | bytes 1572872 | tf_op jit(solution)/shard_map/ppermute | solution.py:419
  10.6 20.6 %collective-permute-start.7 = (bf16[2,128,1024]{2,1,0:T(8,128)(2,1)}, bf16[2,128,1024]{2,1,0:T(8,128)(2,1)S(1)}, u32[]{:S(2)}, u32[]{:S(2)}) collective-permute-start(bf16[2,128,1024]{2,1,0:T(8,128)(2,1)} %get-tuple-element.54), channel_id=1, source_target_pairs={{3,2},{2,1},{1,0},{7,6},{6,5},{5,4},{11,10},{10,9},{9,8},{15,14},{... | collective-permute-start | bytes 1572872 | tf_op jit(solution)/shard_map/ppermute | solution.py:420
  11.9 20.6 %collective-permute-start.6 = (bf16[2,128,1024]{2,1,0:T(8,128)(2,1)}, bf16[2,128,1024]{2,1,0:T(8,128)(2,1)S(1)}, u32[]{:S(2)}, u32[]{:S(2)}) collective-permute-start(bf16[2,128,1024]{2,1,0:T(8,128)(2,1)} %get-tuple-element.54), channel_id=1, source_target_pairs={{0,1},{1,2},{2,3},{4,5},{5,6},{6,7},{8,9},{9,10},{10,11},{12,13},{... | collective-permute-start | bytes 1572872 | tf_op jit(solution)/shard_map/ppermute | solution.py:419
  20.3 53.7 %all-to-all-start = ((bf16[8,2,128,1024]{3,2,1,0:T(8,128)(2,1)}), bf16[8,2,128,1024]{3,2,1,0:T(8,128)(2,1)}, u32[]{:S(2)}, u32[]{:S(2)}) async-start(bf16[8,2,128,1024]{3,2,1,0:T(8,128)(2,1)} %bitcast.14), calls=%async_computation | async-start | bytes 8388608 | tf_op jit(solution)/shard_map/all_to_all | solution.py:447
  24.9 34.0 %copy-start.1 = (bf16[4,128,1024]{2,1,0:T(8,128)(2,1)S(1)}, bf16[4,128,1024]{2,1,0:T(8,128)(2,1)}, u32[]{:S(2)}) copy-start(bf16[4,128,1024]{2,1,0:T(8,128)(2,1)} %refs_2_.3) | copy-start | bytes 3145732
  25.0 11.5 %collective-permute-start.2 = (bf16[2,128,1024]{2,1,0:T(8,128)(2,1)}, bf16[2,128,1024]{2,1,0:T(8,128)(2,1)}, u32[]{:S(2)}, u32[]{:S(2)}) collective-permute-start(bf16[2,128,1024]{2,1,0:T(8,128)(2,1)} %collective-permute-done.refs_3_), channel_id=1, source_target_pairs={{1,2},{2,3},{5,6},{6,7},{9,10},{10,11},{13,14},{14,15},{17,18},{18... | collective-permute-start | bytes 1572872 | tf_op jit(solution)/shard_map/ppermute | solution.py:419
  26.6 19.8 %collective-permute-start.4 = (bf16[2,128,1024]{2,1,0:T(8,128)(2,1)}, bf16[2,128,1024]{2,1,0:T(8,128)(2,1)}, u32[]{:S(2)}, u32[]{:S(2)}) collective-permute-start(bf16[2,128,1024]{2,1,0:T(8,128)(2,1)} %collective-permute-done.1.refs_6_), channel_id=1, source_target_pairs={{2,1},{1,0},{6,5},{5,4},{10,9},{9,8},{14,13},{13,12},{18,17},{17,1... | collective-permute-start | bytes 1572872 | tf_op jit(solution)/shard_map/ppermute | solution.py:420
  32.5 15.3 %collective-permute-start.8 = (bf16[2,128,1024]{2,1,0:T(8,128)(2,1)S(1)}, bf16[2,128,1024]{2,1,0:T(8,128)(2,1)}, u32[]{:S(2)}, u32[]{:S(2)}) collective-permute-start(bf16[2,128,1024]{2,1,0:T(8,128)(2,1)S(1)} %collective-permute-done.6.refs_3_), channel_id=1, source_target_pairs={{1,2},{2,3},{5,6},{6,7},{9,10},{10,11},{13,14},{14,15},{17,18},{18... | collective-permute-start | bytes 1572872 | tf_op jit(solution)/shard_map/ppermute | solution.py:419
  34.0 23.6 %collective-permute-start.10 = (bf16[2,128,1024]{2,1,0:T(8,128)(2,1)S(1)}, bf16[2,128,1024]{2,1,0:T(8,128)(2,1)}, u32[]{:S(2)}, u32[]{:S(2)}) collective-permute-start(bf16[2,128,1024]{2,1,0:T(8,128)(2,1)S(1)} %collective-permute-done.7.refs_6_), channel_id=1, source_target_pairs={{2,1},{1,0},{6,5},{5,4},{10,9},{9,8},{14,13},{13,12},{18,17},{17,1... | collective-permute-start | bytes 1572872 | tf_op jit(solution)/shard_map/ppermute | solution.py:420
  36.5 41.9 %collective-permute-start.3 = (bf16[2,128,1024]{2,1,0:T(8,128)(2,1)}, bf16[2,128,1024]{2,1,0:T(8,128)(2,1)}, u32[]{:S(2)}, u32[]{:S(2)}) collective-permute-start(bf16[2,128,1024]{2,1,0:T(8,128)(2,1)} %collective-permute-done.2.refs_4_), channel_id=1, source_target_pairs={{2,3},{6,7},{10,11},{14,15},{18,19},{22,23},{26,27},{30,31}} | collective-permute-start | bytes 1572872 | tf_op jit(solution)/shard_map/ppermute | solution.py:419
  46.4 32.0 %collective-permute-start.5 = (bf16[2,128,1024]{2,1,0:T(8,128)(2,1)}, bf16[2,128,1024]{2,1,0:T(8,128)(2,1)}, u32[]{:S(2)}, u32[]{:S(2)}) collective-permute-start(bf16[2,128,1024]{2,1,0:T(8,128)(2,1)} %collective-permute-done.4.refs_7_), channel_id=1, source_target_pairs={{1,0},{5,4},{9,8},{13,12},{17,16},{21,20},{25,24},{29,28}} | collective-permute-start | bytes 1572872 | tf_op jit(solution)/shard_map/ppermute | solution.py:420
  47.8 36.8 %collective-permute-start.9 = (bf16[2,128,1024]{2,1,0:T(8,128)(2,1)}, bf16[2,128,1024]{2,1,0:T(8,128)(2,1)}, u32[]{:S(2)}, u32[]{:S(2)}) collective-permute-start(bf16[2,128,1024]{2,1,0:T(8,128)(2,1)} %collective-permute-done.8.refs_4_), channel_id=1, source_target_pairs={{2,3},{6,7},{10,11},{14,15},{18,19},{22,23},{26,27},{30,31}} | collective-permute-start | bytes 1572872 | tf_op jit(solution)/shard_map/ppermute | solution.py:419
  57.6 27.0 %collective-permute-start.11 = (bf16[2,128,1024]{2,1,0:T(8,128)(2,1)}, bf16[2,128,1024]{2,1,0:T(8,128)(2,1)}, u32[]{:S(2)}, u32[]{:S(2)}) collective-permute-start(bf16[2,128,1024]{2,1,0:T(8,128)(2,1)} %collective-permute-done.10.refs_7_), channel_id=1, source_target_pairs={{1,0},{5,4},{9,8},{13,12},{17,16},{21,20},{25,24},{29,28}} | collective-permute-start | bytes 1572872 | tf_op jit(solution)/shard_map/ppermute | solution.py:420
  90.7 1.7 collective-permute-start.14
  90.8 3.7 %collective-permute-start.12 = (f32[4,512]{1,0:T(4,128)S(1)}, f32[4,512]{1,0:T(4,128)S(1)}, u32[]{:S(2)}, u32[]{:S(2)}) collective-permute-start(f32[4,512]{1,0:T(4,128)S(1)} %pad_maximum_fusion), channel_id=1, source_target_pairs={{0,1},{1,0},{2,3},{3,2},{4,5},{5,4},{6,7},{7,6},{8,9},{9,8},{10,11... | collective-permute-start | bytes 24584 | tf_op jit(solution)/shard_map/ppermute | solution.py:375
  92.4 5.1 %collective-permute-start.15 = (f32[40,128]{1,0:T(8,128)S(1)}, f32[40,128]{1,0:T(8,128)S(1)}, u32[]{:S(2)}, u32[]{:S(2)}) collective-permute-start(f32[40,128]{1,0:T(8,128)S(1)} %add_select_fusion.2), channel_id=1, source_target_pairs={{0,8},{4,12},{8,0},{12,4},{16,24},{20,28},{24,16},{28,20},{1,9},{5... | collective-permute-start | bytes 61448 | tf_op jit(solution)/shard_map/ppermute | solution.py:375
  94.5 4.7 %collective-permute-start.13 = (f32[4,512]{1,0:T(4,128)S(1)}, f32[4,512]{1,0:T(4,128)S(1)}, u32[]{:S(2)}, u32[]{:S(2)}) collective-permute-start(f32[4,512]{1,0:T(4,128)S(1)} %multiply_add_fusion.1), channel_id=1, source_target_pairs={{0,2},{1,3},{2,0},{3,1},{4,6},{5,7},{6,4},{7,5},{8,10},{9,11},{10,... | collective-permute-start | bytes 24584 | tf_op jit(solution)/shard_map/ppermute | solution.py:375
  97.6 3.8 %collective-permute-start.16 = (f32[40,128]{1,0:T(8,128)S(1)}, f32[40,128]{1,0:T(8,128)S(1)}, u32[]{:S(2)}, u32[]{:S(2)}) collective-permute-start(f32[40,128]{1,0:T(8,128)S(1)} %add_select_fusion.1), channel_id=1, source_target_pairs={{0,16},{4,20},{8,24},{12,28},{16,0},{20,4},{24,8},{28,12},{1,17},{... | collective-permute-start | bytes 61448 | tf_op jit(solution)/shard_map/ppermute | solution.py:375
  105.0 24.8 %collective-permute-start.17 = (bf16[528,1024]{1,0:T(8,128)(2,1)}, bf16[528,1024]{1,0:T(8,128)(2,1)S(1)}, u32[]{:S(2)}, u32[]{:S(2)}) collective-permute-start(bf16[528,1024]{1,0:T(8,128)(2,1)} %early.1), channel_id=1, source_target_pairs={{0,1},{3,2},{2,0},{1,3},{4,5},{7,6},{6,4},{5,7},{8,9},{11,10},{10,... | collective-permute-start | bytes 3244040 | tf_op jit(solution)/shard_map/ppermute | solution.py:549
  114.8 1.0 copy-start.2
  129.8 57.1 %all-to-all-start.1 = ((bf16[8,272,1024]{2,1,0:T(8,128)(2,1)}), bf16[8,272,1024]{2,1,0:T(8,128)(2,1)}, u32[]{:S(2)}, u32[]{:S(2)}) async-start(bf16[8,272,1024]{2,1,0:T(8,128)(2,1)} %get-tuple-element.43), calls=%async_computation.1 | async-start | bytes 8912896 | tf_op jit(solution)/shard_map/all_to_all | solution.py:553
  137.0 26.6 %collective-permute-start.19 = (bf16[528,1024]{1,0:T(8,128)(2,1)}, bf16[528,1024]{1,0:T(8,128)(2,1)}, u32[]{:S(2)}, u32[]{:S(2)}) collective-permute-start(bf16[528,1024]{1,0:T(8,128)(2,1)} %get-tuple-element.47), channel_id=1, source_target_pairs={{0,1},{1,0},{2,3},{3,2},{4,5},{5,4},{6,7},{7,6},{8,9},{9,8},{10,11... | collective-permute-start | bytes 3244040 | tf_op jit(solution)/shard_map/ppermute | solution.py:549
  137.1 49.9 %collective-permute-start.18 = (bf16[528,1024]{1,0:T(8,128)(2,1)}, bf16[528,1024]{1,0:T(8,128)(2,1)}, u32[]{:S(2)}, u32[]{:S(2)}) collective-permute-start(bf16[528,1024]{1,0:T(8,128)(2,1)} %add_convert_fusion), channel_id=1, source_target_pairs={{2,1},{1,2},{3,0},{0,3},{6,5},{5,6},{7,4},{4,7},{10,9},{9,10},{11,... | collective-permute-start | bytes 3244040 | tf_op jit(solution)/shard_map/ppermute | solution.py:549
  186.9 1.2 copy-start.3
